TPU v7x, 32 devices: a whole 2x2x4 slice. The times are simulated.
32 devices in a mesh: lat: 16 (over z, x, core), lon: 2 (over y).
Axes of the slice: x: 2, y: 2, z: 4, core: 2. Of those that a mesh axis runs over, the one named last changes fastest.
Arguments:
- cotangent: bfloat16 [256, 512, 1024], P(None, 'lat', 'lon'), may hold values from -6 to 6
- block_input: bfloat16 [256, 512, 1024], P(None, 'lat', 'lon'), may hold values from -6 to 6
- filtered: bfloat16 [256, 512, 1024], P(None, 'lat', 'lon'), may hold values from -6 to 6
- spectral_saved: float32 [128, 256, 2, 128], P('lat', 'lon'), may hold values from -6 to 6
- spectral_gain: float32 [128, 256, 2, 128], P('lat', 'lon'), may hold values from -6 to 6
- w_in: bfloat16 [256, 512], replicated, may hold values from -0.375 to 0.375
- w_out: bfloat16 [512, 256], replicated, may hold values from -0.25 to 0.25
- w_disco: bfloat16 [256, 256], replicated, may hold values from -0.375 to 0.375
- quad_weights: float32 [64], replicated, may hold values from 0.05 to 0.35
- lat_offsets: int32 [512, 12], replicated, may hold values from -2 to 2, as said below
- lon_offsets: int32 [512, 12], replicated, may hold values from -2 to 2, as said below
- weight_index: int32 [512, 12], replicated, may hold values from 0 to 63
Outputs:
- grad_input: bfloat16 [256, 512, 1024], P(None, 'lat', 'lon')
- grad_gain: float32 [128, 256, 2, 128], P('lat', 'lon')
- grad_w_in: float32 [256, 512], replicated
- grad_w_out: float32 [512, 256], replicated
- grad_w_disco: float32 [256, 256], replicated
Inputs may be any that keep to these rules, and one draw needn't show every extreme that they name: `lat_offsets`: in every row the first tap lies exactly 2 rows away, to the north in half of the rows and to the south in the other half. `lon_offsets`: in every row the first tap lies exactly 2 columns away, to the east in half of the rows and to the west in the other half.
All inputs are finite; a program needn't handle non-finite values.
Results may differ from a plain program's by a relative error of at most 0.0069.
Values may be sent and summed in bfloat16 or wider, within the bound.
No kernel may reach another device: no remote copies, remote signals or barrier semaphores. Data moves between devices by JAX's collectives and lax.ppermute only.
A program may use at most 320 MiB of HBM per device.

v0:
```python
import math

import jax
import jax.numpy as jnp
import numpy as np
from jax import lax
from jax.sharding import PartitionSpec as P

NLAT = 512
NLON = 1024
L = 128
M = 128
REACH = 2
NQ = 64


root_half = 0.7071067811865476
root_two_pi = 2.5066282746310002


def padded_2(block, sides, width):
    for axis, dim in sides:
        count = lax.axis_size(axis)
        forward = [(i, i + 1) for i in range(count - 1)]
        forward.append((count - 1, 0))
        backward = [(target, source) for source, target in forward]
        low = lax.ppermute(
            lax.slice_in_dim(block, block.shape[dim] - width, None, axis=dim), axis, forward
        )
        high = lax.ppermute(lax.slice_in_dim(block, 0, width, axis=dim), axis, backward)
        block = jnp.concatenate([low, block, high], axis=dim)
    return block


def gelu_value(value):
    return value * 0.5 * (1.0 + lax.erf(value * root_half))


def gelu_slope(value):
    return (
        0.5 * (1.0 + lax.erf(value * root_half))
        + value * jnp.exp(-0.5 * value * value) / root_two_pi
    )


def legendre_tables():
    degree = np.arange(L)[:, None] * 1.0
    order = np.arange(M)[None, :] * 1.0
    upper = np.where(
        degree > order,
        np.sqrt((4.0 * degree * degree - 1.0) / np.maximum(degree * degree - order * order, 1.0)),
        0.0,
    )
    lower = np.where(
        degree > order + 1.0,
        np.sqrt(
            np.maximum((degree - 1.0) ** 2 - order * order, 0.0)
            / np.maximum(4.0 * (degree - 1.0) ** 2 - 1.0, 1.0)
        ),
        0.0,
    )
    counter = np.arange(1, M) * 1.0
    diagonal_log = np.concatenate(
        [np.zeros(1), np.cumsum(0.5 * np.log((2.0 * counter + 1.0) / (2.0 * counter)))]
    ) - 0.5 * np.log(2.0)
    return (upper, lower, diagonal_log)


def legendre_rows(theta):
    upper, lower, diagonal_log = legendre_tables()
    float_type = theta.dtype
    cosine = jnp.cos(theta)[:, None]
    sine = jnp.sin(theta)
    orders = jnp.arange(M, dtype=jnp.int32)
    start_value = jnp.exp(
        jnp.asarray(diagonal_log, float_type)[None, :]
        + orders.astype(float_type)[None, :] * jnp.log(sine)[:, None]
    )

    def advance(carry, inputs):
        previous, before = carry
        degree, coef_up, coef_low = inputs
        fresh = jnp.where(
            (orders == degree)[None, :],
            start_value,
            coef_up[None, :] * (cosine * previous - coef_low[None, :] * before),
        )
        return ((fresh, previous), fresh)

    empty = jnp.zeros_like(start_value)
    final, table = lax.scan(
        advance,
        (empty, empty),
        (
            jnp.arange(L, dtype=jnp.int32),
            jnp.asarray(upper, float_type),
            jnp.asarray(lower, float_type),
        ),
    )
    weight = jnp.sqrt(sine * (math.pi / NLAT))
    return table * weight[None, :, None]


def forward_table():
    column = jnp.arange(NLON, dtype=jnp.int32)[:, None]
    order = jnp.arange(M, dtype=jnp.int32)[None, :]
    angle = (column * order % NLON).astype(jnp.float32) * (2.0 * math.pi / NLON)
    factor = jnp.where(order == 0, 1.0, 2.0).astype(jnp.float32) / math.sqrt(NLON)
    return jnp.concatenate([factor * jnp.cos(angle), -factor * jnp.sin(angle)], axis=1).astype(
        jnp.bfloat16
    )


def inverse_table():
    order = jnp.arange(M, dtype=jnp.int32)[:, None]
    column = jnp.arange(NLON, dtype=jnp.int32)[None, :]
    angle = (column * order % NLON).astype(jnp.float32) * (2.0 * math.pi / NLON)
    return (jnp.concatenate([jnp.cos(angle), -jnp.sin(angle)], axis=0) / math.sqrt(NLON)).astype(
        jnp.bfloat16
    )


def disco_kernel(quad_weights, lat_offsets, lon_offsets, weight_index):
    span = jnp.arange(-REACH, REACH + 1, dtype=jnp.int32)
    slots = jnp.arange(NQ, dtype=jnp.int32)
    values = jnp.sum(
        jnp.where(
            weight_index[:, :, None] == slots[None, None, :], quad_weights[None, None, :], 0.0
        ),
        axis=2,
    )
    north = (lat_offsets[:, :, None] == span[None, None, :]).astype(quad_weights.dtype)
    east = (lon_offsets[:, :, None] == span[None, None, :]).astype(quad_weights.dtype)
    return jnp.sum(values[:, :, None, None] * north[:, :, :, None] * east[:, :, None, :], axis=1)


def disco_apply(padded, kernel):
    height = kernel.shape[0]
    width = padded.shape[2] - 2 * REACH
    total = jnp.zeros((padded.shape[0], height, width), kernel.dtype)
    for north in range(2 * REACH + 1):
        for east in range(2 * REACH + 1):
            total = (
                total
                + kernel[None, :, north, east, None]
                * padded[:, north : north + height, east : east + width]
            )
    return total


def disco_adjoint(padded, kernel_rim):
    height = kernel_rim.shape[0] - 2 * REACH
    width = padded.shape[2] - 2 * REACH
    total = jnp.zeros((padded.shape[0], height, width), kernel_rim.dtype)
    for north in range(2 * REACH + 1):
        for east in range(2 * REACH + 1):
            row_shift = 2 * REACH - north
            col_shift = 2 * REACH - east
            total = (
                total
                + kernel_rim[None, row_shift : row_shift + height, north, east, None]
                * padded[:, row_shift : row_shift + height, col_shift : col_shift + width]
            )
    return total


def inside_rows(padded, first_row):
    height = padded.shape[1]
    latitude = first_row - REACH + jnp.arange(height, dtype=jnp.int32)
    keep = (latitude >= 0) & (latitude < NLAT)
    return jnp.where(keep[None, :, None], padded, jnp.zeros((), padded.dtype))


def shards(
    cotangent,
    block_input,
    filtered,
    spectral_saved,
    spectral_gain,
    w_in,
    w_out,
    w_disco,
    quad_weights,
    lat_offsets,
    lon_offsets,
    weight_index,
):
    channels, rows, columns = cotangent.shape
    lat_count = lax.axis_size("lat")
    first_row = lax.axis_index("lat") * rows
    cells = rows * columns
    flat_in = filtered.reshape(channels, cells)
    flat_cot = cotangent.reshape(channels, cells)
    hidden_pre = lax.dot_general(
        w_in, flat_in, (((0,), (0,)), ((), ())), preferred_element_type=jnp.float32
    )
    activation = gelu_value(hidden_pre).astype(jnp.bfloat16)
    grad_act = jnp.dot(w_out, flat_cot, preferred_element_type=jnp.float32)
    grad_pre = (grad_act * gelu_slope(hidden_pre)).astype(jnp.bfloat16)
    grad_in_part = lax.dot_general(
        flat_in, grad_pre, (((1,), (1,)), ((), ())), preferred_element_type=jnp.float32
    )
    grad_out_part = lax.dot_general(
        activation, flat_cot, (((1,), (1,)), ((), ())), preferred_element_type=jnp.float32
    )
    grad_flat = jnp.dot(w_in, grad_pre, preferred_element_type=jnp.float32).astype(jnp.bfloat16)
    grad_filtered = grad_flat.reshape(channels, rows, columns)
    spread = lax.all_to_all(grad_filtered, "lon", split_axis=0, concat_axis=2, tiled=True)
    local_channels = spread.shape[0]
    coeffs = (
        jnp.dot(
            spread.reshape(local_channels * rows, NLON),
            forward_table(),
            preferred_element_type=jnp.float32,
        )
        .astype(jnp.bfloat16)
        .reshape(local_channels, rows, 2, M)
    )
    theta_rows = ((first_row + jnp.arange(rows, dtype=jnp.int32)).astype(jnp.float32) + 0.5) * (
        math.pi / NLAT
    )
    legendre = legendre_rows(theta_rows).astype(jnp.bfloat16)
    owned_count = L // lat_count
    weights = lax.slice_in_dim(legendre, 0, owned_count * lax.axis_size("lat"), axis=0)
    owned = lax.psum_scatter(
        jnp.einsum("ljm,cjrm->lcrm", weights, coeffs, preferred_element_type=jnp.float32),
        "lat",
        scatter_dimension=0,
        tiled=True,
    )
    real_part = owned[:, :, 0]
    imag_part = owned[:, :, 1]
    grad_gain = jnp.stack(
        [
            real_part * spectral_saved[:, :, 0] + imag_part * spectral_saved[:, :, 1],
            imag_part * spectral_saved[:, :, 0] - real_part * spectral_saved[:, :, 1],
        ],
        axis=2,
    )
    scaled = jnp.stack(
        [
            spectral_gain[:, :, 0] * real_part + spectral_gain[:, :, 1] * imag_part,
            spectral_gain[:, :, 0] * imag_part - spectral_gain[:, :, 1] * real_part,
        ],
        axis=2,
    ).astype(jnp.bfloat16)
    piece = lax.all_gather(scaled, "lat", axis=0, tiled=True)
    weights = lax.slice_in_dim(legendre, 0, piece.shape[0], axis=0)
    synthesis = (
        jnp.zeros((local_channels, rows, 2, M), jnp.float32)
        + jnp.einsum("ljm,lcrm->cjrm", weights, piece, preferred_element_type=jnp.float32)
    ).astype(jnp.bfloat16)
    grid_rows = jnp.dot(
        synthesis.reshape(local_channels * rows, 2 * M),
        inverse_table(),
        preferred_element_type=jnp.float32,
    ).reshape(local_channels, rows, NLON)
    spectral_grad = lax.all_to_all(grid_rows, "lon", split_axis=2, concat_axis=0, tiled=True)
    kernel = disco_kernel(quad_weights, lat_offsets, lon_offsets, weight_index)
    kernel_pad = jnp.pad(kernel, ((REACH, REACH), (0, 0), (0, 0)))
    kernel_rim = lax.dynamic_slice_in_dim(kernel_pad, first_row, rows + 2 * REACH, 0)
    stacked_rims = padded_2(
        jnp.stack((block_input, grad_filtered)), (("lat", 2), ("lon", 3)), REACH
    )
    input_pad = inside_rows(stacked_rims[0], first_row)
    grad_source = inside_rows(stacked_rims[1], first_row)
    grad_pad = lax.dot_general(
        w_disco, grad_source, (((1,), (0,)), ((), ())), preferred_element_type=jnp.float32
    ).astype(jnp.bfloat16)
    mixed = disco_apply(input_pad, kernel_rim[REACH : REACH + rows]).astype(jnp.bfloat16)
    grad_disco_part = lax.dot_general(
        mixed.reshape(channels, cells),
        grad_flat,
        (((1,), (1,)), ((), ())),
        preferred_element_type=jnp.float32,
    )
    disco_grad = disco_adjoint(grad_pad, kernel_rim)
    grad_input = (spectral_grad + disco_grad).astype(jnp.bfloat16)
    total_in, total_out, total_disco = lax.psum(
        (grad_in_part, grad_out_part, grad_disco_part), ("lat", "lon")
    )
    scale = 1.0 / math.sqrt(NLAT * NLON)
    return (grad_input, grad_gain, total_in * scale, total_out * scale, total_disco * scale)


def solution(mesh):
    placed = (
        P(None, "lat", "lon"),
        P(None, "lat", "lon"),
        P(None, "lat", "lon"),
        P("lat", "lon", None, None),
        P("lat", "lon", None, None),
        P(),
        P(),
        P(),
        P(),
        P(),
        P(),
        P(),
    )
    return jax.shard_map(
        shards,
        mesh=mesh,
        in_specs=placed,
        out_specs=(P(None, "lat", "lon"), P("lat", "lon", None, None), P(), P(), P()),
        check_vma=False,
    )
```

profile of v0, /device:TPU:0, one launch (start us, length us, event | category | flops | bytes accessed | tf_op | source)
XLA Modules:
  0.0 1276.3 jit_solution(12290076395764992815)
XLA Ops:
  8.0 15.5 %copy.126 = bf16[32,8,32,512]{3,1,2,0:T(8,128)(2,1)} copy(bf16[32,8,32,512]{3,2,1,0:T(8,128)(2,1)} %bitcast.195) | data formatting | bytes 16777216
  23.6 15.9 %copy.127 = bf16[32,8,32,512]{3,1,2,0:T(8,128)(2,1)} copy(bf16[32,8,32,512]{3,2,1,0:T(8,128)(2,1)} %bitcast.196) | data formatting | bytes 16777216
  39.4 16.7 %fusion.100 = f32[512,16384]{1,0:T(8,128)} fusion(bf16[256,512]{1,0:T(8,128)(2,1)S(1)} %copy-done, bf16[256,16384]{1,0:T(8,128)(2,1)} %bitcast.191), kind=kOutput, calls=%fused_computation.198 | convolution fusion | flops 4294967296 | bytes 42205184 | tf_op jit(solution)/shard_map/dot_general | solution.py:194
  56.1 18.3 %fusion.11 = bf16[512,16384]{1,0:T(8,128)(2,1)} fusion(f32[512,16384]{1,0:T(8,128)} %fusion.100, bf16[512,256]{1,0:T(8,128)(2,1)S(1)} %copy-done.31, bf16[256,16384]{1,0:T(8,128)(2,1)S(1)} %bitcast.200), kind=kOutput, calls=%fused_computation.17 | convolution fusion | flops 4378853376 | bytes 58982400 | tf_op jit(solution)/shard_map/dot_general | solution.py:198
  74.4 13.7 %convolution_convert_fusion = bf16[16384,256]{1,0:T(8,128)(2,1)} fusion(bf16[512,16384]{1,0:T(8,128)(2,1)} %fusion.11, bf16[256,512]{1,0:T(8,128)(2,1)S(1)} %copy-done), kind=kOutput, calls=%fused_computation.20 | convolution fusion | flops 4299161600 | bytes 25427968 | tf_op jit(solution)/shard_map/dot_general | solution.py:206
  88.1 14.6 %copy.97 = bf16[256,32,512]{2,1,0:T(8,128)(2,1)} copy(bf16[256,32,512]{0,2,1:T(8,128)(2,1)} %bitcast.180) | data formatting | bytes 16777216 | tf_op jit(solution)/shard_map/reshape | solution.py:207
  102.8 7.1 all-to-all-start
  110.0 269.4 %while.18 = (s32[]{:T(128)}, f32[32,128]{1,0:T(8,128)S(1)}, f32[32,128]{1,0:T(8,128)S(1)}, f32[128,32,128]{2,1,0:T(8,128)S(1)}, s32[128]{0:T(128)S(1)}, /*index=...) while((s32[]{:T(128)}, f32[32,128]{1,0:T(8,128)S(1)}, ...), condition=%wide.region_1.2_spmd.clone.clone.clone, body=%wide.region_0.1_spmd.sunk.clone.clone.clone.sunk | while | flops 33027 | bytes 88491 | solution.py:91
  385.3 16.4 %copy.98 = bf16[128,32,2,512]{3,2,1,0:T(2,128)(2,1)} copy(bf16[128,32,2,512]{3,1,0,2:T(8,128)(2,1)} %bitcast.3) | data formatting | bytes 16777216 | tf_op jit(solution)/shard_map/all_to_all | solution.py:208
  401.8 9.4 copy.128
  411.1 7.1 convolution_convert_fusion.1
  422.1 5.5 copy.99
  427.7 9.7 convolution_bitcast_fusion
  437.4 18.1 %copy.101 = f32[128,128,2,128]{3,1,2,0:T(8,128)} copy(f32[128,128,2,128]{0,1,2,3:T(8,128)} %convolution_bitcast_fusion) | data formatting | bytes 33554432 | tf_op jit(solution)/shard_map/ljm,cjrm->lcrm/transpose | solution.py:226
  461.5 175.9 %reduce-scatter.2.cloned.1.call-done = f32[8,128,2,128]{3,1,2,0:T(8,128)} async-done(((f32[128,128,2,128]{3,1,2,0:T(8,128)}), f32[8,128,2,128]{3,1,2,0:T(8,128)}) %reduce-scatter.2.cloned.1.call-update) | async-done | bytes 1048592 | tf_op jit(solution)/shard_map/reduce_scatter | solution.py:225
  641.0 13.8 %copy.109 = bf16[256,32,512]{0,2,1:T(8,128)(2,1)} copy(bf16[256,32,512]{2,1,0:T(8,128)(2,1)} %param.18) | data formatting | bytes 16777216 | tf_op args[1]
  667.6 16.9 %fusion.12 = f32[512,256]{1,0:T(8,128)} fusion(bf16[256,16384]{1,0:T(8,128)(2,1)} %bitcast.197, f32[512,16384]{1,0:T(8,128)} %fusion.100), kind=kOutput, calls=%fused_computation.22 | convolution fusion | flops 4336910336 | bytes 42467328 | tf_op jit(solution)/shard_map/dot_general | solution.py:203
  684.5 13.6 %convolution_bitcast_fusion.1 = f32[256,512]{0,1:T(8,128)} fusion(bf16[512,16384]{1,0:T(8,128)(2,1)} %fusion.11, bf16[256,16384]{1,0:T(8,128)(2,1)} %bitcast.192), kind=kOutput, calls=%fused_computation.41 | convolution fusion | flops 4294967296 | bytes 25690112 | tf_op jit(solution)/shard_map/dot_general | solution.py:200
  705.2 25.1 %pad_maximum_fusion = bf16[2,256,36,516]{1,3,2,0:T(8,128)(2,1)} fusion(bf16[2,256,36,2]{1,3,2,0:T(2,128)(2,1)S(1)} %collective-permute-done.3, bf16[2,256,2,512]{1,3,2,0:T(8,128)(2,1)} %collective-permute-done.1, bf16[1,256,32,512]{1,3,2,0:T(8,128)(2,1)} %bitcast.183, bf16[1,256,32,512]{1,3,2,0:T(8,128)(2,1)S(1)} %bitcast.188, ...), kind=kLoop, calls=%fused_computation.21 | loop fusion | flops 114130944 | bytes 38043648 | tf_op jit(solution)/shard_map/concatenate | solution.py:31
  730.3 8.0 fusion.14
  738.3 12.8 %copy.103 = bf16[128,128,2,128]{1,0,2,3:T(8,128)(2,1)} copy(bf16[128,128,2,128]{3,1,2,0:T(8,128)(2,1)} %all-gather.2.cloned.1.call-done) | data formatting | bytes 16777216 | tf_op jit(solution)/shard_map/all_gather | solution.py:247
  757.1 8.2 fusion.31
  765.3 17.4 %copy.107 = f32[128,32,1024]{0,1,2:T(8,128)} copy(f32[128,32,1024]{2,0,1:T(8,128)} %fusion.31) | data formatting | bytes 33554432 | tf_op jit(solution)/shard_map/dot_general | solution.py:253
  782.7 9.8 all-to-all-start.1
  792.6 127.9 %add_convert_fusion = bf16[256,32,512]{0,2,1:T(8,128)(2,1)} fusion(bf16[256,36,516]{0,2,1:T(8,128)(2,1)} %fusion.14, f32[32]{0:T(128)S(1)} %get-tuple-element.243, f32[32]{0:T(128)S(1)} %get-tuple-element.255, f32[32]{0:T(128)S(1)} %get-tuple-element.257, f32[32]{0:T(128)S(1)} %get-tuple-element.258, f32[32]{0:T(128)S(1)} %get-tuple-element.259, ...), kind=kLoop, calls=%fused_computation.24 | loop fusion | flops 314572800 | bytes 218107008 | tf_op jit(solution)/shard_map/convert_element_type | solution.py:270
  920.5 8.9 fusion.101
  929.4 10.1 convert_bitcast_fusion
  939.5 120.4 %all-reduce.4.cloned.1.call-done = (f32[256,512]{0,1:T(8,128)}, f32[512,256]{1,0:T(8,128)}, f32[256,256]{1,0:T(8,128)}) async-done(((f32[256,512]{0,1:T(8,128)}, f32[512,256]{1,0:T(8,128)}, f32[256,256]{1,0:T(8,128)}), (f32[256,512]{0,1:T(8,128)}, f32[512,256]{1,0:T(8,128)}, f32[256,256]{1,0:T(8,128)})) %all-reduce.4.cloned.1.call-update) | async-done | bytes 1310736 | tf_op jit(solution)/shard_map/psum | solution.py:279
  1067.4 28.7 %copy.130 = f32[128,32,2,512]{0,2,3,1:T(2,128)} copy(f32[128,32,2,512]{0,1,3,2:T(8,128)} %bitcast.10) | data formatting | bytes 33554432 | tf_op jit(solution)/shard_map/all_to_all | solution.py:258
  1096.3 21.6 %all_to_all.30 = f32[256,32,512]{0,2,1:T(8,128)} reshape(f32[2,128,32,512]{1,0,3,2:T(2,128)} %bitcast.189) | data formatting | bytes 33554432 | tf_op jit(solution)/shard_map/all_to_all | solution.py:258
  1118.1 135.9 %add_convert_fusion.1 = bf16[256,32,512]{0,2,1:T(8,128)(2,1)} fusion(f32[256,32,512]{0,2,1:T(8,128)} %all_to_all.30, bf16[256,36,516]{0,2,1:T(8,128)(2,1)} %convert_bitcast_fusion, f32[32]{0:T(128)S(1)} %copy-done.17, f32[32]{0:T(128)S(1)} %copy-done.16, f32[32]{0:T(128)S(1)} %copy-done.15, f32[32]{0:T(128)S(1)} %copy-done.18, f32[32]{0:T(128)S(1)} %copy-done.14, ...), kind=kLoop, calls=%fused_computation.25 | loop fusion | flops 318767104 | bytes 234884224 | tf_op jit(solution)/shard_map/convert_element_type | solution.py:278
  1254.0 14.6 %copy.112 = bf16[256,32,512]{2,1,0:T(8,128)(2,1)} copy(bf16[256,32,512]{0,2,1:T(8,128)(2,1)} %add_convert_fusion.1) | data formatting | bytes 16777216
  (770 shorter events, 318.8 us)
Async XLA Ops:
  8.0 31.4 %copy-start = (bf16[256,512]{1,0:T(8,128)(2,1)S(1)}, bf16[256,512]{1,0:T(8,128)(2,1)}, u32[]{:S(2)}) copy-start(bf16[256,512]{1,0:T(8,128)(2,1)} %param.22) | copy-start | bytes 786436
  23.6 32.6 %slice-start.2 = ((s8[8388608]{0:T(1024)(128)(4,1)}), s8[4194304]{0:T(1024)(128)(4,1)S(1)}, s32[]{:S(2)}) async-start(s8[8388608]{0:T(1024)(128)(4,1)} %bitcast.198), calls=%async_computation.8 | async-start | bytes 8388608
  88.1 21.9 %copy-start.9 = (f32[128]{0:T(128)S(1)}, f32[128]{0:T(128)}, u32[]{:S(2)}) copy-start(f32[128]{0:T(128)} %constant.97.clone) | copy-start | bytes 1540
  102.8 282.6 %all-to-all-start = ((bf16[256,32,512]{2,1,0:T(8,128)(2,1)}), bf16[256,32,512]{2,1,0:T(8,128)(2,1)}, u32[]{:S(2)}, u32[]{:S(2)}) async-start(bf16[256,32,512]{2,1,0:T(8,128)(2,1)} %copy.97), calls=%async_computation | async-start | bytes 16777216 | tf_op jit(solution)/shard_map/all_to_all | solution.py:208
  109.8 527.5 %reduce-scatter.2.cloned.1.call-start = ((), (), s32[]{:S(2)}) async-start(), calls=%async_computation.3 | async-start | bytes 17825792 | tf_op jit(solution)/shard_map/reduce_scatter | solution.py:225
  455.5 282.7 %all-gather.2.cloned.1.call-start = ((), (), s32[]{:S(2)}) async-start(), calls=%async_computation.4 | async-start | bytes 8912896 | tf_op jit(solution)/shard_map/all_gather | solution.py:247
  657.8 40.3 %collective-permute-start = (bf16[2,256,2,512]{1,3,2,0:T(8,128)(2,1)}, bf16[2,256,2,512]{1,3,2,0:T(8,128)(2,1)}, u32[]{:S(2)}, u32[]{:S(2)}) collective-permute-start(bf16[2,256,2,512]{1,3,2,0:T(8,128)(2,1)} %get-tuple-element.220), channel_id=1, source_target_pairs={{0,2},{2,4},{4,6},{6,8},{8,10},{10,12},{12,14},{14,16},{16,18},{18... | collective-permute-start | bytes 3145736 | tf_op jit(solution)/shard_map/ppermute | solution.py:27
  657.8 40.3 %collective-permute-start.1 = (bf16[2,256,2,512]{1,3,2,0:T(8,128)(2,1)}, bf16[2,256,2,512]{1,3,2,0:T(8,128)(2,1)}, u32[]{:S(2)}, u32[]{:S(2)}) collective-permute-start(bf16[2,256,2,512]{1,3,2,0:T(8,128)(2,1)} %get-tuple-element.221), channel_id=1, source_target_pairs={{2,0},{4,2},{6,4},{8,6},{10,8},{12,10},{14,12},{16,14},{18,16},{20... | collective-permute-start | bytes 3145736 | tf_op jit(solution)/shard_map/ppermute | solution.py:30
  664.5 33.7 %slice-start = ((s8[8388608]{0:T(1024)(128)(4,1)}), s8[4194304]{0:T(1024)(128)(4,1)S(1)}, s32[]{:S(2)}) async-start(s8[8388608]{0:T(1024)(128)(4,1)} %bitcast.185), calls=%async_computation.6 | async-start | bytes 8388608
  667.6 30.5 %slice-start.1 = ((s8[8388608]{0:T(1024)(128)(4,1)}), s8[4194304]{0:T(1024)(128)(4,1)S(1)}, s32[]{:S(2)}) async-start(s8[8388608]{0:T(1024)(128)(4,1)} %bitcast.185), calls=%async_computation.7 | async-start | bytes 8388608
  699.3 4.4 collective-permute-start.2
  700.9 4.4 collective-permute-start.3
  782.7 284.7 %all-to-all-start.1 = ((f32[128,32,1024]{0,1,2:T(8,128)}), f32[128,32,1024]{0,1,2:T(8,128)}, u32[]{:S(2)}, u32[]{:S(2)}) async-start(f32[128,32,1024]{0,1,2:T(8,128)} %copy.107), calls=%async_computation.2 | async-start | bytes 33554432 | tf_op jit(solution)/shard_map/all_to_all | solution.py:258
  792.5 267.4 %all-reduce.4.cloned.1.call-start = ((), (), s32[]{:S(2)}) async-start(), calls=%async_computation.5 | async-start | bytes 2621440 | tf_op jit(solution)/shard_map/psum | solution.py:279
  929.4 136.2 %copy-start.4 = (f32[8,128,1,128]{3,1,2,0:T(8,128)S(1)}, f32[8,128,1,128]{3,1,2,0:T(8,128)}, u32[]{:S(2)}) copy-start(f32[8,128,1,128]{3,1,2,0:T(8,128)} %get-tuple-element.222) | copy-start | bytes 1572868
  929.4 136.2 %copy-start.5 = (f32[8,128,1,128]{3,1,2,0:T(8,128)S(1)}, f32[8,128,1,128]{3,1,2,0:T(8,128)}, u32[]{:S(2)}) copy-start(f32[8,128,1,128]{3,1,2,0:T(8,128)} %get-tuple-element.223) | copy-start | bytes 1572868
  1096.1 21.8 %copy-start.10 = (f32[32]{0:T(128)S(1)}, f32[32]{0:T(128)}, u32[]{:S(2)}) copy-start(f32[32]{0:T(128)} %get-tuple-element.245) | copy-start | bytes 388
  1096.1 21.8 %copy-start.11 = (f32[32]{0:T(128)S(1)}, f32[32]{0:T(128)}, u32[]{:S(2)}) copy-start(f32[32]{0:T(128)} %get-tuple-element.246) | copy-start | bytes 388
  1096.2 21.8 %copy-start.12 = (f32[32]{0:T(128)S(1)}, f32[32]{0:T(128)}, u32[]{:S(2)}) copy-start(f32[32]{0:T(128)} %get-tuple-element.247) | copy-start | bytes 388
  1096.2 21.8 %copy-start.13 = (f32[32]{0:T(128)S(1)}, f32[32]{0:T(128)}, u32[]{:S(2)}) copy-start(f32[32]{0:T(128)} %get-tuple-element.248) | copy-start | bytes 388
  1096.2 21.8 %copy-start.14 = (f32[32]{0:T(128)S(1)}, f32[32]{0:T(128)}, u32[]{:S(2)}) copy-start(f32[32]{0:T(128)} %get-tuple-element.249) | copy-start | bytes 388
  1096.2 21.8 %copy-start.15 = (f32[32]{0:T(128)S(1)}, f32[32]{0:T(128)}, u32[]{:S(2)}) copy-start(f32[32]{0:T(128)} %get-tuple-element.250) | copy-start | bytes 388
  1096.2 21.8 %copy-start.16 = (f32[32]{0:T(128)S(1)}, f32[32]{0:T(128)}, u32[]{:S(2)}) copy-start(f32[32]{0:T(128)} %get-tuple-element.251) | copy-start | bytes 388
  1096.2 21.8 %copy-start.17 = (f32[32]{0:T(128)S(1)}, f32[32]{0:T(128)}, u32[]{:S(2)}) copy-start(f32[32]{0:T(128)} %get-tuple-element.252) | copy-start | bytes 388
  1096.2 21.8 %copy-start.18 = (f32[32]{0:T(128)S(1)}, f32[32]{0:T(128)}, u32[]{:S(2)}) copy-start(f32[32]{0:T(128)} %get-tuple-element.253) | copy-start | bytes 388
  1096.2 21.8 %copy-start.19 = (f32[32]{0:T(128)S(1)}, f32[32]{0:T(128)}, u32[]{:S(2)}) copy-start(f32[32]{0:T(128)} %get-tuple-element.254) | copy-start | bytes 388
  1096.2 21.8 %copy-start.20 = (f32[32]{0:T(128)S(1)}, f32[32]{0:T(128)}, u32[]{:S(2)}) copy-start(f32[32]{0:T(128)} %get-tuple-element.233) | copy-start | bytes 388
  1096.2 21.8 %copy-start.21 = (f32[32]{0:T(128)S(1)}, f32[32]{0:T(128)}, u32[]{:S(2)}) copy-start(f32[32]{0:T(128)} %get-tuple-element.234) | copy-start | bytes 388
  1096.3 21.8 %copy-start.22 = (f32[32]{0:T(128)S(1)}, f32[32]{0:T(128)}, u32[]{:S(2)}) copy-start(f32[32]{0:T(128)} %get-tuple-element.235) | copy-start | bytes 388
  1096.3 21.8 %copy-start.23 = (f32[32]{0:T(128)S(1)}, f32[32]{0:T(128)}, u32[]{:S(2)}) copy-start(f32[32]{0:T(128)} %get-tuple-element.236) | copy-start | bytes 388
  1096.3 21.8 %copy-start.24 = (f32[32]{0:T(128)S(1)}, f32[32]{0:T(128)}, u32[]{:S(2)}) copy-start(f32[32]{0:T(128)} %get-tuple-element.237) | copy-start | bytes 388
  1118.1 150.5 %copy-start.1 = (bf16[256,512]{1,0:T(8,128)(2,1)S(1)}, bf16[256,512]{1,0:T(8,128)(2,1)}, u32[]{:S(2)}) copy-start(bf16[256,512]{1,0:T(8,128)(2,1)} %param.22) | copy-start | bytes 786436
  (14 other events, 275.1 us)
Sparse Core Ops, SparseCore 0:
  455.7 181.6 reduce-scatter.1
  641.0 83.3 all-gather.1
Sparse Core Ops, SparseCore 1:
  929.5 130.4 all-reduce.3
where the time goes:
time: 1300 us; the launch traced here: 1280 us
  other arithmetic  417 us (32%)
  local copies, waits for them, and re-layouts  388 us (30%)
  waiting for transfers between devices  300 us (23%)
  matrix products  128 us (10%)
  starting transfers between devices  23.5 us (2%)
  between operations  16.4 us (1%)
    reduce_scatter x1, waiting for transfers between devices, shards(): lax.psum_scatter(jnp.einsum('ljm,cjrm->lcrm', weights, coeffs, preferred_...  176 us
    convert_element_type x1, other arithmetic, shards(): grad_input = (spectral_grad + disco_grad).astype(jnp.bfloat16)  136 us
    convert_element_type x1, other arithmetic, shards(): disco_apply(input_pad, kernel_rim[REACH:REACH + rows]).astype(jnp.bfloat16)  128 us
    psum x1, waiting for transfers between devices, shards(): lax.psum((grad_in_part, grad_out_part, grad_disco_part), ('lat', 'lon'))  120 us
    mul x128, local copies, waits for them, and re-layouts, advance(): coef_up[None, :] * (cosine * previous - coef_low[None, :] * before)  91.6 us
    eq x128, other arithmetic, advance(): orders == degree  83.1 us
    dynamic_slice x128, local copies, waits for them, and re-layouts, legendre_rows(): lax.scan(advance, (empty, empty), (jnp.arange(L, dtype=jnp.int32), jnp.as...  75 us
    unnamed x81, local copies, waits for them, and re-layouts  72.1 us
  transfers between devices with their start and end apart: 9, of which 4 were waited for; matrix products, arithmetic and copies ran while one was open for 41% of the time, Pallas kernels for 0%

commit v1 on v0

--- a/solution.py
+++ b/solution.py
@@ -1,9 +1,12 @@
+import functools
 import math
 
 import jax
 import jax.numpy as jnp
 import numpy as np
 from jax import lax
+from jax.experimental import pallas as pl
+from jax.experimental.pallas import tpu as pltpu
 from jax.sharding import PartitionSpec as P
 
 NLAT = 512
@@ -48,7 +51,10 @@
     order = np.arange(M)[None, :] * 1.0
     upper = np.where(
         degree > order,
-        np.sqrt((4.0 * degree * degree - 1.0) / np.maximum(degree * degree - order * order, 1.0)),
+        np.sqrt(
+            np.maximum(4.0 * degree * degree - 1.0, 0.0)
+            / np.maximum(degree * degree - order * order, 1.0)
+        ),
         0.0,
     )
     lower = np.where(
@@ -171,7 +177,7 @@
     return jnp.where(keep[None, :, None], padded, jnp.zeros((), padded.dtype))
 
 
-def shards(
+def shards_general(
     cotangent,
     block_input,
     filtered,
@@ -283,6 +289,575 @@
     return (grad_input, grad_gain, total_in * scale, total_out * scale, total_disco * scale)
 
 
+BAND = 16
+LANES = 128
+MIB = 1024 * 1024
+
+
+def mm(a, b):
+    return jnp.dot(a, b, preferred_element_type=jnp.float32)
+
+
+def mm_nt(a, b):
+    return lax.dot_general(a, b, (((1,), (1,)), ((), ())), preferred_element_type=jnp.float32)
+
+
+def mm_tn(a, b):
+    return lax.dot_general(a, b, (((0,), (0,)), ((), ())), preferred_element_type=jnp.float32)
+
+
+def params(mib):
+    return pltpu.CompilerParams(vmem_limit_bytes=mib * MIB)
+
+
+def whole_block(shape):
+    return pl.BlockSpec(shape, lambda *_: (0,) * len(shape))
+
+
+def rows_first(block, stage, flat, width):
+    channels = block.shape[0]
+    for tile in range(width // LANES):
+        stage[tile] = (
+            block[:, :, tile * LANES : (tile + 1) * LANES]
+            .astype(jnp.float32)
+            .reshape(channels * BAND, LANES)
+        )
+    for row in range(BAND):
+        for tile in range(width // LANES):
+            start = row * width + tile * LANES
+            flat[:, start : start + LANES] = stage[
+                tile, pl.ds(row, channels, stride=BAND), :
+            ].astype(jnp.bfloat16)
+
+
+def gelu_both(value):
+    decay = jnp.exp(value * value * -0.5)
+    base = 1.0 + (0.3275911 * root_half) * jnp.abs(value)
+    inverse = pl.reciprocal(base, approx=True)
+    inverse = inverse * (2.0 - base * inverse)
+    poly = 0.5 * 1.061405429
+    for term in (-1.453152027, 1.421413741, -0.284496736, 0.254829592):
+        poly = poly * inverse + 0.5 * term
+    tail = poly * inverse * decay
+    chance = jnp.where(value >= 0.0, 1.0 - tail, tail)
+    return chance, decay
+
+
+def mlp_kernel(
+    side, x_ref, ct_ref, win_t, win, wout, table,
+    gf_ref, own_ref, send_ref, edge_ref, gin_ref, gout_ref,
+    stage, xs, cs, low, high,
+    *, steps, width, chunk,
+):
+    step = pl.program_id(0)
+
+    @pl.when(step == 0)
+    def _():
+        gin_ref[...] = jnp.zeros_like(gin_ref)
+        gout_ref[...] = jnp.zeros_like(gout_ref)
+
+    rows_first(x_ref, stage, xs, width)
+    rows_first(ct_ref, stage, cs, width)
+    column = pl.multiple_of(step * width, width)
+    per = chunk // width
+
+    def body(index, carry):
+        cells = pl.ds(pl.multiple_of(index * chunk, chunk), chunk)
+        x = xs[:, cells]
+        c = cs[:, cells]
+        pre = mm(win_t[...], x)
+        grad = mm(wout[...], c)
+        chance, decay = gelu_both(pre)
+        act = (pre * chance).astype(jnp.bfloat16)
+        gp = (grad * (chance + pre * decay * (1.0 / root_two_pi))).astype(jnp.bfloat16)
+        gf = mm(win[...], gp).astype(jnp.bfloat16)
+        for part in range(per):
+            gf_ref[index * per + part, :, pl.ds(column, width)] = gf[
+                :, part * width : (part + 1) * width
+            ]
+        gin_ref[...] += mm_nt(x, gp)
+        gout_ref[...] += mm_nt(act, c)
+        return carry
+
+    lax.fori_loop(0, BAND * width // chunk, body, 0)
+
+    @pl.when(step == steps - 1)
+    def _():
+        orders = low.shape[0] // BAND
+
+        def transform(row, carry):
+            out = mm_nt(table[...], gf_ref[row])
+            low[pl.ds(row, orders, stride=BAND), :] = out[:orders, :LANES]
+            high[pl.ds(row, orders, stride=BAND), :] = out[:orders, LANES:]
+            edge_ref[row] = out[orders:].astype(jnp.bfloat16)
+            return carry
+
+        lax.fori_loop(0, BAND, transform, 0)
+        first = side[0] == 0
+        shape = own_ref.shape
+
+        @pl.when(first)
+        def _():
+            own_ref[...] = low[...].astype(jnp.bfloat16).reshape(shape)
+            send_ref[...] = high[...].astype(jnp.bfloat16).reshape(shape)
+
+        @pl.when(jnp.logical_not(first))
+        def _():
+            own_ref[...] = high[...].astype(jnp.bfloat16).reshape(shape)
+            send_ref[...] = low[...].astype(jnp.bfloat16).reshape(shape)
+
+
+def mlp_call(band, side, filtered, cotangent, win_t, win, wout, table):
+    channels, rows, columns = filtered.shape
+    hidden = wout.shape[0]
+    width = LANES
+    steps = columns // width
+    chunk = 4 * width
+    orders = table.shape[0] - 16
+    block = pl.BlockSpec((channels, BAND, width), lambda i: (0, band, i))
+    cells = BAND * columns
+    return pl.pallas_call(
+        functools.partial(mlp_kernel, steps=steps, width=width, chunk=chunk),
+        grid=(steps,),
+        in_specs=[
+            pl.BlockSpec(memory_space=pltpu.SMEM),
+            block,
+            block,
+            whole_block(win_t.shape),
+            whole_block(win.shape),
+            whole_block(wout.shape),
+            whole_block(table.shape),
+        ],
+        out_specs=[
+            whole_block((BAND, channels, columns)),
+            whole_block((orders, BAND, LANES)),
+            whole_block((orders, BAND, LANES)),
+            whole_block((BAND, 16, channels)),
+            whole_block((channels, hidden)),
+            whole_block((hidden, channels)),
+        ],
+        out_shape=[
+            jax.ShapeDtypeStruct((BAND, channels, columns), jnp.bfloat16),
+            jax.ShapeDtypeStruct((orders, BAND, LANES), jnp.bfloat16),
+            jax.ShapeDtypeStruct((orders, BAND, LANES), jnp.bfloat16),
+            jax.ShapeDtypeStruct((BAND, 16, channels), jnp.bfloat16),
+            jax.ShapeDtypeStruct((channels, hidden), jnp.float32),
+            jax.ShapeDtypeStruct((hidden, channels), jnp.float32),
+        ],
+        scratch_shapes=[
+            pltpu.VMEM((width // LANES, channels * BAND, LANES), jnp.float32),
+            pltpu.VMEM((channels, BAND * width), jnp.bfloat16),
+            pltpu.VMEM((channels, BAND * width), jnp.bfloat16),
+            pltpu.VMEM((orders * BAND, LANES), jnp.float32),
+            pltpu.VMEM((orders * BAND, LANES), jnp.float32),
+        ],
+        compiler_params=params(56),
+        cost_estimate=pl.CostEstimate(
+            flops=2 * cells * channels * (5 * hidden + orders),
+            bytes_accessed=6 * channels * cells,
+            transcendentals=2 * hidden * cells,
+        ),
+        name="mlp",
+    )(side, filtered, cotangent, win_t, win, wout, table)
+
+
+def stencil_kernel(
+    taps, first, second, top, bottom, edges, place, bi_ref,
+    q_ref, gd_ref,
+    field, rim, stage, flat,
+    *, rows,
+):
+    band = pl.program_id(0)
+    channels, columns = field.shape[1:]
+
+    @pl.when(band == 0)
+    def _():
+        gd_ref[...] = jnp.zeros_like(gd_ref)
+        field[0:REACH] = top[...]
+        field[REACH : REACH + BAND] = first[...]
+        field[REACH + BAND : REACH + 2 * BAND] = second[...]
+        field[rows + REACH :] = bottom[...]
+
+        def spread(row, carry):
+            rim[row] = mm_tn(edges[row], place[...]).astype(jnp.bfloat16)
+            return carry
+
+        lax.fori_loop(0, rows + 2 * REACH, spread, 0)
+
+    rows_first(bi_ref, stage, flat, columns)
+    lane = lax.broadcasted_iota(jnp.int32, (16, LANES), 1)
+    span = 2 * REACH + 1
+
+    def row_body(row, carry):
+        top_row = band * BAND + row
+
+        def tile_body(tile, inner):
+            part = pl.ds(pl.multiple_of(tile * 16, 16), 16)
+            sums = [None] * span
+            for north in range(span):
+                source = top_row + 2 * REACH - north
+                here = field[source, part, :].astype(jnp.float32)
+                ends = rim[source, part, :].astype(jnp.float32)
+                for east in range(span):
+                    past = east - REACH
+                    shifted = here
+                    if past < 0:
+                        rim_tile = jnp.where(lane < -past, ends, here[:, :LANES])
+                        shifted = jnp.concatenate([rim_tile, here[:, LANES:]], axis=1)
+                    if past > 0:
+                        rim_tile = jnp.where(lane >= LANES - past, ends, here[:, -LANES:])
+                        shifted = jnp.concatenate([here[:, :-LANES], rim_tile], axis=1)
+                    weight = taps[(source * span + north) * span + east]
+                    term = shifted * weight
+                    sums[east] = term if sums[east] is None else sums[east] + term
+            total = sums[REACH]
+            for east in range(span):
+                if east != REACH:
+                    total = total + pltpu.roll(sums[east], (east - REACH) % columns, 1)
+            q_ref[row, part, :] = total.astype(jnp.bfloat16)
+            return inner
+
+        lax.fori_loop(0, channels // 16, tile_body, 0)
+        cells = pl.ds(pl.multiple_of(row * columns, columns), columns)
+        gd_ref[...] += mm_nt(flat[:, cells], q_ref[row])
+        return carry
+
+    lax.fori_loop(0, BAND, row_body, 0)
+
+
+def stencil_call(taps, first, second, top, bottom, edges, place, block_input):
+    channels, rows, columns = block_input.shape
+    cells = rows * columns
+    vmem = pl.BlockSpec(memory_space=pltpu.VMEM)
+    return pl.pallas_call(
+        functools.partial(stencil_kernel, rows=rows),
+        grid=(rows // BAND,),
+        in_specs=[pl.BlockSpec(memory_space=pltpu.SMEM)]
+        + [vmem] * 6
+        + [pl.BlockSpec((channels, BAND, columns), lambda i: (0, i, 0))],
+        out_specs=[
+            pl.BlockSpec((BAND, channels, columns), lambda i: (i, 0, 0)),
+            whole_block((channels, channels)),
+        ],
+        out_shape=[
+            jax.ShapeDtypeStruct((rows, channels, columns), jnp.bfloat16),
+            jax.ShapeDtypeStruct((channels, channels), jnp.float32),
+        ],
+        scratch_shapes=[
+            pltpu.VMEM((rows + 2 * REACH, channels, columns), jnp.bfloat16),
+            pltpu.VMEM((rows + 2 * REACH, channels, LANES), jnp.bfloat16),
+            pltpu.VMEM((columns // LANES, channels * BAND, LANES), jnp.float32),
+            pltpu.VMEM((channels, BAND * columns), jnp.bfloat16),
+        ],
+        compiler_params=params(60),
+        cost_estimate=pl.CostEstimate(
+            flops=60 * channels * cells + 2 * channels * channels * cells,
+            bytes_accessed=6 * channels * cells,
+            transcendentals=0,
+        ),
+        name="stencil",
+    )(taps, first, second, top, bottom, edges, place, block_input)
+
+
+def legendre_kernel(leg, r0, r1, gain, owned_ref, s0, s1, stage, *, steps, block):
+    order = pl.program_id(0)
+    degrees = leg.shape[1]
+    half = leg.shape[2] // 2
+    total = None
+    for band, ref in enumerate((r0, r1)):
+        pair = jnp.concatenate(
+            [ref[:, r].reshape(half, LANES) for r in range(2)], axis=1
+        )
+        term = mm(leg[0, :, band * half : (band + 1) * half], pair)
+        total = term if total is None else total + term
+    real = total[:, :LANES]
+    imag = total[:, LANES:]
+    owned_ref[:, 0, 0] = real.reshape(owned_ref.shape[0], -1, LANES)
+    owned_ref[:, 0, 1] = imag.reshape(owned_ref.shape[0], -1, LANES)
+    g = gain[:, 0, 0].reshape(degrees, LANES)
+    k = gain[:, 0, 1].reshape(degrees, LANES)
+    scaled = jnp.concatenate([g * real + k * imag, g * imag - k * real], axis=1).astype(
+        jnp.bfloat16
+    )
+    synth = mm_tn(leg[0], scaled)
+    for r in range(2):
+        stage[pl.ds(r * steps + order, 2 * half, stride=block), :] = synth[
+            :, r * LANES : (r + 1) * LANES
+        ]
+
+    @pl.when(order == steps - 1)
+    def _():
+        s0[...] = stage[: half * block].astype(jnp.bfloat16).reshape(s0.shape)
+        s1[...] = stage[half * block :].astype(jnp.bfloat16).reshape(s1.shape)
+
+
+def legendre_call(leg, r0, r1, gain):
+    owners, _, steps, band, lanes = r0.shape
+    degrees = leg.shape[1]
+    block = 2 * steps
+    r_spec = pl.BlockSpec((owners, 2, None, band, lanes), lambda m: (0, 0, m, 0, 0))
+    g_shape = (owners, 1, 2, degrees // owners, lanes)
+    g_spec = pl.BlockSpec(g_shape, lambda m: (0, m, 0, 0, 0))
+    out = (owners, band, block, lanes)
+    return pl.pallas_call(
+        functools.partial(legendre_kernel, steps=steps, block=block),
+        grid=(steps,),
+        in_specs=[
+            pl.BlockSpec((1, degrees, leg.shape[2]), lambda m: (m, 0, 0)),
+            r_spec,
+            r_spec,
+            g_spec,
+        ],
+        out_specs=[g_spec, whole_block(out), whole_block(out)],
+        out_shape=[
+            jax.ShapeDtypeStruct(gain.shape, jnp.float32),
+            jax.ShapeDtypeStruct(out, jnp.bfloat16),
+            jax.ShapeDtypeStruct(out, jnp.bfloat16),
+        ],
+        scratch_shapes=[pltpu.VMEM((2 * owners * band * block, lanes), jnp.float32)],
+        compiler_params=params(48),
+        cost_estimate=pl.CostEstimate(
+            flops=8 * steps * degrees * leg.shape[2] * 256,
+            bytes_accessed=7 * MIB,
+            transcendentals=0,
+        ),
+        name="legendre",
+    )(leg, r0, r1, gain)
+
+
+def final_kernel(side, q_ref, own, other, table, wd, *rest):
+    out_ref, stage = rest[-2:]
+    width = q_ref.shape[2]
+    orders = table.shape[0]
+
+    def body(row, carry):
+        q = q_ref[row]
+        for half, ref in enumerate((own, other)):
+            base = pl.multiple_of((side[0] + half) % 2 * LANES, LANES)
+            synth = ref[:, row].reshape(orders, LANES)
+            out = mm_tn(synth, table[...]) + mm(wd[pl.ds(base, LANES), :], q)
+            for tile in range(width // LANES):
+                stage[tile, pl.ds(base * BAND + row, LANES, stride=BAND), :] = out[
+                    :, tile * LANES : (tile + 1) * LANES
+                ]
+        return carry
+
+    lax.fori_loop(0, BAND, body, 0)
+    channels = out_ref.shape[0]
+    for tile in range(width // LANES):
+        out_ref[:, :, tile * LANES : (tile + 1) * LANES] = (
+            stage[tile].astype(jnp.bfloat16).reshape(channels, BAND, LANES)
+        )
+
+
+def final_call(band, side, q, own, other, table, wd, previous):
+    rows, channels, columns = q.shape
+    width = 2 * LANES
+    cells = BAND * columns
+    extra = [] if previous is None else [previous]
+    return pl.pallas_call(
+        final_kernel,
+        grid=(columns // width,),
+        in_specs=[
+            pl.BlockSpec(memory_space=pltpu.SMEM),
+            pl.BlockSpec((BAND, channels, width), lambda i: (band, 0, i)),
+            whole_block(own.shape),
+            whole_block(other.shape),
+            pl.BlockSpec((table.shape[0], width), lambda i: (0, i)),
+            whole_block(wd.shape),
+        ]
+        + [pl.BlockSpec(memory_space=pl.ANY)] * len(extra),
+        out_specs=pl.BlockSpec((channels, BAND, width), lambda i: (0, band, i)),
+        out_shape=jax.ShapeDtypeStruct((channels, rows, columns), jnp.bfloat16),
+        scratch_shapes=[pltpu.VMEM((width // LANES, channels * BAND, LANES), jnp.float32)],
+        input_output_aliases={6: 0} if extra else {},
+        compiler_params=params(48),
+        cost_estimate=pl.CostEstimate(
+            flops=2 * cells * channels * (channels + table.shape[0]),
+            bytes_accessed=5 * channels * cells,
+            transcendentals=0,
+        ),
+        name="final",
+    )(side, q, own, other, table, wd, *extra)
+
+
+def gain_kernel(gain, out, *, degrees):
+    for degree in range(degrees):
+        for r in range(2):
+            part = gain[pl.ds(degree * 2 * LANES + r, LANES, stride=2), :]
+            out[pl.ds(r * degrees + degree, LANES, stride=2 * degrees), :] = part.T
+
+
+def gain_call(gain):
+    degrees, channels, _, orders = gain.shape
+    flat = gain.reshape(degrees * channels * 2, orders)
+    return pl.pallas_call(
+        functools.partial(gain_kernel, degrees=degrees),
+        out_shape=jax.ShapeDtypeStruct((orders * 2 * degrees, channels), jnp.float32),
+        name="gain",
+    )(flat)
+
+
+def grad_gain_kernel(owned, saved, out, *, degrees):
+    for degree in range(degrees):
+        real = owned[pl.ds(degree, LANES, stride=2 * degrees), :].T
+        imag = owned[pl.ds(degrees + degree, LANES, stride=2 * degrees), :].T
+        start = degree * 2 * LANES
+        s = saved[pl.ds(start, LANES, stride=2), :]
+        t = saved[pl.ds(start + 1, LANES, stride=2), :]
+        out[pl.ds(start, LANES, stride=2), :] = real * s + imag * t
+        out[pl.ds(start + 1, LANES, stride=2), :] = imag * s - real * t
+
+
+def grad_gain_call(owned, saved):
+    degrees, channels, _, orders = saved.shape
+    flat = saved.reshape(degrees * channels * 2, orders)
+    out = pl.pallas_call(
+        functools.partial(grad_gain_kernel, degrees=degrees),
+        out_shape=jax.ShapeDtypeStruct(flat.shape, jnp.float32),
+        name="grad_gain",
+    )(owned, flat)
+    return out.reshape(saved.shape)
+
+
+def legendre_whole():
+    upper, lower, diagonal_log = legendre_tables()
+    theta = (np.arange(NLAT) + 0.5) * (math.pi / NLAT)
+    sine, cosine = np.sin(theta)[None], np.cos(theta)[None]
+    orders = np.arange(M)
+    start = np.exp(diagonal_log[:, None] + orders[:, None] * np.log(sine))
+    table = np.zeros((M, L, NLAT))
+    previous = before = np.zeros((M, NLAT))
+    for degree in range(L):
+        fresh = np.where(
+            (orders == degree)[:, None],
+            start,
+            upper[degree][:, None] * (cosine * previous - lower[degree][:, None] * before),
+        )
+        table[:, degree] = fresh
+        previous, before = fresh, previous
+    return table * np.sqrt(sine * (math.pi / NLAT))[None]
+
+
+def host_tables(lat_count, lon_count):
+    columns, rows, own = NLON // lon_count, NLAT // lat_count, M // lat_count
+    angle = (np.arange(M)[:, None] * np.arange(NLON)[None, :] % NLON) * (2.0 * math.pi / NLON)
+    waves = np.stack([np.cos(angle), -np.sin(angle)]) / math.sqrt(NLON)
+    factor = np.where(np.arange(M) == 0, 1.0, 2.0)[None, :, None]
+
+    def arrange(table):
+        table = table.reshape(2, lat_count, own, lon_count, columns)
+        return table.transpose(3, 1, 0, 2, 4).reshape(lon_count, 2 * M, columns)
+
+    pick = np.zeros((lon_count, 16, columns))
+    for row, column in enumerate((0, 1, columns - 2, columns - 1)):
+        pick[:, row, column] = 1.0
+    forward = np.concatenate([arrange(waves * factor), pick], axis=1)
+    legendre = legendre_whole().reshape(M, L, lat_count, rows // BAND, BAND)
+    legendre = legendre.transpose(0, 1, 3, 2, 4).reshape(M, L, NLAT)
+    kind = jnp.bfloat16
+    return forward.astype(kind), arrange(waves).astype(kind), legendre.astype(kind)
+
+
+def shards_banded(
+    cotangent,
+    block_input,
+    filtered,
+    spectral_saved,
+    spectral_gain,
+    w_in,
+    w_out,
+    w_disco,
+    quad_weights,
+    lat_offsets,
+    lon_offsets,
+    weight_index,
+):
+    channels, rows, columns = cotangent.shape
+    lat_count = lax.axis_size("lat")
+    lon_count = lax.axis_size("lon")
+    lat_index = lax.axis_index("lat")
+    lon_index = lax.axis_index("lon")
+    own = M // lat_count
+    degrees = L // lat_count
+    side = lon_index.reshape(1).astype(jnp.int32)
+    forward, inverse, legendre = host_tables(lat_count, lon_count)
+    forward = lax.dynamic_index_in_dim(jnp.asarray(forward), lon_index, 0, keepdims=False)
+    inverse = lax.dynamic_index_in_dim(jnp.asarray(inverse), lon_index, 0, keepdims=False)
+    legendre = lax.dynamic_slice_in_dim(jnp.asarray(legendre), lat_index * own, own, 0)
+    swap = [(i, (i + 1) % lon_count) for i in range(lon_count)]
+    exchange = functools.partial(lax.all_to_all, axis_name="lat", split_axis=0, concat_axis=0, tiled=True)
+
+    gain = exchange(
+        gain_call(spectral_gain).reshape(lat_count, own, 2, degrees, LANES)
+    )
+    w_in_t = w_in.T
+    bands = []
+    received = []
+    for band in range(rows // BAND):
+        bands.append(mlp_call(band, side, filtered, cotangent, w_in_t, w_in, w_out, forward))
+        _, kept, sent, _, _, _ = bands[-1]
+        arrived = lax.ppermute(sent, "lon", swap)
+        summed = (kept.astype(jnp.float32) + arrived.astype(jnp.float32)).astype(jnp.bfloat16)
+        received.append(exchange(summed.reshape(lat_count, 2, own, BAND, LANES)))
+    first, second = bands[0], bands[1]
+
+    kernel = disco_kernel(quad_weights, lat_offsets, lon_offsets, weight_index)
+    kernel_pad = jnp.pad(kernel, ((REACH, REACH), (0, 0), (0, 0)))
+    kernel_rim = lax.dynamic_slice_in_dim(kernel_pad, lat_index * rows, rows + 2 * REACH, 0)
+    down = [(i, (i + 1) % lat_count) for i in range(lat_count)]
+    up = [(target, source) for source, target in down]
+    sides = lax.ppermute(jnp.concatenate([first[3], second[3]], axis=0), "lon", swap)
+    top, top_side = lax.ppermute(
+        (second[0][BAND - REACH :], sides[rows - REACH :]), "lat", down
+    )
+    bottom, bottom_side = lax.ppermute((first[0][:REACH], sides[:REACH]), "lat", up)
+    edges = jnp.concatenate([top_side, sides, bottom_side], axis=0)
+    place = np.zeros((16, LANES), np.float32)
+    for row, lane in enumerate((0, 1, LANES - 2, LANES - 1)):
+        place[row, lane] = 1.0
+    q, disco_part = stencil_call(
+        kernel_rim.reshape(-1),
+        first[0],
+        second[0],
+        top,
+        bottom,
+        edges,
+        jnp.asarray(place, jnp.bfloat16),
+        block_input,
+    )
+    total_in, total_out, total_disco = lax.psum(
+        (first[4] + second[4], first[5] + second[5], disco_part), ("lat", "lon")
+    )
+
+    owned, s0, s1 = legendre_call(legendre, received[0], received[1], gain)
+    result = None
+    for band, synth in enumerate((s0, s1)):
+        local = exchange(synth)
+        other = lax.ppermute(local, "lon", swap)
+        result = final_call(band, side, q, local, other, inverse, w_disco, result)
+    owned = exchange(owned).reshape(M * 2 * degrees, LANES)
+    grad_gain = grad_gain_call(owned, spectral_saved)
+    scale = 1.0 / math.sqrt(NLAT * NLON)
+    return (result, grad_gain, total_in * scale, total_out * scale, total_disco * scale)
+
+
+def shards(*arrays):
+    channels, rows, columns = arrays[0].shape
+    lat_count = lax.axis_size("lat")
+    lon_count = lax.axis_size("lon")
+    fits = (
+        rows == 2 * BAND
+        and lon_count == 2
+        and channels == lon_count * LANES
+        and columns % (2 * LANES) == 0
+        and M == LANES
+        and M // lat_count == 8
+        and L // lat_count == 8
+    )
+    return shards_banded(*arrays) if fits else shards_general(*arrays)
+
+
 def solution(mesh):
     placed = (
         P(None, "lat", "lon"),

time: 1300 us -> 586 us (0.45); the launches traced: 1280 us -> 584 us
  other arithmetic: 417 us -> 17.1 us
  local copies, waits for them, and re-layouts: 388 us -> 11.7 us
  Pallas kernels: 0 us -> 233 us
  matrix products: 128 us -> 0 us
  waiting for transfers between devices: 300 us -> 225 us
  blocking collectives: 0 us -> 31.5 us
  starting transfers between devices: 23.5 us -> 51.4 us
    convert_element_type x4 -> x2, other arithmetic: 264 us -> 4.95 us  [shards_banded(): (kept.astype(jnp.float32) + arrived.astype(jnp.float32)).astype(jnp.bfloa...]
    pallas_call x0 -> x8, Pallas kernels: none -> 233 us  [the longest x1 98.6 us: stencil_call(): pl.pallas_call(functools.partial(stencil_kernel, rows=rows), grid=(rows /...]
    reduce_scatter x1 -> x0, waiting for transfers between devices: 176 us -> none  [shards(): lax.psum_scatter(jnp.einsum('ljm,cjrm->lcrm', weights, coeffs, preferred_...]
    dot_general x11 -> x0, matrix products: 128 us -> none  [the longest x1 18.3 us: shards(): grad_act = jnp.dot(w_out, flat_cot, preferred_element_type=jnp.float32)]
    mul x132 -> x0, local copies, waits for them, and re-layouts: 93.2 us -> none  [the longest x128 91.6 us: advance(): coef_up[None, :] * (cosine * previous - coef_low[None, :] * before)]
    eq x128 -> x0, other arithmetic: 83.1 us -> none  [advance(): orders == degree]
    dynamic_slice x128 -> x3, local copies, waits for them, and re-layouts: 75 us -> 2.89 us  [the longest x2 1.56 us: shards_banded(): lax.dynamic_slice_in_dim(kernel_pad, lat_index * rows, rows + 2 * REACH, 0)]
    unnamed x81 -> x27, local copies, waits for them, and re-layouts: 72.1 us -> 1.88 us
  transfers between devices with their start and end apart: 9 -> 15, of which waited for: 4 -> 6; matrix products, arithmetic and copies ran while one was open for 41% -> 5% of each run, Pallas kernels for 0% -> 36%
where the time goes in v1:
time: 586 us; the launch traced here: 584 us
  Pallas kernels  233 us (40%)
  waiting for transfers between devices  225 us (38%)
  starting transfers between devices  51.4 us (9%)
  blocking collectives  31.5 us (5%)
  other arithmetic  17.1 us (3%)
  between operations  14.2 us (2%)
  local copies, waits for them, and re-layouts  11.7 us (2%)
    psum x1, waiting for transfers between devices, shards_banded(): lax.psum((first[4] + second[4], first[5] + second[5], disco_part), ('lat'...  131 us
    pallas_call x1, Pallas kernels, stencil_call(): pl.pallas_call(functools.partial(stencil_kernel, rows=rows), grid=(rows /...  98.6 us
    pallas_call x2, Pallas kernels, mlp_call(): pl.pallas_call(functools.partial(mlp_kernel, steps=steps, width=width, ch...  91.4 us
    ppermute x2, waiting for transfers between devices, shards_banded(): arrived = lax.ppermute(sent, 'lon', swap)  48.3 us
    all_to_all x1, blocking collectives, shards_banded(): local = exchange(synth)  31.5 us
    pallas_call x2, Pallas kernels, final_call(): pl.pallas_call(final_kernel, grid=(columns // width,), in_specs=[pl.Block...  29.5 us
    all_to_all x2, waiting for transfers between devices, shards_banded(): received.append(exchange(summed.reshape(lat_count, 2, own, BAND, LANES)))  21.6 us
    all_to_all x1, waiting for transfers between devices, shards_banded(): local = exchange(synth)  12.5 us
  transfers between devices with their start and end apart: 15, of which 6 were waited for; matrix products, arithmetic and copies ran while one was open for 5% of the time, Pallas kernels for 36%

profile of v1, /device:TPU:0, one launch (start us, length us, event | category | flops | bytes accessed | tf_op | source)
XLA Modules:
  0.0 584.4 jit_solution(9506055885934994878)
XLA Ops:
  7.2 2.7 gain.1
  9.9 7.4 %all-to-all-start.2 = ((f32[16,8,2,8,128]{4,3,2,1,0:T(8,128)}), f32[16,8,2,8,128]{4,3,2,1,0:T(8,128)S(1)}, u32[]{:S(2)}, u32[]{:S(2)}) async-start(f32[16,8,2,8,128]{4,3,2,1,0:T(8,128)} %bitcast.13), calls=%async_computation.2 | async-start | bytes 2097152 | tf_op jit(solution)/shard_map/all_to_all | solution.py:791
  18.8 45.7 %mlp.3 = (bf16[16,256,512]{2,1,0:T(8,128)(2,1)}, bf16[256,16,128]{2,1,0:T(8,128)(2,1)}, bf16[256,16,128]{2,1,0:T(8,128)(2,1)}, bf16[16,16,256]{2,1,0:T(8,128)(2,...) custom-call(s32[1]{0:T(128)} %bitcast.side, bf16[256,32,512]{2,1,0:T(8,128)(2,1)} %x_ref.3, bf16[256,32,512]{2,1,0:T(8,128)(2,1)} %ct_ref.3, ...), custom_call_target="tpu_custom_call" | custom-call | flops 11811160064 | bytes 12582912 | tf_op jit(solution)/shard_map/mlp/pallas_call | solution.py:419
  66.0 24.2 %collective-permute-done.6 = bf16[256,16,128]{2,1,0:T(8,128)(2,1)S(1)} collective-permute-done((bf16[256,16,128]{2,1,0:T(8,128)(2,1)}, bf16[256,16,128]{2,1,0:T(8,128)(2,1)S(1)}, u32[]{:S(2)}, u32[]{:S(2)}) %collective-permute-start.6) | collective-permute-done | bytes 1048608 | tf_op jit(solution)/shard_map/ppermute | solution.py:800
  90.2 2.5 add_convert_fusion
  92.7 5.7 all-to-all-start.1
  98.4 45.7 %mlp.2 = (bf16[16,256,512]{2,1,0:T(8,128)(2,1)}, bf16[256,16,128]{2,1,0:T(8,128)(2,1)}, bf16[256,16,128]{2,1,0:T(8,128)(2,1)}, bf16[16,16,256]{2,1,0:T(8,128)(2,...) custom-call(s32[1]{0:T(128)} %bitcast.side, bf16[256,32,512]{2,1,0:T(8,128)(2,1)} %x_ref.3, bf16[256,32,512]{2,1,0:T(8,128)(2,1)} %ct_ref.3, ...), custom_call_target="tpu_custom_call" | custom-call | flops 11811160064 | bytes 12582912 | tf_op jit(solution)/shard_map/mlp/pallas_call | solution.py:419
  145.7 24.1 %collective-permute-done.5 = bf16[256,16,128]{2,1,0:T(8,128)(2,1)S(1)} collective-permute-done((bf16[256,16,128]{2,1,0:T(8,128)(2,1)}, bf16[256,16,128]{2,1,0:T(8,128)(2,1)S(1)}, u32[]{:S(2)}, u32[]{:S(2)}) %collective-permute-start.5) | collective-permute-done | bytes 1048608 | tf_op jit(solution)/shard_map/ppermute | solution.py:800
  169.9 2.5 add_convert_fusion.1
  173.3 5.8 all-to-all-start
  180.4 21.6 %all-to-all-done.r0 = bf16[16,2,8,16,128]{4,3,2,1,0:T(8,128)(2,1)S(1)} async-done(((bf16[16,2,8,16,128]{4,3,2,1,0:T(8,128)(2,1)}), bf16[16,2,8,16,128]{4,3,2,1,0:T(8,128)(2,1)S(1)}, u32[]{:S(2)}, u32[]{:S(2)}) %all-to-all-start) | async-done | bytes 1048608 | tf_op jit(solution)/shard_map/all_to_all | solution.py:802
  202.0 8.2 %legendre.1 = (f32[16,8,2,8,128]{4,3,2,1,0:T(8,128)}, bf16[16,16,16,128]{3,2,1,0:T(8,128)(2,1)}, bf16[16,16,16,128]{3,2,1,0:T(8,128)(2,1)S(1)}) custom-call(bf16[8,128,512]{2,1,0:T(8,128)(2,1)S(1)} %constant_dynamic-slice_fusion.leg, bf16[16,2,8,16,128]{4,3,2,1,0:T(8,128)(2,1)S(1)} %all-to-all-done.r0, bf16[16,2,8,16,128]{4,3,2,1,0:T(8,128)(2,1)} %copy-done.2, ...), custom_call_target="tpu_custom_call" | custom-call | flops 1073741824 | bytes 7340032 | tf_op jit(solution)/shard_map/legendre/pallas_call | solution.py:602
  210.2 31.5 %all_to_all.30.own = bf16[16,16,16,128]{3,2,1,0:T(8,128)(2,1)S(1)} all-to-all(bf16[16,16,16,128]{3,2,1,0:T(8,128)(2,1)S(1)} %get-tuple-element.31), channel_id=1, replica_groups=mesh['lat'=16,'lon'=2] {'lat'}, dimensions={0} | all-to-all | bytes 2097152 | tf_op jit(solution)/shard_map/all_to_all | solution.py:836
  241.7 5.1 all-to-all-start.4
  246.9 1.9 slice.12
  251.4 1.9 slice.13
  253.4 3.8 collective-permute-start.1
  257.8 12.5 %all-to-all-done.4.own = bf16[16,16,16,128]{3,2,1,0:T(8,128)(2,1)S(1)} async-done(((bf16[16,16,16,128]{3,2,1,0:T(8,128)(2,1)}), bf16[16,16,16,128]{3,2,1,0:T(8,128)(2,1)S(1)}, u32[]{:S(2)}, u32[]{:S(2)}) %all-to-all-start.4) | async-done | bytes 1048608 | tf_op jit(solution)/shard_map/all_to_all | solution.py:836
  270.3 12.1 %all-to-all-start.5 = ((f32[16,8,2,8,128]{4,3,2,1,0:T(8,128)}), f32[16,8,2,8,128]{4,3,2,1,0:T(8,128)}, u32[]{:S(2)}, u32[]{:S(2)}) async-start(f32[16,8,2,8,128]{4,3,2,1,0:T(8,128)} %get-tuple-element.33), calls=%async_computation.5 | async-start | bytes 2097152 | tf_op jit(solution)/shard_map/all_to_all | solution.py:839
  283.4 4.1 collective-permute-start.4
  289.9 1.9 add.48
  291.8 1.9 add.47
  293.7 11.6 %collective-permute-done.3 = bf16[2,16,256]{2,1,0:T(8,128)(2,1)} collective-permute-done((bf16[2,16,256]{2,1,0:T(8,128)(2,1)}, bf16[2,16,256]{2,1,0:T(8,128)(2,1)}, u32[]{:S(2)}, u32[]{:S(2)}) %collective-permute-start.3) | collective-permute-done | bytes 16416 | tf_op jit(solution)/shard_map/ppermute | solution.py:811
  306.8 98.6 %stencil.1 = (bf16[32,256,512]{2,1,0:T(8,128)(2,1)}, f32[256,256]{1,0:T(8,128)}) custom-call(f32[900]{0:T(1024)} %reshape.54.taps, bf16[16,256,512]{2,1,0:T(8,128)(2,1)} %get-tuple-element.22.first, bf16[16,256,512]{2,1,0:T(8,128)(2,1)} %get-tuple-element.23.second, bf16[2,256,512]{2,1,0:T(8,128)(2,1)} %collective-permute-done.top, ...), custom_call_target="tpu_custom_call" | custom-call | flops 2399141888 | bytes 25165824 | tf_op jit(solution)/shard_map/stencil/pallas_call | solution.py:532
  405.4 1.6 collective-permute-start.8
  408.5 131.2 %all-reduce.4.cloned.1.call-done = (f32[256,512]{1,0:T(8,128)}, f32[512,256]{1,0:T(8,128)}, f32[256,256]{1,0:T(8,128)}) async-done(((f32[256,512]{1,0:T(8,128)}, f32[512,256]{1,0:T(8,128)}, f32[256,256]{1,0:T(8,128)}), (f32[256,512]{1,0:T(8,128)}, f32[512,256]{1,0:T(8,128)}, f32[256,256]{1,0:T(8,128)})) %all-reduce.4.cloned.1.call-update) | async-done | bytes 1310736 | tf_op jit(solution)/shard_map/psum | solution.py:829
  539.7 1.7 broadcast_multiply_fusion.2
  541.3 1.9 broadcast_multiply_fusion.1
  543.2 1.9 broadcast_multiply_fusion
  545.1 2.9 grad_gain.1
  548.1 14.9 %final.2.rest_0_ = bf16[256,32,512]{2,1,0:T(8,128)(2,1)} custom-call(s32[1]{0:T(128)} %bitcast.side, bf16[32,256,512]{2,1,0:T(8,128)(2,1)} %get-tuple-element.26.q_ref, bf16[16,16,16,128]{3,2,1,0:T(8,128)(2,1)S(1)} %all-to-all-done.4.own, bf16[16,16,16,128]{3,2,1,0:T(8,128)(2,1)} %collective-permute-done.8.other, ...), custom_call_target="tpu_custom_call" | custom-call | flops 2147483648 | bytes 10485760 | tf_op jit(solution)/shard_map/final/pallas_call | solution.py:658
  563.0 14.6 %final.3 = bf16[256,32,512]{2,1,0:T(8,128)(2,1)} custom-call(s32[1]{0:T(128)} %bitcast.side, bf16[32,256,512]{2,1,0:T(8,128)(2,1)} %get-tuple-element.26.q_ref, bf16[16,16,16,128]{3,2,1,0:T(8,128)(2,1)S(1)} %all_to_all.30.own, bf16[16,16,16,128]{3,2,1,0:T(8,128)(2,1)S(1)} %collective-permute-done.7.other, ...), custom_call_target="tpu_custom_call", output_to_operand_aliasing={{}: (6, {})} | custom-call | flops 2147483648 | bytes 10485760 | tf_op jit(solution)/shard_map/final/pallas_call | solution.py:658
  (58 shorter events, 16.7 us)
Async XLA Ops:
  7.2 10.1 %copy-start.5 = (bf16[256,512]{1,0:T(8,128)(2,1)S(1)}, bf16[256,512]{1,0:T(8,128)(2,1)}, u32[]{:S(2)}) copy-start(bf16[256,512]{1,0:T(8,128)(2,1)} %win.3) | copy-start | bytes 786436
  7.2 10.9 %copy-start.6 = (bf16[2,272,512]{2,1,0:T(8,128)(2,1)S(1)}, bf16[2,272,512]{2,1,0:T(8,128)(2,1)}, u32[]{:S(2)}) copy-start(bf16[2,272,512]{2,1,0:T(8,128)(2,1)} %constant.45.clone) | copy-start | bytes 1671172
  9.9 82.8 %all-to-all-start.2 = ((f32[16,8,2,8,128]{4,3,2,1,0:T(8,128)}), f32[16,8,2,8,128]{4,3,2,1,0:T(8,128)S(1)}, u32[]{:S(2)}, u32[]{:S(2)}) async-start(f32[16,8,2,8,128]{4,3,2,1,0:T(8,128)} %bitcast.13), calls=%async_computation.2 | async-start | bytes 2097152 | tf_op jit(solution)/shard_map/all_to_all | solution.py:791
  64.5 25.7 %collective-permute-start.6 = (bf16[256,16,128]{2,1,0:T(8,128)(2,1)}, bf16[256,16,128]{2,1,0:T(8,128)(2,1)S(1)}, u32[]{:S(2)}, u32[]{:S(2)}) collective-permute-start(bf16[256,16,128]{2,1,0:T(8,128)(2,1)} %get-tuple-element.30), channel_id=1, source_target_pairs={{0,1},{1,0},{2,3},{3,2},{4,5},{5,4},{6,7},{7,6},{8,9},{9,8},{10,11... | collective-permute-start | bytes 3145736 | tf_op jit(solution)/shard_map/ppermute | solution.py:800
  92.7 51.4 %copy-start.1 = (f32[16,8,2,8,128]{4,3,2,1,0:T(8,128)}, f32[16,8,2,8,128]{4,3,2,1,0:T(8,128)S(1)}, u32[]{:S(2)}) copy-start(f32[16,8,2,8,128]{4,3,2,1,0:T(8,128)S(1)} %all-to-all-done.2.gain) | copy-start | bytes 3145732
  92.7 79.6 %all-to-all-start.1 = ((bf16[16,2,8,16,128]{4,3,2,1,0:T(8,128)(2,1)}), bf16[16,2,8,16,128]{4,3,2,1,0:T(8,128)(2,1)S(1)}, u32[]{:S(2)}, u32[]{:S(2)}) async-start(bf16[16,2,8,16,128]{4,3,2,1,0:T(8,128)(2,1)} %bitcast.4), calls=%async_computation.1 | async-start | bytes 2097152 | tf_op jit(solution)/shard_map/all_to_all | solution.py:802
  144.1 25.7 %collective-permute-start.5 = (bf16[256,16,128]{2,1,0:T(8,128)(2,1)}, bf16[256,16,128]{2,1,0:T(8,128)(2,1)S(1)}, u32[]{:S(2)}, u32[]{:S(2)}) collective-permute-start(bf16[256,16,128]{2,1,0:T(8,128)(2,1)} %get-tuple-element.28), channel_id=1, source_target_pairs={{0,1},{1,0},{2,3},{3,2},{4,5},{5,4},{6,7},{7,6},{8,9},{9,8},{10,11... | collective-permute-start | bytes 3145736 | tf_op jit(solution)/shard_map/ppermute | solution.py:800
  172.3 1.0 copy-start.2
  173.3 28.7 %all-to-all-start = ((bf16[16,2,8,16,128]{4,3,2,1,0:T(8,128)(2,1)}), bf16[16,2,8,16,128]{4,3,2,1,0:T(8,128)(2,1)S(1)}, u32[]{:S(2)}, u32[]{:S(2)}) async-start(bf16[16,2,8,16,128]{4,3,2,1,0:T(8,128)(2,1)} %bitcast.3), calls=%async_computation | async-start | bytes 2097152 | tf_op jit(solution)/shard_map/all_to_all | solution.py:802
  241.7 7.5 %copy-start.7 = (bf16[16,16,256]{2,1,0:T(8,128)(2,1)S(1)}, bf16[16,16,256]{2,1,0:T(8,128)(2,1)}, u32[]{:S(2)}) copy-start(bf16[16,16,256]{2,1,0:T(8,128)(2,1)} %get-tuple-element.25) | copy-start | bytes 393220
  241.7 7.5 %copy-start.8 = (bf16[16,16,256]{2,1,0:T(8,128)(2,1)S(1)}, bf16[16,16,256]{2,1,0:T(8,128)(2,1)}, u32[]{:S(2)}) copy-start(bf16[16,16,256]{2,1,0:T(8,128)(2,1)} %get-tuple-element.24) | copy-start | bytes 393220
  241.7 15.4 %copy-start.10 = (s32[512,12]{0,1:T(8,128)S(1)}, s32[512,12]{0,1:T(8,128)}, u32[]{:S(2)}) copy-start(s32[512,12]{0,1:T(8,128)} %param.27) | copy-start | bytes 73732
  241.7 15.4 %copy-start.12 = (f32[64]{0:T(128)S(1)}, f32[64]{0:T(128)}, u32[]{:S(2)}) copy-start(f32[64]{0:T(128)} %param.24) | copy-start | bytes 772
  241.7 15.7 %copy-start.9 = (s32[512,12]{0,1:T(8,128)S(1)}, s32[512,12]{0,1:T(8,128)}, u32[]{:S(2)}) copy-start(s32[512,12]{0,1:T(8,128)} %param.25) | copy-start | bytes 73732
  241.7 15.8 %copy-start.11 = (s32[512,12]{0,1:T(8,128)S(1)}, s32[512,12]{0,1:T(8,128)}, u32[]{:S(2)}) copy-start(s32[512,12]{0,1:T(8,128)} %param.26) | copy-start | bytes 73732
  241.7 28.6 %all-to-all-start.4 = ((bf16[16,16,16,128]{3,2,1,0:T(8,128)(2,1)}), bf16[16,16,16,128]{3,2,1,0:T(8,128)(2,1)S(1)}, u32[]{:S(2)}, u32[]{:S(2)}) async-start(bf16[16,16,16,128]{3,2,1,0:T(8,128)(2,1)} %get-tuple-element.32), calls=%async_computation.4 | async-start | bytes 2097152 | tf_op jit(solution)/shard_map/all_to_all | solution.py:836
  248.8 58.0 %collective-permute-start = (bf16[2,256,512]{2,1,0:T(8,128)(2,1)}, bf16[2,256,512]{2,1,0:T(8,128)(2,1)}, u32[]{:S(2)}, u32[]{:S(2)}) collective-permute-start(bf16[2,256,512]{2,1,0:T(8,128)(2,1)} %slice.12), channel_id=1, source_target_pairs={{0,2},{2,4},{4,6},{6,8},{8,10},{10,12},{12,14},{14,16},{16,18},{18... | collective-permute-start | bytes 1572872 | tf_op jit(solution)/shard_map/ppermute | solution.py:811
  249.9 32.6 %collective-permute-start.2 = (bf16[32,16,256]{2,1,0:T(8,128)(2,1)}, bf16[32,16,256]{2,1,0:T(8,128)(2,1)S(1)}, u32[]{:S(2)}, u32[]{:S(2)}) collective-permute-start(bf16[32,16,256]{2,1,0:T(8,128)(2,1)} %pad_maximum_fusion.1), channel_id=1, source_target_pairs={{0,1},{1,0},{2,3},{3,2},{4,5},{5,4},{6,7},{7,6},{8,9},{9,8},{10,11... | collective-permute-start | bytes 786440 | tf_op jit(solution)/shard_map/ppermute | solution.py:810
  251.4 38.5 %copy-start.4 = (f32[512,256]{1,0:T(8,128)S(1)}, f32[512,256]{1,0:T(8,128)}, u32[]{:S(2)}) copy-start(f32[512,256]{1,0:T(8,128)} %get-tuple-element.37) | copy-start | bytes 1572868
  253.4 53.4 %collective-permute-start.1 = (bf16[2,256,512]{2,1,0:T(8,128)(2,1)}, bf16[2,256,512]{2,1,0:T(8,128)(2,1)}, u32[]{:S(2)}, u32[]{:S(2)}) collective-permute-start(bf16[2,256,512]{2,1,0:T(8,128)(2,1)} %slice.13), channel_id=1, source_target_pairs={{2,0},{4,2},{6,4},{8,6},{10,8},{12,10},{14,12},{16,14},{18,16},{20... | collective-permute-start | bytes 1572872 | tf_op jit(solution)/shard_map/ppermute | solution.py:814
  257.8 34.0 %copy-start.3 = (f32[256,512]{1,0:T(8,128)S(1)}, f32[256,512]{1,0:T(8,128)}, u32[]{:S(2)}) copy-start(f32[256,512]{1,0:T(8,128)} %get-tuple-element.35) | copy-start | bytes 1572868
  270.3 274.8 %all-to-all-start.5 = ((f32[16,8,2,8,128]{4,3,2,1,0:T(8,128)}), f32[16,8,2,8,128]{4,3,2,1,0:T(8,128)}, u32[]{:S(2)}, u32[]{:S(2)}) async-start(f32[16,8,2,8,128]{4,3,2,1,0:T(8,128)} %get-tuple-element.33), calls=%async_computation.5 | async-start | bytes 2097152 | tf_op jit(solution)/shard_map/all_to_all | solution.py:839
  282.4 257.3 %all-reduce.4.cloned.1.call-start = ((), (), s32[]{:S(2)}) async-start(), calls=%async_computation.6 | async-start | bytes 2621440 | tf_op jit(solution)/shard_map/psum | solution.py:829
  283.1 22.2 %collective-permute-start.3 = (bf16[2,16,256]{2,1,0:T(8,128)(2,1)}, bf16[2,16,256]{2,1,0:T(8,128)(2,1)}, u32[]{:S(2)}, u32[]{:S(2)}) collective-permute-start(bf16[2,16,256]{2,1,0:T(8,128)(2,1)} %get-tuple-element.42), channel_id=1, source_target_pairs={{0,2},{2,4},{4,6},{6,8},{8,10},{10,12},{12,14},{14,16},{16,18},{18... | collective-permute-start | bytes 49160 | tf_op jit(solution)/shard_map/ppermute | solution.py:811
  283.4 21.9 %collective-permute-start.4 = (bf16[2,16,256]{2,1,0:T(8,128)(2,1)}, bf16[2,16,256]{2,1,0:T(8,128)(2,1)}, u32[]{:S(2)}, u32[]{:S(2)}) collective-permute-start(bf16[2,16,256]{2,1,0:T(8,128)(2,1)} %get-tuple-element.43), channel_id=1, source_target_pairs={{2,0},{4,2},{6,4},{8,6},{10,8},{12,10},{14,12},{16,14},{18,16},{20... | collective-permute-start | bytes 49160 | tf_op jit(solution)/shard_map/ppermute | solution.py:814
  405.4 142.6 %collective-permute-start.8 = (bf16[16,16,16,128]{3,2,1,0:T(8,128)(2,1)S(1)}, bf16[16,16,16,128]{3,2,1,0:T(8,128)(2,1)}, u32[]{:S(2)}, u32[]{:S(2)}) collective-permute-start(bf16[16,16,16,128]{3,2,1,0:T(8,128)(2,1)S(1)} %all-to-all-done.4.own), channel_id=1, source_target_pairs={{0,1},{1,0},{2,3},{3,2},{4,5},{5,4},{6,7},{7,6},{8,9},{9,8},{10,11... | collective-permute-start | bytes 3145736 | tf_op jit(solution)/shard_map/ppermute | solution.py:837
  407.0 155.9 %collective-permute-start.7 = (bf16[16,16,16,128]{3,2,1,0:T(8,128)(2,1)S(1)}, bf16[16,16,16,128]{3,2,1,0:T(8,128)(2,1)S(1)}, u32[]{:S(2)}, u32[]{:S(2)}) collective-permute-start(bf16[16,16,16,128]{3,2,1,0:T(8,128)(2,1)S(1)} %all_to_all.30.own), channel_id=1, source_target_pairs={{0,1},{1,0},{2,3},{3,2},{4,5},{5,4},{6,7},{7,6},{8,9},{9,8},{10,11... | collective-permute-start | bytes 3145736 | tf_op jit(solution)/shard_map/ppermute | solution.py:837
  543.2 4.9 copy-start
Sparse Core Ops, SparseCore 0:
  405.6 134.0 all-reduce.3

commit v2 on v1

--- a/solution.py
+++ b/solution.py
@@ -291,6 +291,7 @@
 
 BAND = 16
 LANES = 128
+PARTS = 2
 MIB = 1024 * 1024
 
 
@@ -461,41 +462,28 @@
     )(side, filtered, cotangent, win_t, win, wout, table)
 
 
-def stencil_kernel(
-    taps, first, second, top, bottom, edges, place, bi_ref,
-    q_ref, gd_ref,
-    field, rim, stage, flat,
-    *, rows,
-):
-    band = pl.program_id(0)
+def stencil_kernel(taps, first, second, top, bottom, edges, place, *rest, rows):
+    q_ref, field, rim = rest[-3:]
     channels, columns = field.shape[1:]
-
-    @pl.when(band == 0)
-    def _():
-        gd_ref[...] = jnp.zeros_like(gd_ref)
-        field[0:REACH] = top[...]
-        field[REACH : REACH + BAND] = first[...]
-        field[REACH + BAND : REACH + 2 * BAND] = second[...]
-        field[rows + REACH :] = bottom[...]
-
-        def spread(row, carry):
-            rim[row] = mm_tn(edges[row], place[...]).astype(jnp.bfloat16)
-            return carry
-
-        lax.fori_loop(0, rows + 2 * REACH, spread, 0)
-
-    rows_first(bi_ref, stage, flat, columns)
+    field[0:REACH] = top[...]
+    field[REACH : REACH + BAND] = first[...]
+    field[REACH + BAND : REACH + 2 * BAND] = second[...]
+    field[rows + REACH :] = bottom[...]
+
+    def spread(row, carry):
+        rim[row] = mm_tn(edges[row], place[...])[: rim.shape[1]].astype(jnp.bfloat16)
+        return carry
+
+    lax.fori_loop(0, rows + 2 * REACH, spread, 0)
     lane = lax.broadcasted_iota(jnp.int32, (16, LANES), 1)
     span = 2 * REACH + 1
 
     def row_body(row, carry):
-        top_row = band * BAND + row
-
         def tile_body(tile, inner):
             part = pl.ds(pl.multiple_of(tile * 16, 16), 16)
             sums = [None] * span
             for north in range(span):
-                source = top_row + 2 * REACH - north
+                source = row + 2 * REACH - north
                 here = field[source, part, :].astype(jnp.float32)
                 ends = rim[source, part, :].astype(jnp.float32)
                 for east in range(span):
@@ -517,46 +505,90 @@
             q_ref[row, part, :] = total.astype(jnp.bfloat16)
             return inner
 
-        lax.fori_loop(0, channels // 16, tile_body, 0)
+        return lax.fori_loop(0, channels // 16, tile_body, carry)
+
+    lax.fori_loop(0, rows, row_body, 0)
+
+
+def stencil_call(part, parts, taps, first, second, top, bottom, edges, place, previous):
+    rows = edges.shape[0] - 2 * REACH
+    _, channels, columns = first.shape
+    some = channels // parts
+    extra = [] if previous is None else [previous]
+
+    def piece(count):
+        return pl.BlockSpec((count, some, columns), lambda i: (0, part, 0))
+
+    return pl.pallas_call(
+        functools.partial(stencil_kernel, rows=rows),
+        grid=(1,),
+        in_specs=[
+            pl.BlockSpec(memory_space=pltpu.SMEM),
+            piece(BAND),
+            piece(BAND),
+            piece(REACH),
+            piece(REACH),
+            pl.BlockSpec(edges.shape[:2] + (LANES,), lambda i: (0, 0, part * some // LANES)),
+            pl.BlockSpec(memory_space=pltpu.VMEM),
+        ]
+        + [pl.BlockSpec(memory_space=pl.ANY)] * len(extra),
+        out_specs=piece(rows),
+        out_shape=jax.ShapeDtypeStruct((rows, channels, columns), jnp.bfloat16),
+        scratch_shapes=[
+            pltpu.VMEM((rows + 2 * REACH, some, columns), jnp.bfloat16),
+            pltpu.VMEM((rows + 2 * REACH, some, LANES), jnp.bfloat16),
+        ],
+        input_output_aliases={7: 0} if extra else {},
+        compiler_params=params(48),
+        cost_estimate=pl.CostEstimate(
+            flops=60 * some * rows * columns,
+            bytes_accessed=4 * some * rows * columns,
+            transcendentals=0,
+        ),
+        name="stencil",
+    )(taps, first, second, top, bottom, edges, place, *extra)
+
+
+def disco_kernel_grad(bi_ref, q_ref, gd_ref, stage, flat):
+    columns = q_ref.shape[2]
+
+    @pl.when(pl.program_id(0) == 0)
+    def _():
+        gd_ref[...] = jnp.zeros_like(gd_ref)
+
+    rows_first(bi_ref, stage, flat, columns)
+
+    def body(row, carry):
         cells = pl.ds(pl.multiple_of(row * columns, columns), columns)
         gd_ref[...] += mm_nt(flat[:, cells], q_ref[row])
         return carry
 
-    lax.fori_loop(0, BAND, row_body, 0)
-
-
-def stencil_call(taps, first, second, top, bottom, edges, place, block_input):
+    lax.fori_loop(0, BAND, body, 0)
+
+
+def disco_grad_call(block_input, q):
     channels, rows, columns = block_input.shape
-    cells = rows * columns
-    vmem = pl.BlockSpec(memory_space=pltpu.VMEM)
     return pl.pallas_call(
-        functools.partial(stencil_kernel, rows=rows),
+        disco_kernel_grad,
         grid=(rows // BAND,),
-        in_specs=[pl.BlockSpec(memory_space=pltpu.SMEM)]
-        + [vmem] * 6
-        + [pl.BlockSpec((channels, BAND, columns), lambda i: (0, i, 0))],
-        out_specs=[
+        in_specs=[
+            pl.BlockSpec((channels, BAND, columns), lambda i: (0, i, 0)),
             pl.BlockSpec((BAND, channels, columns), lambda i: (i, 0, 0)),
-            whole_block((channels, channels)),
-        ],
-        out_shape=[
-            jax.ShapeDtypeStruct((rows, channels, columns), jnp.bfloat16),
-            jax.ShapeDtypeStruct((channels, channels), jnp.float32),
-        ],
+        ],
+        out_specs=whole_block((channels, channels)),
+        out_shape=jax.ShapeDtypeStruct((channels, channels), jnp.float32),
         scratch_shapes=[
-            pltpu.VMEM((rows + 2 * REACH, channels, columns), jnp.bfloat16),
-            pltpu.VMEM((rows + 2 * REACH, channels, LANES), jnp.bfloat16),
             pltpu.VMEM((columns // LANES, channels * BAND, LANES), jnp.float32),
             pltpu.VMEM((channels, BAND * columns), jnp.bfloat16),
         ],
-        compiler_params=params(60),
+        compiler_params=params(48),
         cost_estimate=pl.CostEstimate(
-            flops=60 * channels * cells + 2 * channels * channels * cells,
-            bytes_accessed=6 * channels * cells,
+            flops=2 * channels * channels * rows * columns,
+            bytes_accessed=4 * channels * rows * columns,
             transcendentals=0,
         ),
-        name="stencil",
-    )(taps, first, second, top, bottom, edges, place, block_input)
+        name="disco_weight",
+    )(block_input, q)
 
 
 def legendre_kernel(leg, r0, r1, gain, owned_ref, s0, s1, stage, *, steps, block):
@@ -791,20 +823,23 @@
     gain = exchange(
         gain_call(spectral_gain).reshape(lat_count, own, 2, degrees, LANES)
     )
-    w_in_t = w_in.T
-    bands = []
-    received = []
-    for band in range(rows // BAND):
-        bands.append(mlp_call(band, side, filtered, cotangent, w_in_t, w_in, w_out, forward))
-        _, kept, sent, _, _, _ = bands[-1]
-        arrived = lax.ppermute(sent, "lon", swap)
-        summed = (kept.astype(jnp.float32) + arrived.astype(jnp.float32)).astype(jnp.bfloat16)
-        received.append(exchange(summed.reshape(lat_count, 2, own, BAND, LANES)))
-    first, second = bands[0], bands[1]
-
     kernel = disco_kernel(quad_weights, lat_offsets, lon_offsets, weight_index)
     kernel_pad = jnp.pad(kernel, ((REACH, REACH), (0, 0), (0, 0)))
     kernel_rim = lax.dynamic_slice_in_dim(kernel_pad, lat_index * rows, rows + 2 * REACH, 0)
+    taps = kernel_rim.reshape(-1)
+    place = np.zeros((16, LANES), np.float32)
+    for row, lane in enumerate((0, 1, LANES - 2, LANES - 1)):
+        place[row, lane] = 1.0
+    place = jnp.asarray(place, jnp.bfloat16)
+    w_in_t = w_in.T
+
+    def summed(kept, arrived):
+        total = (kept.astype(jnp.float32) + arrived.astype(jnp.float32)).astype(jnp.bfloat16)
+        return total.reshape(lat_count, 2, own, BAND, LANES)
+
+    first = mlp_call(0, side, filtered, cotangent, w_in_t, w_in, w_out, forward)
+    arrived0 = lax.ppermute(first[2], "lon", swap)
+    second = mlp_call(1, side, filtered, cotangent, w_in_t, w_in, w_out, forward)
     down = [(i, (i + 1) % lat_count) for i in range(lat_count)]
     up = [(target, source) for source, target in down]
     sides = lax.ppermute(jnp.concatenate([first[3], second[3]], axis=0), "lon", swap)
@@ -813,30 +848,31 @@
     )
     bottom, bottom_side = lax.ppermute((first[0][:REACH], sides[:REACH]), "lat", up)
     edges = jnp.concatenate([top_side, sides, bottom_side], axis=0)
-    place = np.zeros((16, LANES), np.float32)
-    for row, lane in enumerate((0, 1, LANES - 2, LANES - 1)):
-        place[row, lane] = 1.0
-    q, disco_part = stencil_call(
-        kernel_rim.reshape(-1),
-        first[0],
-        second[0],
-        top,
-        bottom,
-        edges,
-        jnp.asarray(place, jnp.bfloat16),
-        block_input,
-    )
-    total_in, total_out, total_disco = lax.psum(
-        (first[4] + second[4], first[5] + second[5], disco_part), ("lat", "lon")
-    )
-
-    owned, s0, s1 = legendre_call(legendre, received[0], received[1], gain)
-    result = None
-    for band, synth in enumerate((s0, s1)):
-        local = exchange(synth)
-        other = lax.ppermute(local, "lon", swap)
-        result = final_call(band, side, q, local, other, inverse, w_disco, result)
+    arrived1 = lax.ppermute(second[2], "lon", swap)
+    total_in, total_out = lax.psum((first[4] + second[4], first[5] + second[5]), ("lat", "lon"))
+    sum0, edges = lax.optimization_barrier((summed(first[1], arrived0), edges))
+    received0 = exchange(sum0)
+    stencil = functools.partial(
+        stencil_call, taps=taps, first=first[0], second=second[0], top=top, bottom=bottom,
+        edges=edges, place=place,
+    )
+    q = stencil(0, PARTS, previous=None)
+    arrived1, q = lax.optimization_barrier((arrived1, q))
+    received1 = exchange(summed(second[1], arrived1))
+    q = stencil(1, PARTS, previous=q)
+    received0, received1, q = lax.optimization_barrier((received0, received1, q))
+    owned, s0, s1 = legendre_call(legendre, received0, received1, gain)
+    local0 = exchange(s0)
+    local1 = exchange(s1)
+    q, owned = lax.optimization_barrier((q, owned))
+    disco_part = disco_grad_call(block_input, q)
+    disco_part, total_in, total_out = lax.optimization_barrier((disco_part, total_in, total_out))
+    total_disco = lax.psum(disco_part, ("lat", "lon"))
+    other0 = lax.ppermute(local0, "lon", swap)
+    other1 = lax.ppermute(local1, "lon", swap)
     owned = exchange(owned).reshape(M * 2 * degrees, LANES)
+    result = final_call(0, side, q, local0, other0, inverse, w_disco, None)
+    result = final_call(1, side, q, local1, other1, inverse, w_disco, result)
     grad_gain = grad_gain_call(owned, spectral_saved)
     scale = 1.0 / math.sqrt(NLAT * NLON)
     return (result, grad_gain, total_in * scale, total_out * scale, total_disco * scale)

time: 586 us -> 674 us (1.15)
  waiting for transfers between devices: 225 us -> 311 us
  Pallas kernels: 233 us -> 244 us
  starting transfers between devices: 51.4 us -> 42.4 us
    psum x1 -> x2, waiting for transfers between devices: 131 us -> 239 us  [the longest x1 127 us: shards_banded(): total_disco = lax.psum(disco_part, ('lat', 'lon'))]
    ppermute x4, waiting for transfers between devices: 48.3 us -> 0.01 us  [the longest x1 0.01 us: shards_banded(): arrived0 = lax.ppermute(first[2], 'lon', swap)]
    pallas_call x1 -> x3, Pallas kernels: 98.6 us -> 109 us  [the longest x2 87.2 us: stencil_call(): pl.pallas_call(functools.partial(stencil_kernel, rows=rows), grid=(1,), i...]
    all_to_all x3, waiting for transfers between devices: 34.1 us -> 43.2 us  [the longest x1 22.9 us: shards_banded(): local0 = exchange(s0)]
    ppermute x2, waiting for transfers between devices: 11.6 us -> 19.7 us  [shards_banded(): lax.ppermute((second[0][BAND - REACH:], sides[rows - REACH:]), 'lat', down)]
    ppermute x1, waiting for transfers between devices: 0.01 us -> 7.63 us  [shards_banded(): lax.ppermute(jnp.concatenate([first[3], second[3]], axis=0), 'lon', swap)]
  transfers between devices with their start and end apart: 15 -> 16, of which waited for: 6 -> 8; matrix products, arithmetic and copies ran while one was open for 5% -> 3% of each run, Pallas kernels for 36% -> 26%
where the time goes in v2:
time: 674 us; the launch traced here: 673 us
  waiting for transfers between devices  311 us (46%)
  Pallas kernels  244 us (36%)
  starting transfers between devices  42.4 us (6%)
  blocking collectives  30.7 us (5%)
  local copies, waits for them, and re-layouts  15.9 us (2%)
  other arithmetic  15 us (2%)
  between operations  14.3 us (2%)
    psum x1, waiting for transfers between devices, shards_banded(): total_disco = lax.psum(disco_part, ('lat', 'lon'))  127 us
    psum x1, waiting for transfers between devices, shards_banded(): lax.psum((first[4] + second[4], first[5] + second[5]), ('lat', 'lon'))  111 us
    pallas_call x2, Pallas kernels, mlp_call(): pl.pallas_call(functools.partial(mlp_kernel, steps=steps, width=width, ch...  91.3 us
    pallas_call x2, Pallas kernels, stencil_call(): pl.pallas_call(functools.partial(stencil_kernel, rows=rows), grid=(1,), i...  87.2 us
    all_to_all x1, blocking collectives, shards_banded(): local1 = exchange(s1)  30.7 us
    pallas_call x2, Pallas kernels, final_call(): pl.pallas_call(final_kernel, grid=(columns // width,), in_specs=[pl.Block...  29.5 us
    all_to_all x1, waiting for transfers between devices, shards_banded(): local0 = exchange(s0)  22.9 us
    pallas_call x1, Pallas kernels, disco_grad_call(): pl.pallas_call(disco_kernel_grad, grid=(rows // BAND,), in_specs=[pl.Bloc...  22.2 us
  transfers between devices with their start and end apart: 16, of which 8 were waited for; matrix products, arithmetic and copies ran while one was open for 3% of the time, Pallas kernels for 26%

profile of v2, /device:TPU:0, one launch (start us, length us, event | category | flops | bytes accessed | tf_op | source)
XLA Modules:
  0.0 673.0 jit_solution(1752702139079098753)
XLA Ops:
  10.6 45.7 %mlp.2 = (bf16[16,256,512]{2,1,0:T(8,128)(2,1)}, bf16[256,16,128]{2,1,0:T(8,128)(2,1)}, bf16[256,16,128]{2,1,0:T(8,128)(2,1)}, bf16[16,16,256]{2,1,0:T(8,128)(2,...) custom-call(s32[1]{0:T(128)} %bitcast.side, bf16[256,32,512]{2,1,0:T(8,128)(2,1)} %x_ref.3, bf16[256,32,512]{2,1,0:T(8,128)(2,1)} %ct_ref.3, ...), custom_call_target="tpu_custom_call" | custom-call | flops 11811160064 | bytes 12582912 | tf_op jit(solution)/shard_map/mlp/pallas_call | solution.py:420
  56.3 3.0 collective-permute-start
  59.4 45.6 %mlp.3 = (bf16[16,256,512]{2,1,0:T(8,128)(2,1)}, bf16[256,16,128]{2,1,0:T(8,128)(2,1)}, bf16[256,16,128]{2,1,0:T(8,128)(2,1)}, bf16[16,16,256]{2,1,0:T(8,128)(2,...) custom-call(s32[1]{0:T(128)} %bitcast.side, bf16[256,32,512]{2,1,0:T(8,128)(2,1)} %x_ref.3, bf16[256,32,512]{2,1,0:T(8,128)(2,1)} %ct_ref.3, ...), custom_call_target="tpu_custom_call" | custom-call | flops 11811160064 | bytes 12582912 | tf_op jit(solution)/shard_map/mlp/pallas_call | solution.py:420
  106.1 7.6 %collective-permute-done.1 = bf16[32,16,256]{2,1,0:T(8,128)(2,1)S(1)} collective-permute-done((bf16[32,16,256]{2,1,0:T(8,128)(2,1)S(1)}, bf16[32,16,256]{2,1,0:T(8,128)(2,1)S(1)}, u32[]{:S(2)}, u32[]{:S(2)}) %collective-permute-start.1) | collective-permute-done | bytes 262176 | tf_op jit(solution)/shard_map/ppermute | solution.py:845
  113.8 2.8 collective-permute-start.3
  118.0 4.4 collective-permute-done.2
  123.7 3.7 all-to-all-start
  130.0 1.9 slice.15
  131.9 4.4 collective-permute-start.6
  140.6 15.3 %collective-permute-done.5.top = bf16[2,256,512]{2,1,0:T(8,128)(2,1)S(1)} collective-permute-done((bf16[2,256,512]{2,1,0:T(8,128)(2,1)}, bf16[2,256,512]{2,1,0:T(8,128)(2,1)S(1)}, u32[]{:S(2)}, u32[]{:S(2)}) %collective-permute-start.5) | collective-permute-done | bytes 524320 | tf_op jit(solution)/shard_map/ppermute | solution.py:846
  155.9 2.2 copy-done
  158.1 43.6 %stencil.2.rest_0_ = bf16[32,256,512]{2,1,0:T(8,128)(2,1)} custom-call(f32[900]{0:T(1024)S(1)} %reshape.55.taps, bf16[16,256,512]{2,1,0:T(8,128)(2,1)S(1)} %copy-done, bf16[16,256,512]{2,1,0:T(8,128)(2,1)} %get-tuple-element.40.second, bf16[2,256,512]{2,1,0:T(8,128)(2,1)S(1)} %collective-permute-done.5.top, ...), custom_call_target="tpu_custom_call" | custom-call | flops 125829120 | bytes 8388608 | tf_op jit(solution)/shard_map/stencil/pallas_call | solution.py:522
  203.0 6.5 all-to-all-start.1
  209.5 2.6 gain.1
  212.2 20.3 %all-to-all-done.1.r1 = bf16[16,2,8,16,128]{4,3,2,1,0:T(8,128)(2,1)S(1)} async-done(((bf16[16,2,8,16,128]{4,3,2,1,0:T(8,128)(2,1)}), bf16[16,2,8,16,128]{4,3,2,1,0:T(8,128)(2,1)S(1)}, u32[]{:S(2)}, u32[]{:S(2)}) %all-to-all-start.1) | async-done | bytes 1048608 | tf_op jit(solution)/shard_map/all_to_all | solution.py:861
  232.5 6.9 %all-to-all-start.2 = ((f32[16,8,2,8,128]{4,3,2,1,0:T(8,128)}), f32[16,8,2,8,128]{4,3,2,1,0:T(8,128)}, u32[]{:S(2)}, u32[]{:S(2)}) async-start(f32[16,8,2,8,128]{4,3,2,1,0:T(8,128)} %bitcast.13), calls=%async_computation.2 | async-start | bytes 2097152 | tf_op jit(solution)/shard_map/all_to_all | solution.py:823
  240.7 2.2 copy-done.1
  242.9 43.6 %stencil.3.q_ref = bf16[32,256,512]{2,1,0:T(8,128)(2,1)} custom-call(f32[900]{0:T(1024)S(1)} %reshape.55.taps, bf16[16,256,512]{2,1,0:T(8,128)(2,1)S(1)} %copy-done.1, bf16[16,256,512]{2,1,0:T(8,128)(2,1)} %get-tuple-element.40.second, bf16[2,256,512]{2,1,0:T(8,128)(2,1)S(1)} %collective-permute-done.5.top, ...), custom_call_target="tpu_custom_call", output_to_operand_aliasing={{}: (7, {})} | custom-call | flops 125829120 | bytes 8388608 | tf_op jit(solution)/shard_map/stencil/pallas_call | solution.py:522
  286.5 8.3 %legendre.1 = (f32[16,8,2,8,128]{4,3,2,1,0:T(8,128)}, bf16[16,16,16,128]{3,2,1,0:T(8,128)(2,1)}, bf16[16,16,16,128]{3,2,1,0:T(8,128)(2,1)S(1)}) custom-call(bf16[8,128,512]{2,1,0:T(8,128)(2,1)S(1)} %constant_dynamic-slice_fusion.leg, bf16[16,2,8,16,128]{4,3,2,1,0:T(8,128)(2,1)S(1)} %all-to-all-done.r0, bf16[16,2,8,16,128]{4,3,2,1,0:T(8,128)(2,1)} %copy-done.4, ...), custom_call_target="tpu_custom_call" | custom-call | flops 1073741824 | bytes 7340032 | tf_op jit(solution)/shard_map/legendre/pallas_call | solution.py:634
  294.8 30.7 %all_to_all.30.own = bf16[16,16,16,128]{3,2,1,0:T(8,128)(2,1)S(1)} all-to-all(bf16[16,16,16,128]{3,2,1,0:T(8,128)(2,1)S(1)} %get-tuple-element.49), channel_id=1, replica_groups=mesh['lat'=16,'lon'=2] {'lat'}, dimensions={0} | all-to-all | bytes 2097152 | tf_op jit(solution)/shard_map/all_to_all | solution.py:866
  325.5 5.0 all-to-all-start.4
  330.5 22.9 %all-to-all-done.4.own = bf16[16,16,16,128]{3,2,1,0:T(8,128)(2,1)S(1)} async-done(((bf16[16,16,16,128]{3,2,1,0:T(8,128)(2,1)}), bf16[16,16,16,128]{3,2,1,0:T(8,128)(2,1)S(1)}, u32[]{:S(2)}, u32[]{:S(2)}) %all-to-all-start.4) | async-done | bytes 1048608 | tf_op jit(solution)/shard_map/all_to_all | solution.py:865
  353.4 6.9 %all-to-all-start.5 = ((f32[16,8,2,8,128]{4,3,2,1,0:T(8,128)}), f32[16,8,2,8,128]{4,3,2,1,0:T(8,128)}, u32[]{:S(2)}, u32[]{:S(2)}) async-start(f32[16,8,2,8,128]{4,3,2,1,0:T(8,128)} %get-tuple-element.51), calls=%async_computation.5 | async-start | bytes 2097152 | tf_op jit(solution)/shard_map/all_to_all | solution.py:873
  360.4 1.9 add.47
  362.3 1.9 add.48
  367.4 22.2 %disco_weight.1 = f32[256,256]{1,0:T(8,128)} custom-call(bf16[256,32,512]{2,1,0:T(8,128)(2,1)} %bi_ref.1, bf16[32,256,512]{2,1,0:T(8,128)(2,1)} %stencil.3.q_ref), custom_call_target="tpu_custom_call" | custom-call | flops 2147483648 | bytes 16777216 | tf_op jit(solution)/shard_map/disco_weight/pallas_call | solution.py:571
  389.7 111.4 %all-reduce.7.cloned.1.call-done = (f32[256,512]{1,0:T(8,128)}, f32[512,256]{1,0:T(8,128)}) async-done(((f32[256,512]{1,0:T(8,128)}, f32[512,256]{1,0:T(8,128)}), (f32[256,512]{1,0:T(8,128)}, f32[512,256]{1,0:T(8,128)})) %all-reduce.7.cloned.1.call-update) | async-done | bytes 1048592 | tf_op jit(solution)/shard_map/psum | solution.py:852
  501.1 1.9 broadcast_multiply_fusion.1
  504.8 127.2 %all-reduce.5.cloned.1.call-done = f32[256,256]{1,0:T(8,128)} async-done(((f32[256,256]{1,0:T(8,128)}), f32[256,256]{1,0:T(8,128)}) %all-reduce.5.cloned.1.call-update) | async-done | bytes 262160 | tf_op jit(solution)/shard_map/psum | solution.py:870
  633.8 2.9 grad_gain.1
  636.7 14.9 %final.2.rest_0_ = bf16[256,32,512]{2,1,0:T(8,128)(2,1)} custom-call(s32[1]{0:T(128)} %bitcast.side, bf16[32,256,512]{2,1,0:T(8,128)(2,1)} %stencil.3.q_ref, bf16[16,16,16,128]{3,2,1,0:T(8,128)(2,1)S(1)} %all-to-all-done.4.own, bf16[16,16,16,128]{3,2,1,0:T(8,128)(2,1)} %collective-permute-done.8.other, ...), custom_call_target="tpu_custom_call" | custom-call | flops 2147483648 | bytes 10485760 | tf_op jit(solution)/shard_map/final/pallas_call | solution.py:690
  651.6 14.6 %final.3 = bf16[256,32,512]{2,1,0:T(8,128)(2,1)} custom-call(s32[1]{0:T(128)} %bitcast.side, bf16[32,256,512]{2,1,0:T(8,128)(2,1)} %stencil.3.q_ref, bf16[16,16,16,128]{3,2,1,0:T(8,128)(2,1)S(1)} %all_to_all.30.own, bf16[16,16,16,128]{3,2,1,0:T(8,128)(2,1)S(1)} %collective-permute-done.7.other, ...), custom_call_target="tpu_custom_call", output_to_operand_aliasing={{}: (6, {})} | custom-call | flops 2147483648 | bytes 10485760 | tf_op jit(solution)/shard_map/final/pallas_call | solution.py:690
  (65 shorter events, 23.6 us)
Async XLA Ops:
  56.3 48.6 %copy-start.9 = (bf16[16,16,256]{2,1,0:T(8,128)(2,1)S(1)}, bf16[16,16,256]{2,1,0:T(8,128)(2,1)}, u32[]{:S(2)}) copy-start(bf16[16,16,256]{2,1,0:T(8,128)(2,1)} %get-tuple-element.34) | copy-start | bytes 393220
  56.3 66.1 %copy-start.6 = (bf16[256,16,128]{2,1,0:T(8,128)(2,1)S(1)}, bf16[256,16,128]{2,1,0:T(8,128)(2,1)}, u32[]{:S(2)}) copy-start(bf16[256,16,128]{2,1,0:T(8,128)(2,1)} %get-tuple-element.32) | copy-start | bytes 3145732
  56.3 66.1 %collective-permute-start = (bf16[256,16,128]{2,1,0:T(8,128)(2,1)}, bf16[256,16,128]{2,1,0:T(8,128)(2,1)S(1)}, u32[]{:S(2)}, u32[]{:S(2)}) collective-permute-start(bf16[256,16,128]{2,1,0:T(8,128)(2,1)} %get-tuple-element.33), channel_id=1, source_target_pairs={{0,1},{1,0},{2,3},{3,2},{4,5},{5,4},{6,7},{7,6},{8,9},{9,8},{10,11... | collective-permute-start | bytes 3145736 | tf_op jit(solution)/shard_map/ppermute | solution.py:841
  105.0 31.4 %copy-start.12 = (s32[512,12]{0,1:T(8,128)S(1)}, s32[512,12]{0,1:T(8,128)}, u32[]{:S(2)}) copy-start(s32[512,12]{0,1:T(8,128)} %param.26) | copy-start | bytes 73732
  105.9 31.2 %copy-start.11 = (s32[512,12]{0,1:T(8,128)S(1)}, s32[512,12]{0,1:T(8,128)}, u32[]{:S(2)}) copy-start(s32[512,12]{0,1:T(8,128)} %param.27) | copy-start | bytes 73732
  105.9 31.1 %copy-start.13 = (f32[64]{0:T(128)S(1)}, f32[64]{0:T(128)}, u32[]{:S(2)}) copy-start(f32[64]{0:T(128)} %param.24) | copy-start | bytes 772
  105.9 31.5 %copy-start.10 = (s32[512,12]{0,1:T(8,128)S(1)}, s32[512,12]{0,1:T(8,128)}, u32[]{:S(2)}) copy-start(s32[512,12]{0,1:T(8,128)} %param.25) | copy-start | bytes 73732
  106.0 7.8 %collective-permute-start.1 = (bf16[32,16,256]{2,1,0:T(8,128)(2,1)S(1)}, bf16[32,16,256]{2,1,0:T(8,128)(2,1)S(1)}, u32[]{:S(2)}, u32[]{:S(2)}) collective-permute-start(bf16[32,16,256]{2,1,0:T(8,128)(2,1)S(1)} %pad_maximum_fusion.1), channel_id=1, source_target_pairs={{0,1},{1,0},{2,3},{3,2},{4,5},{5,4},{6,7},{7,6},{8,9},{9,8},{10,11... | collective-permute-start | bytes 786440 | tf_op jit(solution)/shard_map/ppermute | solution.py:845
  113.8 4.2 collective-permute-start.3
  116.5 5.9 collective-permute-start.2
  122.5 33.4 %copy-start.3 = (bf16[16,128]{1,0:T(8,128)(2,1)S(1)}, bf16[16,128]{1,0:T(8,128)(2,1)}, u32[]{:S(2)}) copy-start(bf16[16,128]{1,0:T(8,128)(2,1)} %constant.48.clone.place) | copy-start | bytes 12292
  123.7 79.3 %all-to-all-start = ((bf16[16,2,8,16,128]{4,3,2,1,0:T(8,128)(2,1)}), bf16[16,2,8,16,128]{4,3,2,1,0:T(8,128)(2,1)S(1)}, u32[]{:S(2)}, u32[]{:S(2)}) async-start(bf16[16,2,8,16,128]{4,3,2,1,0:T(8,128)(2,1)} %bitcast.3), calls=%async_computation | async-start | bytes 2097152 | tf_op jit(solution)/shard_map/all_to_all | solution.py:854
  127.4 74.3 %collective-permute-start.4 = (bf16[256,16,128]{2,1,0:T(8,128)(2,1)}, bf16[256,16,128]{2,1,0:T(8,128)(2,1)S(1)}, u32[]{:S(2)}, u32[]{:S(2)}) collective-permute-start(bf16[256,16,128]{2,1,0:T(8,128)(2,1)} %get-tuple-element.38), channel_id=1, source_target_pairs={{0,1},{1,0},{2,3},{3,2},{4,5},{5,4},{6,7},{7,6},{8,9},{9,8},{10,11... | collective-permute-start | bytes 3145736 | tf_op jit(solution)/shard_map/ppermute | solution.py:851
  130.0 25.9 %collective-permute-start.5 = (bf16[2,256,512]{2,1,0:T(8,128)(2,1)}, bf16[2,256,512]{2,1,0:T(8,128)(2,1)S(1)}, u32[]{:S(2)}, u32[]{:S(2)}) collective-permute-start(bf16[2,256,512]{2,1,0:T(8,128)(2,1)} %slice.14), channel_id=1, source_target_pairs={{0,2},{2,4},{4,6},{6,8},{8,10},{10,12},{12,14},{14,16},{16,18},{18... | collective-permute-start | bytes 1572872 | tf_op jit(solution)/shard_map/ppermute | solution.py:846
  131.9 24.0 %collective-permute-start.6 = (bf16[2,256,512]{2,1,0:T(8,128)(2,1)}, bf16[2,256,512]{2,1,0:T(8,128)(2,1)S(1)}, u32[]{:S(2)}, u32[]{:S(2)}) collective-permute-start(bf16[2,256,512]{2,1,0:T(8,128)(2,1)} %slice.15), channel_id=1, source_target_pairs={{2,0},{4,2},{6,4},{8,6},{10,8},{12,10},{14,12},{16,14},{18,16},{20... | collective-permute-start | bytes 1572872 | tf_op jit(solution)/shard_map/ppermute | solution.py:849
  155.9 2.2 copy-start
  158.1 43.6 %copy-start.5 = (bf16[256,16,128]{2,1,0:T(8,128)(2,1)S(1)}, bf16[256,16,128]{2,1,0:T(8,128)(2,1)}, u32[]{:S(2)}) copy-start(bf16[256,16,128]{2,1,0:T(8,128)(2,1)} %get-tuple-element.37) | copy-start | bytes 3145732
  203.0 29.4 %all-to-all-start.1 = ((bf16[16,2,8,16,128]{4,3,2,1,0:T(8,128)(2,1)}), bf16[16,2,8,16,128]{4,3,2,1,0:T(8,128)(2,1)S(1)}, u32[]{:S(2)}, u32[]{:S(2)}) async-start(bf16[16,2,8,16,128]{4,3,2,1,0:T(8,128)(2,1)} %bitcast.4), calls=%async_computation.1 | async-start | bytes 2097152 | tf_op jit(solution)/shard_map/all_to_all | solution.py:861
  232.5 6.9 %copy-start.4 = (bf16[16,2,8,16,128]{4,3,2,1,0:T(8,128)(2,1)}, bf16[16,2,8,16,128]{4,3,2,1,0:T(8,128)(2,1)S(1)}, u32[]{:S(2)}) copy-start(bf16[16,2,8,16,128]{4,3,2,1,0:T(8,128)(2,1)S(1)} %all-to-all-done.1.r1) | copy-start | bytes 3145732
  232.5 54.0 %all-to-all-start.2 = ((f32[16,8,2,8,128]{4,3,2,1,0:T(8,128)}), f32[16,8,2,8,128]{4,3,2,1,0:T(8,128)}, u32[]{:S(2)}, u32[]{:S(2)}) async-start(f32[16,8,2,8,128]{4,3,2,1,0:T(8,128)} %bitcast.13), calls=%async_computation.2 | async-start | bytes 2097152 | tf_op jit(solution)/shard_map/all_to_all | solution.py:823
  240.7 2.2 copy-start.1
  294.7 65.7 %copy-start.8 = (f32[256,512]{1,0:T(8,128)S(1)}, f32[256,512]{1,0:T(8,128)}, u32[]{:S(2)}) copy-start(f32[256,512]{1,0:T(8,128)} %get-tuple-element.52) | copy-start | bytes 1572868
  294.7 67.6 %copy-start.7 = (f32[512,256]{1,0:T(8,128)S(1)}, f32[512,256]{1,0:T(8,128)}, u32[]{:S(2)}) copy-start(f32[512,256]{1,0:T(8,128)} %get-tuple-element.54) | copy-start | bytes 1572868
  325.5 27.9 %all-to-all-start.4 = ((bf16[16,16,16,128]{3,2,1,0:T(8,128)(2,1)}), bf16[16,16,16,128]{3,2,1,0:T(8,128)(2,1)S(1)}, u32[]{:S(2)}, u32[]{:S(2)}) async-start(bf16[16,16,16,128]{3,2,1,0:T(8,128)(2,1)} %get-tuple-element.50), calls=%async_computation.4 | async-start | bytes 2097152 | tf_op jit(solution)/shard_map/all_to_all | solution.py:865
  353.4 280.3 %all-to-all-start.5 = ((f32[16,8,2,8,128]{4,3,2,1,0:T(8,128)}), f32[16,8,2,8,128]{4,3,2,1,0:T(8,128)}, u32[]{:S(2)}, u32[]{:S(2)}) async-start(f32[16,8,2,8,128]{4,3,2,1,0:T(8,128)} %get-tuple-element.51), calls=%async_computation.5 | async-start | bytes 2097152 | tf_op jit(solution)/shard_map/all_to_all | solution.py:873
  360.4 140.7 %all-reduce.7.cloned.1.call-start = ((), (), s32[]{:S(2)}) async-start(), calls=%async_computation.7 | async-start | bytes 2097152 | tf_op jit(solution)/shard_map/psum | solution.py:852
  364.3 267.8 %all-reduce.5.cloned.1.call-start = ((), (), s32[]{:S(2)}) async-start(), calls=%async_computation.6 | async-start | bytes 524288 | tf_op jit(solution)/shard_map/psum | solution.py:870
  364.3 272.4 %collective-permute-start.8 = (bf16[16,16,16,128]{3,2,1,0:T(8,128)(2,1)S(1)}, bf16[16,16,16,128]{3,2,1,0:T(8,128)(2,1)}, u32[]{:S(2)}, u32[]{:S(2)}) collective-permute-start(bf16[16,16,16,128]{3,2,1,0:T(8,128)(2,1)S(1)} %all-to-all-done.4.own), channel_id=1, source_target_pairs={{0,1},{1,0},{2,3},{3,2},{4,5},{5,4},{6,7},{7,6},{8,9},{9,8},{10,11... | collective-permute-start | bytes 3145736 | tf_op jit(solution)/shard_map/ppermute | solution.py:871
  366.0 285.6 %collective-permute-start.7 = (bf16[16,16,16,128]{3,2,1,0:T(8,128)(2,1)S(1)}, bf16[16,16,16,128]{3,2,1,0:T(8,128)(2,1)S(1)}, u32[]{:S(2)}, u32[]{:S(2)}) collective-permute-start(bf16[16,16,16,128]{3,2,1,0:T(8,128)(2,1)S(1)} %all_to_all.30.own), channel_id=1, source_target_pairs={{0,1},{1,0},{2,3},{3,2},{4,5},{5,4},{6,7},{7,6},{8,9},{9,8},{10,11... | collective-permute-start | bytes 3145736 | tf_op jit(solution)/shard_map/ppermute | solution.py:872
  389.7 247.0 %copy-start.2 = (bf16[256,256]{1,0:T(8,128)(2,1)S(1)}, bf16[256,256]{1,0:T(8,128)(2,1)}, u32[]{:S(2)}) copy-start(bf16[256,256]{1,0:T(8,128)(2,1)} %wd.3) | copy-start | bytes 393220
Sparse Core Ops, SparseCore 0:
  367.1 133.8 all-reduce.6
  508.0 123.9 all-reduce.4

commit v3 on v2

--- a/solution.py
+++ b/solution.py
@@ -484,8 +484,8 @@
             sums = [None] * span
             for north in range(span):
                 source = row + 2 * REACH - north
-                here = field[source, part, :].astype(jnp.float32)
-                ends = rim[source, part, :].astype(jnp.float32)
+                here = field[source, part, :]
+                ends = rim[source, part, :]
                 for east in range(span):
                     past = east - REACH
                     shifted = here
@@ -495,13 +495,14 @@
                     if past > 0:
                         rim_tile = jnp.where(lane >= LANES - past, ends, here[:, -LANES:])
                         shifted = jnp.concatenate([here[:, :-LANES], rim_tile], axis=1)
-                    weight = taps[(source * span + north) * span + east]
+                    weight = taps[(source * span + north) * span + east].astype(jnp.bfloat16)
                     term = shifted * weight
                     sums[east] = term if sums[east] is None else sums[east] + term
-            total = sums[REACH]
+            total = sums[REACH].astype(jnp.float32)
             for east in range(span):
                 if east != REACH:
-                    total = total + pltpu.roll(sums[east], (east - REACH) % columns, 1)
+                    moved = pltpu.roll(sums[east], (east - REACH) % columns, 1)
+                    total = total + moved.astype(jnp.float32)
             q_ref[row, part, :] = total.astype(jnp.bfloat16)
             return inner
 
@@ -820,9 +821,6 @@
     swap = [(i, (i + 1) % lon_count) for i in range(lon_count)]
     exchange = functools.partial(lax.all_to_all, axis_name="lat", split_axis=0, concat_axis=0, tiled=True)
 
-    gain = exchange(
-        gain_call(spectral_gain).reshape(lat_count, own, 2, degrees, LANES)
-    )
     kernel = disco_kernel(quad_weights, lat_offsets, lon_offsets, weight_index)
     kernel_pad = jnp.pad(kernel, ((REACH, REACH), (0, 0), (0, 0)))
     kernel_rim = lax.dynamic_slice_in_dim(kernel_pad, lat_index * rows, rows + 2 * REACH, 0)
@@ -849,16 +847,21 @@
     bottom, bottom_side = lax.ppermute((first[0][:REACH], sides[:REACH]), "lat", up)
     edges = jnp.concatenate([top_side, sides, bottom_side], axis=0)
     arrived1 = lax.ppermute(second[2], "lon", swap)
-    total_in, total_out = lax.psum((first[4] + second[4], first[5] + second[5]), ("lat", "lon"))
-    sum0, edges = lax.optimization_barrier((summed(first[1], arrived0), edges))
+    spectral_gain, kept1 = lax.optimization_barrier((spectral_gain, second[1]))
+    gain = gain_call(spectral_gain).reshape(lat_count, own, 2, degrees, LANES)
+    sums = (first[4] + second[4], first[5] + second[5])
+    sum0, gain, sums, edges = lax.optimization_barrier(
+        (summed(first[1], arrived0), gain, sums, edges)
+    )
     received0 = exchange(sum0)
+    gain = exchange(gain)
     stencil = functools.partial(
         stencil_call, taps=taps, first=first[0], second=second[0], top=top, bottom=bottom,
         edges=edges, place=place,
     )
     q = stencil(0, PARTS, previous=None)
     arrived1, q = lax.optimization_barrier((arrived1, q))
-    received1 = exchange(summed(second[1], arrived1))
+    received1 = exchange(summed(kept1, arrived1))
     q = stencil(1, PARTS, previous=q)
     received0, received1, q = lax.optimization_barrier((received0, received1, q))
     owned, s0, s1 = legendre_call(legendre, received0, received1, gain)
@@ -866,9 +869,20 @@
     local1 = exchange(s1)
     q, owned = lax.optimization_barrier((q, owned))
     disco_part = disco_grad_call(block_input, q)
-    disco_part, total_in, total_out = lax.optimization_barrier((disco_part, total_in, total_out))
-    total_disco = lax.psum(disco_part, ("lat", "lon"))
+    local0, disco_part = lax.optimization_barrier((local0, disco_part))
     other0 = lax.ppermute(local0, "lon", swap)
+    everyone = functools.partial(
+        lax.all_to_all, axis_name=("lat", "lon"), split_axis=0, concat_axis=0, tiled=True
+    )
+    count = lat_count * lon_count
+    half = w_in.shape[1] // 2
+    parts = (sums[0][:, :half], sums[0][:, half:], sums[1], disco_part)
+    stacked = jnp.concatenate(parts, axis=0).astype(jnp.bfloat16)
+    shares = everyone(stacked.reshape(count, -1, channels)).astype(jnp.float32).sum(axis=0)
+    shares = jnp.broadcast_to(shares.astype(jnp.bfloat16)[None], (count,) + shares.shape)
+    totals = everyone(shares).reshape(-1, channels).astype(jnp.float32)
+    total_in = jnp.concatenate([totals[:channels], totals[channels : 2 * channels]], axis=1)
+    total_out, total_disco = jnp.split(totals[2 * channels :], (2 * half,), axis=0)
     other1 = lax.ppermute(local1, "lon", swap)
     owned = exchange(owned).reshape(M * 2 * degrees, LANES)
     result = final_call(0, side, q, local0, other0, inverse, w_disco, None)

time: 674 us -> 465 us (0.69)
  waiting for transfers between devices: 311 us -> 62.3 us
  blocking collectives: 30.7 us -> 85.6 us
  between operations: 14.3 us -> 0.94 us
    psum x2 -> x0, waiting for transfers between devices: 239 us -> none  [the longest x1 127 us: shards_banded(): total_disco = lax.psum(disco_part, ('lat', 'lon'))]
    all_to_all x1 -> x3, blocking collectives: 30.7 us -> 85.6 us  [the longest x1 31.3 us: shards_banded(): received1 = exchange(summed(kept1, arrived1))]
    all_to_all x3, waiting for transfers between devices: 43.2 us -> 1.28 us  [the longest x1 1.27 us: shards_banded(): local1 = exchange(s1)]
    all_to_all x1, waiting for transfers between devices: 0.01 us -> 20.2 us  [shards_banded(): owned = exchange(owned).reshape(M * 2 * degrees, LANES)]
    ppermute x1, waiting for transfers between devices: 0.01 us -> 12.1 us  [shards_banded(): other1 = lax.ppermute(local1, 'lon', swap)]
  transfers between devices with their start and end apart: 16 -> 14, of which waited for: 8 -> 6; matrix products, arithmetic and copies ran while one was open for 3% -> 3% of each run, Pallas kernels for 26% -> 42%
where the time goes in v3:
time: 465 us; the launch traced here: 464 us
  Pallas kernels  249 us (54%)
  blocking collectives  85.6 us (18%)
  waiting for transfers between devices  62.3 us (13%)
  starting transfers between devices  39.8 us (9%)
  local copies, waits for them, and re-layouts  15.2 us (3%)
  other arithmetic  11 us (2%)
    pallas_call x2, Pallas kernels, stencil_call(): pl.pallas_call(functools.partial(stencil_kernel, rows=rows), grid=(1,), i...  93.1 us
    pallas_call x2, Pallas kernels, mlp_call(): pl.pallas_call(functools.partial(mlp_kernel, steps=steps, width=width, ch...  91.3 us
    all_to_all x1, blocking collectives, shards_banded(): received1 = exchange(summed(kept1, arrived1))  31.3 us
    all_to_all x1, blocking collectives, shards_banded(): local0 = exchange(s0)  30.7 us
    pallas_call x2, Pallas kernels, final_call(): pl.pallas_call(final_kernel, grid=(columns // width,), in_specs=[pl.Block...  29.5 us
    all_to_all x1, blocking collectives, shards_banded(): everyone(stacked.reshape(count, -1, channels)).astype(jnp.float32)  23.6 us
    pallas_call x1, Pallas kernels, disco_grad_call(): pl.pallas_call(disco_kernel_grad, grid=(rows // BAND,), in_specs=[pl.Bloc...  21.5 us
    ppermute x2, waiting for transfers between devices, shards_banded(): lax.ppermute((second[0][BAND - REACH:], sides[rows - REACH:]), 'lat', down)  21 us
  transfers between devices with their start and end apart: 14, of which 6 were waited for; matrix products, arithmetic and copies ran while one was open for 3% of the time, Pallas kernels for 42%

profile of v3, /device:TPU:0, one launch (start us, length us, event | category | flops | bytes accessed | tf_op | source)
XLA Modules:
  0.0 463.9 jit_solution(9295704728642897671)
XLA Ops:
  0.6 1.8 copy.31
  2.4 1.7 dynamic-slice_bitcast_fusion.table
  4.1 45.7 %mlp.2 = (bf16[16,256,512]{2,1,0:T(8,128)(2,1)}, bf16[256,16,128]{2,1,0:T(8,128)(2,1)}, bf16[256,16,128]{2,1,0:T(8,128)(2,1)}, bf16[16,16,256]{2,1,0:T(8,128)(2,...) custom-call(s32[1]{0:T(128)} %bitcast.side, bf16[256,32,512]{2,1,0:T(8,128)(2,1)} %x_ref.3, bf16[256,32,512]{2,1,0:T(8,128)(2,1)} %ct_ref.3, ...), custom_call_target="tpu_custom_call" | custom-call | flops 11811160064 | bytes 12582912 | tf_op jit(solution)/shard_map/mlp/pallas_call | solution.py:420
  49.8 3.0 collective-permute-start
  52.8 45.6 %mlp.3 = (bf16[16,256,512]{2,1,0:T(8,128)(2,1)}, bf16[256,16,128]{2,1,0:T(8,128)(2,1)}, bf16[256,16,128]{2,1,0:T(8,128)(2,1)}, bf16[16,16,256]{2,1,0:T(8,128)(2,...) custom-call(s32[1]{0:T(128)} %bitcast.side, bf16[256,32,512]{2,1,0:T(8,128)(2,1)} %x_ref.3, bf16[256,32,512]{2,1,0:T(8,128)(2,1)} %ct_ref.3, ...), custom_call_target="tpu_custom_call" | custom-call | flops 11811160064 | bytes 12582912 | tf_op jit(solution)/shard_map/mlp/pallas_call | solution.py:420
  99.6 7.7 %collective-permute-done.1 = bf16[32,16,256]{2,1,0:T(8,128)(2,1)S(1)} collective-permute-done((bf16[32,16,256]{2,1,0:T(8,128)(2,1)S(1)}, bf16[32,16,256]{2,1,0:T(8,128)(2,1)S(1)}, u32[]{:S(2)}, u32[]{:S(2)}) %collective-permute-start.1) | collective-permute-done | bytes 262176 | tf_op jit(solution)/shard_map/ppermute | solution.py:843
  108.0 2.8 collective-permute-start.3
  110.8 2.6 gain.1
  115.0 1.7 collective-permute-done.2
  118.0 4.3 all-to-all-start
  124.2 1.9 slice.32
  126.1 4.3 collective-permute-start.6
  131.6 19.4 %collective-permute-done.5.top = bf16[2,256,512]{2,1,0:T(8,128)(2,1)S(1)} collective-permute-done((bf16[2,256,512]{2,1,0:T(8,128)(2,1)S(1)}, bf16[2,256,512]{2,1,0:T(8,128)(2,1)S(1)}, u32[]{:S(2)}, u32[]{:S(2)}) %collective-permute-start.5) | collective-permute-done | bytes 524320 | tf_op jit(solution)/shard_map/ppermute | solution.py:844
  150.9 2.2 copy-done
  153.1 46.5 %stencil.2.rest_0_ = bf16[32,256,512]{2,1,0:T(8,128)(2,1)} custom-call(f32[900]{0:T(1024)S(1)} %reshape.64.taps, bf16[16,256,512]{2,1,0:T(8,128)(2,1)S(1)} %copy-done, bf16[16,256,512]{2,1,0:T(8,128)(2,1)} %get-tuple-element.50.second, bf16[2,256,512]{2,1,0:T(8,128)(2,1)S(1)} %collective-permute-done.5.top, ...), custom_call_target="tpu_custom_call" | custom-call | flops 125829120 | bytes 8388608 | tf_op jit(solution)/shard_map/stencil/pallas_call | solution.py:523
  201.2 31.3 %all_to_all.40.r1 = bf16[16,2,8,16,128]{4,3,2,1,0:T(8,128)(2,1)} all-to-all(bf16[16,2,8,16,128]{4,3,2,1,0:T(8,128)(2,1)S(1)} %bitcast.17), channel_id=1, replica_groups=mesh['lat'=16,'lon'=2] {'lat'}, dimensions={0} | all-to-all | bytes 2097152 | tf_op jit(solution)/shard_map/all_to_all | solution.py:864
  232.5 5.0 %all-to-all-start.2 = ((f32[16,8,2,8,128]{4,3,2,1,0:T(8,128)}), f32[16,8,2,8,128]{4,3,2,1,0:T(8,128)}, u32[]{:S(2)}, u32[]{:S(2)}) async-start(f32[16,8,2,8,128]{4,3,2,1,0:T(8,128)} %bitcast.18), calls=%async_computation.2 | async-start | bytes 2097152 | tf_op jit(solution)/shard_map/all_to_all | solution.py:857
  238.9 2.2 copy-done.1
  241.0 46.5 %stencil.3.q_ref = bf16[32,256,512]{2,1,0:T(8,128)(2,1)} custom-call(f32[900]{0:T(1024)S(1)} %reshape.64.taps, bf16[16,256,512]{2,1,0:T(8,128)(2,1)S(1)} %copy-done.1, bf16[16,256,512]{2,1,0:T(8,128)(2,1)} %get-tuple-element.50.second, bf16[2,256,512]{2,1,0:T(8,128)(2,1)S(1)} %collective-permute-done.5.top, ...), custom_call_target="tpu_custom_call", output_to_operand_aliasing={{}: (7, {})} | custom-call | flops 125829120 | bytes 8388608 | tf_op jit(solution)/shard_map/stencil/pallas_call | solution.py:523
  287.6 8.2 %legendre.1 = (f32[16,8,2,8,128]{4,3,2,1,0:T(8,128)}, bf16[16,16,16,128]{3,2,1,0:T(8,128)(2,1)S(1)}, bf16[16,16,16,128]{3,2,1,0:T(8,128)(2,1)}) custom-call(bf16[8,128,512]{2,1,0:T(8,128)(2,1)S(1)} %constant_dynamic-slice_fusion.leg, bf16[16,2,8,16,128]{4,3,2,1,0:T(8,128)(2,1)S(1)} %all-to-all-done.r0, bf16[16,2,8,16,128]{4,3,2,1,0:T(8,128)(2,1)} %all_to_all.40.r1, ...), custom_call_target="tpu_custom_call" | custom-call | flops 1073741824 | bytes 7340032 | tf_op jit(solution)/shard_map/legendre/pallas_call | solution.py:635
  295.8 30.7 %all_to_all.41.own = bf16[16,16,16,128]{3,2,1,0:T(8,128)(2,1)S(1)} all-to-all(bf16[16,16,16,128]{3,2,1,0:T(8,128)(2,1)S(1)} %get-tuple-element.61), channel_id=1, replica_groups=mesh['lat'=16,'lon'=2] {'lat'}, dimensions={0} | all-to-all | bytes 2097152 | tf_op jit(solution)/shard_map/all_to_all | solution.py:868
  326.5 5.0 %all-to-all-start.3 = ((bf16[16,16,16,128]{3,2,1,0:T(8,128)(2,1)}), bf16[16,16,16,128]{3,2,1,0:T(8,128)(2,1)S(1)}, u32[]{:S(2)}, u32[]{:S(2)}) async-start(bf16[16,16,16,128]{3,2,1,0:T(8,128)(2,1)} %get-tuple-element.60), calls=%async_computation.3 | async-start | bytes 2097152 | tf_op jit(solution)/shard_map/all_to_all | solution.py:869
  331.5 21.5 %disco_weight.1 = f32[256,256]{1,0:T(8,128)S(1)} custom-call(bf16[256,32,512]{2,1,0:T(8,128)(2,1)} %bi_ref.1, bf16[32,256,512]{2,1,0:T(8,128)(2,1)} %stencil.3.q_ref), custom_call_target="tpu_custom_call" | custom-call | flops 2147483648 | bytes 16777216 | tf_op jit(solution)/shard_map/disco_weight/pallas_call | solution.py:572
  354.4 23.6 %all_to_all.42 = bf16[32,40,256]{2,1,0:T(8,128)(2,1)} all-to-all(bf16[32,40,256]{2,1,0:T(8,128)(2,1)S(1)} %bitcast.19), channel_id=1, replica_groups=mesh['lat'=16,'lon'=2] {'lat','lon'}, dimensions={0} | all-to-all | bytes 1310720 | tf_op jit(solution)/shard_map/all_to_all | solution.py:881
  378.0 4.3 all-to-all-start.5
  385.1 20.2 %all-to-all-done.5 = f32[16,8,2,8,128]{4,3,2,1,0:T(8,128)} async-done(((f32[16,8,2,8,128]{4,3,2,1,0:T(8,128)}), f32[16,8,2,8,128]{4,3,2,1,0:T(8,128)}, u32[]{:S(2)}, u32[]{:S(2)}) %all-to-all-start.5) | async-done | bytes 1048608 | tf_op jit(solution)/shard_map/all_to_all | solution.py:887
  406.2 6.9 %all-to-all-start.7 = ((bf16[32,40,256]{2,1,0:T(8,128)(2,1)}), bf16[32,40,256]{2,1,0:T(8,128)(2,1)}, u32[]{:S(2)}, u32[]{:S(2)}) async-start(bf16[32,40,256]{2,1,0:T(8,128)(2,1)} %broadcast_in_dim.16), calls=%async_computation.7 | async-start | bytes 1310720 | tf_op jit(solution)/shard_map/all_to_all | solution.py:883
  413.0 1.8 collective-permute-start.7
  415.8 2.9 grad_gain.1
  418.7 14.6 %final.2.rest_0_ = bf16[256,32,512]{2,1,0:T(8,128)(2,1)} custom-call(s32[1]{0:T(128)} %bitcast.side, bf16[32,256,512]{2,1,0:T(8,128)(2,1)} %stencil.3.q_ref, bf16[16,16,16,128]{3,2,1,0:T(8,128)(2,1)S(1)} %all_to_all.41.own, bf16[16,16,16,128]{3,2,1,0:T(8,128)(2,1)S(1)} %collective-permute-done.8.other, ...), custom_call_target="tpu_custom_call" | custom-call | flops 2147483648 | bytes 10485760 | tf_op jit(solution)/shard_map/final/pallas_call | solution.py:691
  433.3 12.1 %collective-permute-done.7.other = bf16[16,16,16,128]{3,2,1,0:T(8,128)(2,1)} collective-permute-done((bf16[16,16,16,128]{3,2,1,0:T(8,128)(2,1)S(1)}, bf16[16,16,16,128]{3,2,1,0:T(8,128)(2,1)}, u32[]{:S(2)}, u32[]{:S(2)}) %collective-permute-start.7) | collective-permute-done | bytes 1048608 | tf_op jit(solution)/shard_map/ppermute | solution.py:886
  445.4 14.9 %final.3 = bf16[256,32,512]{2,1,0:T(8,128)(2,1)} custom-call(s32[1]{0:T(128)} %bitcast.side, bf16[32,256,512]{2,1,0:T(8,128)(2,1)} %stencil.3.q_ref, bf16[16,16,16,128]{3,2,1,0:T(8,128)(2,1)S(1)} %all-to-all-done.3.own, bf16[16,16,16,128]{3,2,1,0:T(8,128)(2,1)} %collective-permute-done.7.other, ...), custom_call_target="tpu_custom_call", output_to_operand_aliasing={{}: (6, {})} | custom-call | flops 2147483648 | bytes 10485760 | tf_op jit(solution)/shard_map/final/pallas_call | solution.py:691
  (77 shorter events, 20.2 us)
Async XLA Ops:
  49.8 48.6 %copy-start.14 = (bf16[16,16,256]{2,1,0:T(8,128)(2,1)S(1)}, bf16[16,16,256]{2,1,0:T(8,128)(2,1)}, u32[]{:S(2)}) copy-start(bf16[16,16,256]{2,1,0:T(8,128)(2,1)} %get-tuple-element.44) | copy-start | bytes 393220
  49.8 66.9 %collective-permute-start = (bf16[256,16,128]{2,1,0:T(8,128)(2,1)}, bf16[256,16,128]{2,1,0:T(8,128)(2,1)S(1)}, u32[]{:S(2)}, u32[]{:S(2)}) collective-permute-start(bf16[256,16,128]{2,1,0:T(8,128)(2,1)} %get-tuple-element.37), channel_id=1, source_target_pairs={{0,1},{1,0},{2,3},{3,2},{4,5},{5,4},{6,7},{7,6},{8,9},{9,8},{10,11... | collective-permute-start | bytes 3145736 | tf_op jit(solution)/shard_map/ppermute | solution.py:839
  98.4 15.1 %copy-start.9 = (f32[256,512]{1,0:T(8,128)S(1)}, f32[256,512]{1,0:T(8,128)}, u32[]{:S(2)}) copy-start(f32[256,512]{1,0:T(8,128)} %get-tuple-element.40) | copy-start | bytes 1572868
  98.4 15.1 %copy-start.11 = (f32[256,512]{1,0:T(8,128)S(1)}, f32[256,512]{1,0:T(8,128)}, u32[]{:S(2)}) copy-start(f32[256,512]{1,0:T(8,128)} %get-tuple-element.41) | copy-start | bytes 1572868
  98.4 15.9 %copy-start.8 = (f32[512,256]{1,0:T(8,128)S(1)}, f32[512,256]{1,0:T(8,128)}, u32[]{:S(2)}) copy-start(f32[512,256]{1,0:T(8,128)} %get-tuple-element.42) | copy-start | bytes 1572868
  98.4 15.8 %copy-start.10 = (f32[512,256]{1,0:T(8,128)S(1)}, f32[512,256]{1,0:T(8,128)}, u32[]{:S(2)}) copy-start(f32[512,256]{1,0:T(8,128)} %get-tuple-element.43) | copy-start | bytes 1572868
  99.5 7.8 %collective-permute-start.1 = (bf16[32,16,256]{2,1,0:T(8,128)(2,1)S(1)}, bf16[32,16,256]{2,1,0:T(8,128)(2,1)S(1)}, u32[]{:S(2)}, u32[]{:S(2)}) collective-permute-start(bf16[32,16,256]{2,1,0:T(8,128)(2,1)S(1)} %pad_maximum_fusion.2), channel_id=1, source_target_pairs={{0,1},{1,0},{2,3},{3,2},{4,5},{5,4},{6,7},{7,6},{8,9},{9,8},{10,11... | collective-permute-start | bytes 786440 | tf_op jit(solution)/shard_map/ppermute | solution.py:843
  108.0 7.0 %collective-permute-start.3 = (bf16[2,16,256]{2,1,0:T(8,128)(2,1)S(1)}, bf16[2,16,256]{2,1,0:T(8,128)(2,1)S(1)}, u32[]{:S(2)}, u32[]{:S(2)}) collective-permute-start(bf16[2,16,256]{2,1,0:T(8,128)(2,1)S(1)} %get-tuple-element.73), channel_id=1, source_target_pairs={{2,0},{4,2},{6,4},{8,6},{10,8},{12,10},{14,12},{16,14},{18,16},{20... | collective-permute-start | bytes 49160 | tf_op jit(solution)/shard_map/ppermute | solution.py:847
  110.8 5.9 %collective-permute-start.2 = (bf16[2,16,256]{2,1,0:T(8,128)(2,1)S(1)}, bf16[2,16,256]{2,1,0:T(8,128)(2,1)S(1)}, u32[]{:S(2)}, u32[]{:S(2)}) collective-permute-start(bf16[2,16,256]{2,1,0:T(8,128)(2,1)S(1)} %get-tuple-element.72), channel_id=1, source_target_pairs={{0,2},{2,4},{4,6},{6,8},{8,10},{10,12},{12,14},{14,16},{16,18},{18... | collective-permute-start | bytes 49160 | tf_op jit(solution)/shard_map/ppermute | solution.py:844
  113.5 3.2 copy-start.13
  113.5 3.3 copy-start.5
  118.0 12.4 %copy-start.17 = (s32[512,12]{0,1:T(8,128)S(1)}, s32[512,12]{0,1:T(8,128)}, u32[]{:S(2)}) copy-start(s32[512,12]{0,1:T(8,128)} %param.26) | copy-start | bytes 73732
  118.0 12.5 %copy-start.16 = (s32[512,12]{0,1:T(8,128)S(1)}, s32[512,12]{0,1:T(8,128)}, u32[]{:S(2)}) copy-start(s32[512,12]{0,1:T(8,128)} %param.27) | copy-start | bytes 73732
  118.0 12.5 %copy-start.18 = (f32[64]{0:T(128)S(1)}, f32[64]{0:T(128)}, u32[]{:S(2)}) copy-start(f32[64]{0:T(128)} %param.24) | copy-start | bytes 772
  118.0 12.8 %copy-start.15 = (s32[512,12]{0,1:T(8,128)S(1)}, s32[512,12]{0,1:T(8,128)}, u32[]{:S(2)}) copy-start(s32[512,12]{0,1:T(8,128)} %param.25) | copy-start | bytes 73732
  118.0 83.1 %all-to-all-start = ((bf16[16,2,8,16,128]{4,3,2,1,0:T(8,128)(2,1)}), bf16[16,2,8,16,128]{4,3,2,1,0:T(8,128)(2,1)S(1)}, u32[]{:S(2)}, u32[]{:S(2)}) async-start(bf16[16,2,8,16,128]{4,3,2,1,0:T(8,128)(2,1)} %bitcast.3), calls=%async_computation | async-start | bytes 2097152 | tf_op jit(solution)/shard_map/all_to_all | solution.py:856
  122.4 28.6 %copy-start.3 = (bf16[16,128]{1,0:T(8,128)(2,1)S(1)}, bf16[16,128]{1,0:T(8,128)(2,1)}, u32[]{:S(2)}) copy-start(bf16[16,128]{1,0:T(8,128)(2,1)} %constant.50.clone.place) | copy-start | bytes 12292
  122.4 77.3 %collective-permute-start.4 = (bf16[256,16,128]{2,1,0:T(8,128)(2,1)}, bf16[256,16,128]{2,1,0:T(8,128)(2,1)}, u32[]{:S(2)}, u32[]{:S(2)}) collective-permute-start(bf16[256,16,128]{2,1,0:T(8,128)(2,1)} %get-tuple-element.48), channel_id=1, source_target_pairs={{0,1},{1,0},{2,3},{3,2},{4,5},{5,4},{6,7},{7,6},{8,9},{9,8},{10,11... | collective-permute-start | bytes 3145736 | tf_op jit(solution)/shard_map/ppermute | solution.py:849
  124.0 26.9 %collective-permute-start.5 = (bf16[2,256,512]{2,1,0:T(8,128)(2,1)S(1)}, bf16[2,256,512]{2,1,0:T(8,128)(2,1)S(1)}, u32[]{:S(2)}, u32[]{:S(2)}) collective-permute-start(bf16[2,256,512]{2,1,0:T(8,128)(2,1)S(1)} %slice.31), channel_id=1, source_target_pairs={{0,2},{2,4},{4,6},{6,8},{8,10},{10,12},{12,14},{14,16},{16,18},{18... | collective-permute-start | bytes 1572872 | tf_op jit(solution)/shard_map/ppermute | solution.py:844
  126.1 24.8 %collective-permute-start.6 = (bf16[2,256,512]{2,1,0:T(8,128)(2,1)}, bf16[2,256,512]{2,1,0:T(8,128)(2,1)S(1)}, u32[]{:S(2)}, u32[]{:S(2)}) collective-permute-start(bf16[2,256,512]{2,1,0:T(8,128)(2,1)} %slice.32), channel_id=1, source_target_pairs={{2,0},{4,2},{6,4},{8,6},{10,8},{12,10},{14,12},{16,14},{18,16},{20... | collective-permute-start | bytes 1572872 | tf_op jit(solution)/shard_map/ppermute | solution.py:847
  150.9 2.2 copy-start
  153.1 46.5 %copy-start.4 = (bf16[256,16,128]{2,1,0:T(8,128)(2,1)S(1)}, bf16[256,16,128]{2,1,0:T(8,128)(2,1)}, u32[]{:S(2)}) copy-start(bf16[256,16,128]{2,1,0:T(8,128)(2,1)} %get-tuple-element.47) | copy-start | bytes 3145732
  232.5 55.1 %all-to-all-start.2 = ((f32[16,8,2,8,128]{4,3,2,1,0:T(8,128)}), f32[16,8,2,8,128]{4,3,2,1,0:T(8,128)}, u32[]{:S(2)}, u32[]{:S(2)}) async-start(f32[16,8,2,8,128]{4,3,2,1,0:T(8,128)} %bitcast.18), calls=%async_computation.2 | async-start | bytes 2097152 | tf_op jit(solution)/shard_map/all_to_all | solution.py:857
  238.9 2.2 copy-start.1
  295.8 35.7 %copy-start.7 = (bf16[256,512]{1,0:T(8,128)(2,1)S(1)}, bf16[256,512]{1,0:T(8,128)(2,1)}, u32[]{:S(2)}) copy-start(bf16[256,512]{1,0:T(8,128)(2,1)} %add.37) | copy-start | bytes 786436
  326.5 27.9 %all-to-all-start.3 = ((bf16[16,16,16,128]{3,2,1,0:T(8,128)(2,1)}), bf16[16,16,16,128]{3,2,1,0:T(8,128)(2,1)S(1)}, u32[]{:S(2)}, u32[]{:S(2)}) async-start(bf16[16,16,16,128]{3,2,1,0:T(8,128)(2,1)} %get-tuple-element.60), calls=%async_computation.3 | async-start | bytes 2097152 | tf_op jit(solution)/shard_map/all_to_all | solution.py:869
  331.5 21.6 %copy-start.6 = (bf16[512,256]{1,0:T(8,128)(2,1)S(1)}, bf16[512,256]{1,0:T(8,128)(2,1)}, u32[]{:S(2)}) copy-start(bf16[512,256]{1,0:T(8,128)(2,1)} %add.38) | copy-start | bytes 786436
  378.0 27.3 %all-to-all-start.5 = ((f32[16,8,2,8,128]{4,3,2,1,0:T(8,128)}), f32[16,8,2,8,128]{4,3,2,1,0:T(8,128)}, u32[]{:S(2)}, u32[]{:S(2)}) async-start(f32[16,8,2,8,128]{4,3,2,1,0:T(8,128)} %get-tuple-element.63), calls=%async_computation.5 | async-start | bytes 2097152 | tf_op jit(solution)/shard_map/all_to_all | solution.py:887
  382.3 36.4 %collective-permute-start.8 = (bf16[16,16,16,128]{3,2,1,0:T(8,128)(2,1)S(1)}, bf16[16,16,16,128]{3,2,1,0:T(8,128)(2,1)S(1)}, u32[]{:S(2)}, u32[]{:S(2)}) collective-permute-start(bf16[16,16,16,128]{3,2,1,0:T(8,128)(2,1)S(1)} %all_to_all.41.own), channel_id=1, source_target_pairs={{0,1},{1,0},{2,3},{3,2},{4,5},{5,4},{6,7},{7,6},{8,9},{9,8},{10,11... | collective-permute-start | bytes 3145736 | tf_op jit(solution)/shard_map/ppermute | solution.py:873
  406.2 54.1 %all-to-all-start.7 = ((bf16[32,40,256]{2,1,0:T(8,128)(2,1)}), bf16[32,40,256]{2,1,0:T(8,128)(2,1)}, u32[]{:S(2)}, u32[]{:S(2)}) async-start(bf16[32,40,256]{2,1,0:T(8,128)(2,1)} %broadcast_in_dim.16), calls=%async_computation.7 | async-start | bytes 1310720 | tf_op jit(solution)/shard_map/all_to_all | solution.py:883
  413.0 5.7 %copy-start.2 = (bf16[256,256]{1,0:T(8,128)(2,1)S(1)}, bf16[256,256]{1,0:T(8,128)(2,1)}, u32[]{:S(2)}) copy-start(bf16[256,256]{1,0:T(8,128)(2,1)} %wd.3) | copy-start | bytes 393220
  413.0 32.3 %collective-permute-start.7 = (bf16[16,16,16,128]{3,2,1,0:T(8,128)(2,1)S(1)}, bf16[16,16,16,128]{3,2,1,0:T(8,128)(2,1)}, u32[]{:S(2)}, u32[]{:S(2)}) collective-permute-start(bf16[16,16,16,128]{3,2,1,0:T(8,128)(2,1)S(1)} %all-to-all-done.3.own), channel_id=1, source_target_pairs={{0,1},{1,0},{2,3},{3,2},{4,5},{5,4},{6,7},{7,6},{8,9},{9,8},{10,11... | collective-permute-start | bytes 3145736 | tf_op jit(solution)/shard_map/ppermute | solution.py:886
  (1 other events, 0.7 us)

commit v4 on v3

--- a/solution.py
+++ b/solution.py
@@ -291,7 +291,6 @@
 
 BAND = 16
 LANES = 128
-PARTS = 2
 MIB = 1024 * 1024
 
 
@@ -346,9 +345,9 @@
 
 def mlp_kernel(
     side, x_ref, ct_ref, win_t, win, wout, table,
-    gf_ref, own_ref, send_ref, edge_ref, gin_ref, gout_ref,
+    gf_ref, own_ref, send_ref, edge_ref, halo_ref, gin_ref, gout_ref,
     stage, xs, cs, low, high,
-    *, steps, width, chunk,
+    *, steps, width, chunk, halo,
 ):
     step = pl.program_id(0)
 
@@ -380,10 +379,11 @@
         gout_ref[...] += mm_nt(act, c)
         return carry
 
-    lax.fori_loop(0, BAND * width // chunk, body, 0)
+    lax.fori_loop(0, BAND * width // chunk, body, 0, unroll=2)
 
     @pl.when(step == steps - 1)
     def _():
+        halo_ref[...] = gf_ref[halo : halo + REACH]
         orders = low.shape[0] // BAND
 
         def transform(row, carry):
@@ -393,7 +393,7 @@
             edge_ref[row] = out[orders:].astype(jnp.bfloat16)
             return carry
 
-        lax.fori_loop(0, BAND, transform, 0)
+        lax.fori_loop(0, BAND, transform, 0, unroll=2)
         first = side[0] == 0
         shape = own_ref.shape
 
@@ -418,7 +418,9 @@
     block = pl.BlockSpec((channels, BAND, width), lambda i: (0, band, i))
     cells = BAND * columns
     return pl.pallas_call(
-        functools.partial(mlp_kernel, steps=steps, width=width, chunk=chunk),
+        functools.partial(
+            mlp_kernel, steps=steps, width=width, chunk=chunk, halo=band * (BAND - REACH)
+        ),
         grid=(steps,),
         in_specs=[
             pl.BlockSpec(memory_space=pltpu.SMEM),
@@ -434,6 +436,7 @@
             whole_block((orders, BAND, LANES)),
             whole_block((orders, BAND, LANES)),
             whole_block((BAND, 16, channels)),
+            whole_block((REACH, channels, columns)),
             whole_block((channels, hidden)),
             whole_block((hidden, channels)),
         ],
@@ -442,6 +445,7 @@
             jax.ShapeDtypeStruct((orders, BAND, LANES), jnp.bfloat16),
             jax.ShapeDtypeStruct((orders, BAND, LANES), jnp.bfloat16),
             jax.ShapeDtypeStruct((BAND, 16, channels), jnp.bfloat16),
+            jax.ShapeDtypeStruct((REACH, channels, columns), jnp.bfloat16),
             jax.ShapeDtypeStruct((channels, hidden), jnp.float32),
             jax.ShapeDtypeStruct((hidden, channels), jnp.float32),
         ],
@@ -462,23 +466,29 @@
     )(side, filtered, cotangent, win_t, win, wout, table)
 
 
-def stencil_kernel(taps, first, second, top, bottom, edges, place, *rest, rows):
-    q_ref, field, rim = rest[-3:]
+def stencil_kernel(taps, before, rows, after, edges, place, q_ref, field, rim, *, first):
     channels, columns = field.shape[1:]
-    field[0:REACH] = top[...]
-    field[REACH : REACH + BAND] = first[...]
-    field[REACH + BAND : REACH + 2 * BAND] = second[...]
-    field[rows + REACH :] = bottom[...]
+    field[0:REACH] = before[...]
+    field[REACH : REACH + BAND] = rows[...]
+    field[REACH + BAND :] = after[...]
 
     def spread(row, carry):
-        rim[row] = mm_tn(edges[row], place[...])[: rim.shape[1]].astype(jnp.bfloat16)
+        rim[row] = mm_tn(edges[row], place[...]).astype(jnp.bfloat16)
         return carry
 
-    lax.fori_loop(0, rows + 2 * REACH, spread, 0)
+    lax.fori_loop(0, BAND + 2 * REACH, spread, 0, unroll=5)
     lane = lax.broadcasted_iota(jnp.int32, (16, LANES), 1)
     span = 2 * REACH + 1
 
     def row_body(row, carry):
+        weights = {}
+        for north in range(span):
+            source = row + 2 * REACH - north
+            for east in range(span):
+                weights[north, east] = taps[((first + source) * span + north) * span + east].astype(
+                    jnp.bfloat16
+                )
+
         def tile_body(tile, inner):
             part = pl.ds(pl.multiple_of(tile * 16, 16), 16)
             sums = [None] * span
@@ -495,8 +505,7 @@
                     if past > 0:
                         rim_tile = jnp.where(lane >= LANES - past, ends, here[:, -LANES:])
                         shifted = jnp.concatenate([here[:, :-LANES], rim_tile], axis=1)
-                    weight = taps[(source * span + north) * span + east].astype(jnp.bfloat16)
-                    term = shifted * weight
+                    term = shifted * weights[north, east]
                     sums[east] = term if sums[east] is None else sums[east] + term
             total = sums[REACH].astype(jnp.float32)
             for east in range(span):
@@ -506,57 +515,47 @@
             q_ref[row, part, :] = total.astype(jnp.bfloat16)
             return inner
 
-        return lax.fori_loop(0, channels // 16, tile_body, carry)
-
-    lax.fori_loop(0, rows, row_body, 0)
-
-
-def stencil_call(part, parts, taps, first, second, top, bottom, edges, place, previous):
-    rows = edges.shape[0] - 2 * REACH
-    _, channels, columns = first.shape
-    some = channels // parts
-    extra = [] if previous is None else [previous]
-
-    def piece(count):
-        return pl.BlockSpec((count, some, columns), lambda i: (0, part, 0))
+        return lax.fori_loop(0, channels // 16, tile_body, carry, unroll=4)
+
+    lax.fori_loop(0, BAND, row_body, 0)
+
+
+def stencil_call(band, taps, before, rows, after, edges, place):
+    _, channels, columns = rows.shape
+
+    def pair(index):
+        return pl.BlockSpec((REACH, channels, columns), lambda i: (index, 0, 0))
 
     return pl.pallas_call(
-        functools.partial(stencil_kernel, rows=rows),
+        functools.partial(stencil_kernel, first=band * BAND),
         grid=(1,),
         in_specs=[
             pl.BlockSpec(memory_space=pltpu.SMEM),
-            piece(BAND),
-            piece(BAND),
-            piece(REACH),
-            piece(REACH),
-            pl.BlockSpec(edges.shape[:2] + (LANES,), lambda i: (0, 0, part * some // LANES)),
-            pl.BlockSpec(memory_space=pltpu.VMEM),
-        ]
-        + [pl.BlockSpec(memory_space=pl.ANY)] * len(extra),
-        out_specs=piece(rows),
-        out_shape=jax.ShapeDtypeStruct((rows, channels, columns), jnp.bfloat16),
+            pair(before[1]),
+            whole_block(rows.shape),
+            pair(after[1]),
+            whole_block(edges.shape),
+            whole_block(place.shape),
+        ],
+        out_specs=whole_block(rows.shape),
+        out_shape=jax.ShapeDtypeStruct(rows.shape, jnp.bfloat16),
         scratch_shapes=[
-            pltpu.VMEM((rows + 2 * REACH, some, columns), jnp.bfloat16),
-            pltpu.VMEM((rows + 2 * REACH, some, LANES), jnp.bfloat16),
-        ],
-        input_output_aliases={7: 0} if extra else {},
+            pltpu.VMEM((BAND + 2 * REACH, channels, columns), jnp.bfloat16),
+            pltpu.VMEM((BAND + 2 * REACH, channels, LANES), jnp.bfloat16),
+        ],
         compiler_params=params(48),
         cost_estimate=pl.CostEstimate(
-            flops=60 * some * rows * columns,
-            bytes_accessed=4 * some * rows * columns,
+            flops=60 * channels * BAND * columns,
+            bytes_accessed=4 * channels * BAND * columns,
             transcendentals=0,
         ),
         name="stencil",
-    )(taps, first, second, top, bottom, edges, place, *extra)
+    )(taps, before[0], rows, after[0], edges, place)
 
 
 def disco_kernel_grad(bi_ref, q_ref, gd_ref, stage, flat):
     columns = q_ref.shape[2]
-
-    @pl.when(pl.program_id(0) == 0)
-    def _():
-        gd_ref[...] = jnp.zeros_like(gd_ref)
-
+    gd_ref[...] = jnp.zeros_like(gd_ref)
     rows_first(bi_ref, stage, flat, columns)
 
     def body(row, carry):
@@ -564,17 +563,17 @@
         gd_ref[...] += mm_nt(flat[:, cells], q_ref[row])
         return carry
 
-    lax.fori_loop(0, BAND, body, 0)
-
-
-def disco_grad_call(block_input, q):
-    channels, rows, columns = block_input.shape
+    lax.fori_loop(0, BAND, body, 0, unroll=4)
+
+
+def disco_grad_call(band, block_input, q):
+    channels, _, columns = block_input.shape
     return pl.pallas_call(
         disco_kernel_grad,
-        grid=(rows // BAND,),
+        grid=(1,),
         in_specs=[
-            pl.BlockSpec((channels, BAND, columns), lambda i: (0, i, 0)),
-            pl.BlockSpec((BAND, channels, columns), lambda i: (i, 0, 0)),
+            pl.BlockSpec((channels, BAND, columns), lambda i: (0, band, 0)),
+            whole_block(q.shape),
         ],
         out_specs=whole_block((channels, channels)),
         out_shape=jax.ShapeDtypeStruct((channels, channels), jnp.float32),
@@ -584,8 +583,8 @@
         ],
         compiler_params=params(48),
         cost_estimate=pl.CostEstimate(
-            flops=2 * channels * channels * rows * columns,
-            bytes_accessed=4 * channels * rows * columns,
+            flops=2 * channels * channels * BAND * columns,
+            bytes_accessed=4 * channels * BAND * columns,
             transcendentals=0,
         ),
         name="disco_weight",
@@ -662,29 +661,31 @@
     out_ref, stage = rest[-2:]
     width = q_ref.shape[2]
     orders = table.shape[0]
+    channels = out_ref.shape[0]
+    first = side[0] == 0
 
     def body(row, carry):
-        q = q_ref[row]
-        for half, ref in enumerate((own, other)):
-            base = pl.multiple_of((side[0] + half) % 2 * LANES, LANES)
-            synth = ref[:, row].reshape(orders, LANES)
-            out = mm_tn(synth, table[...]) + mm(wd[pl.ds(base, LANES), :], q)
-            for tile in range(width // LANES):
-                stage[tile, pl.ds(base * BAND + row, LANES, stride=BAND), :] = out[
-                    :, tile * LANES : (tile + 1) * LANES
-                ]
+        mine = own[:, row].reshape(orders, LANES)
+        theirs = other[:, row].reshape(orders, LANES)
+        synth = jnp.concatenate(
+            [jnp.where(first, mine, theirs), jnp.where(first, theirs, mine)], axis=1
+        )
+        out = mm_tn(synth, table[...]) + mm(wd[...], q_ref[row])
+        for tile in range(width // LANES):
+            stage[tile, pl.ds(row, channels, stride=BAND), :] = out[
+                :, tile * LANES : (tile + 1) * LANES
+            ]
         return carry
 
-    lax.fori_loop(0, BAND, body, 0)
-    channels = out_ref.shape[0]
+    lax.fori_loop(0, BAND, body, 0, unroll=2)
     for tile in range(width // LANES):
         out_ref[:, :, tile * LANES : (tile + 1) * LANES] = (
             stage[tile].astype(jnp.bfloat16).reshape(channels, BAND, LANES)
         )
 
 
-def final_call(band, side, q, own, other, table, wd, previous):
-    rows, channels, columns = q.shape
+def final_call(band, rows, side, q, own, other, table, wd, previous):
+    _, channels, columns = q.shape
     width = 2 * LANES
     cells = BAND * columns
     extra = [] if previous is None else [previous]
@@ -693,7 +694,7 @@
         grid=(columns // width,),
         in_specs=[
             pl.BlockSpec(memory_space=pltpu.SMEM),
-            pl.BlockSpec((BAND, channels, width), lambda i: (band, 0, i)),
+            pl.BlockSpec((BAND, channels, width), lambda i: (0, 0, i)),
             whole_block(own.shape),
             whole_block(other.shape),
             pl.BlockSpec((table.shape[0], width), lambda i: (0, i)),
@@ -831,62 +832,72 @@
     place = jnp.asarray(place, jnp.bfloat16)
     w_in_t = w_in.T
 
+    down = [(i, (i + 1) % lat_count) for i in range(lat_count)]
+    up = [(target, source) for source, target in down]
+
+    def across(moves):
+        return [
+            (a * lon_count + i, b * lon_count + j) for a, b in moves for i, j in swap
+        ]
+
     def summed(kept, arrived):
         total = (kept.astype(jnp.float32) + arrived.astype(jnp.float32)).astype(jnp.bfloat16)
         return total.reshape(lat_count, 2, own, BAND, LANES)
 
-    first = mlp_call(0, side, filtered, cotangent, w_in_t, w_in, w_out, forward)
-    arrived0 = lax.ppermute(first[2], "lon", swap)
-    second = mlp_call(1, side, filtered, cotangent, w_in_t, w_in, w_out, forward)
-    down = [(i, (i + 1) % lat_count) for i in range(lat_count)]
-    up = [(target, source) for source, target in down]
-    sides = lax.ppermute(jnp.concatenate([first[3], second[3]], axis=0), "lon", swap)
-    top, top_side = lax.ppermute(
-        (second[0][BAND - REACH :], sides[rows - REACH :]), "lat", down
-    )
-    bottom, bottom_side = lax.ppermute((first[0][:REACH], sides[:REACH]), "lat", up)
-    edges = jnp.concatenate([top_side, sides, bottom_side], axis=0)
-    arrived1 = lax.ppermute(second[2], "lon", swap)
-    spectral_gain, kept1 = lax.optimization_barrier((spectral_gain, second[1]))
     gain = gain_call(spectral_gain).reshape(lat_count, own, 2, degrees, LANES)
-    sums = (first[4] + second[4], first[5] + second[5])
-    sum0, gain, sums, edges = lax.optimization_barrier(
-        (summed(first[1], arrived0), gain, sums, edges)
-    )
+    gain = exchange(gain)
+    gf0, kept0, sent0, ends0, head, gin0, gout0 = mlp_call(
+        0, side, filtered, cotangent, w_in_t, w_in, w_out, forward
+    )
+    arrived0 = lax.ppermute(sent0, "lon", swap)
+    bottom = lax.ppermute(head, "lat", up)
+    sides0 = lax.ppermute(ends0, "lon", swap)
+    bottom_side = lax.ppermute(ends0[:REACH], ("lat", "lon"), across(up))
+    gain, w_in_t = lax.optimization_barrier((gain, w_in_t))
+    gf1, kept1, sent1, ends1, tail, gin1, gout1 = mlp_call(
+        1, side, filtered, cotangent, w_in_t, w_in, w_out, forward
+    )
+    sides1 = lax.ppermute(ends1, "lon", swap)
+    top = lax.ppermute(tail, "lat", down)
+    top_side = lax.ppermute(ends1[BAND - REACH :], ("lat", "lon"), across(down))
+    sent1, sides1 = lax.optimization_barrier((sent1, sides1))
+    arrived1 = lax.ppermute(sent1, "lon", swap)
+    edges1 = jnp.concatenate([sides0[BAND - REACH :], sides1, bottom_side], axis=0)
+    sum0, edges1 = lax.optimization_barrier((summed(kept0, arrived0), edges1))
     received0 = exchange(sum0)
-    gain = exchange(gain)
-    stencil = functools.partial(
-        stencil_call, taps=taps, first=first[0], second=second[0], top=top, bottom=bottom,
-        edges=edges, place=place,
-    )
-    q = stencil(0, PARTS, previous=None)
-    arrived1, q = lax.optimization_barrier((arrived1, q))
+    q1 = stencil_call(1, taps, (gf0, BAND // REACH - 1), gf1, (bottom, 0), edges1, place)
+    arrived1, q1 = lax.optimization_barrier((arrived1, q1))
     received1 = exchange(summed(kept1, arrived1))
-    q = stencil(1, PARTS, previous=q)
-    received0, received1, q = lax.optimization_barrier((received0, received1, q))
+    edges0 = jnp.concatenate([top_side, sides0, sides1[:REACH]], axis=0)
+    q0 = stencil_call(0, taps, (top, 0), gf0, (gf1, 0), edges0, place)
+    received0, received1, q0 = lax.optimization_barrier((received0, received1, q0))
     owned, s0, s1 = legendre_call(legendre, received0, received1, gain)
     local0 = exchange(s0)
+    q1, owned = lax.optimization_barrier((q1, owned))
+    disco1 = disco_grad_call(1, block_input, q1)
+    local0, disco1, s1, q0 = lax.optimization_barrier((local0, disco1, s1, q0))
     local1 = exchange(s1)
-    q, owned = lax.optimization_barrier((q, owned))
-    disco_part = disco_grad_call(block_input, q)
-    local0, disco_part = lax.optimization_barrier((local0, disco_part))
+    disco0 = disco_grad_call(0, block_input, q0)
     other0 = lax.ppermute(local0, "lon", swap)
     everyone = functools.partial(
         lax.all_to_all, axis_name=("lat", "lon"), split_axis=0, concat_axis=0, tiled=True
     )
     count = lat_count * lon_count
     half = w_in.shape[1] // 2
-    parts = (sums[0][:, :half], sums[0][:, half:], sums[1], disco_part)
+    gin = gin0 + gin1
+    parts = (gin[:, :half], gin[:, half:], gout0 + gout1, disco0 + disco1)
     stacked = jnp.concatenate(parts, axis=0).astype(jnp.bfloat16)
+    stacked, local1 = lax.optimization_barrier((stacked, local1))
     shares = everyone(stacked.reshape(count, -1, channels)).astype(jnp.float32).sum(axis=0)
     shares = jnp.broadcast_to(shares.astype(jnp.bfloat16)[None], (count,) + shares.shape)
+    shares, owned = lax.optimization_barrier((shares, owned))
     totals = everyone(shares).reshape(-1, channels).astype(jnp.float32)
     total_in = jnp.concatenate([totals[:channels], totals[channels : 2 * channels]], axis=1)
     total_out, total_disco = jnp.split(totals[2 * channels :], (2 * half,), axis=0)
     other1 = lax.ppermute(local1, "lon", swap)
     owned = exchange(owned).reshape(M * 2 * degrees, LANES)
-    result = final_call(0, side, q, local0, other0, inverse, w_disco, None)
-    result = final_call(1, side, q, local1, other1, inverse, w_disco, result)
+    result = final_call(0, rows, side, q0, local0, other0, inverse, w_disco, None)
+    result = final_call(1, rows, side, q1, local1, other1, inverse, w_disco, result)
     grad_gain = grad_gain_call(owned, spectral_saved)
     scale = 1.0 / math.sqrt(NLAT * NLON)
     return (result, grad_gain, total_in * scale, total_out * scale, total_disco * scale)

time: 465 us -> 393 us (0.85)
  Pallas kernels: 249 us -> 176 us
  blocking collectives: 85.6 us -> 23.5 us
  waiting for transfers between devices: 62.3 us -> 104 us
  starting transfers between devices: 39.8 us -> 63.1 us
    all_to_all x2 -> x0, blocking collectives: 62 us -> none  [the longest x1 31.3 us: shards_banded(): received1 = exchange(summed(kept1, arrived1))]
    pallas_call x3 -> x4, Pallas kernels: 115 us -> 56.5 us  [the longest x2 38.9 us: stencil_call(): pl.pallas_call(functools.partial(stencil_kernel, first=band * BAND), grid...]
    all_to_all x1, waiting for transfers between devices: 20.2 us -> 0.01 us  [shards_banded(): owned = exchange(owned).reshape(M * 2 * degrees, LANES)]
    all_to_all x0 -> x2, starting transfers between devices: none -> 17.5 us  [the longest x1 10.9 us: shards_banded(): received1 = exchange(summed(kept1, arrived1))]
    ppermute x7 -> x8, waiting for transfers between devices: 28.8 us -> 44.9 us  [the longest x1 24.5 us: shards_banded(): top_side = lax.ppermute(ends1[BAND - REACH:], ('lat', 'lon'), across(down))]
    all_to_all x1, waiting for transfers between devices: 0.01 us -> 15.7 us  [shards_banded(): totals = everyone(shares).reshape(-1, channels).astype(jnp.float32)]
    all_to_all x0 -> x2, waiting for transfers between devices: none -> 11.9 us  [the longest x1 11.9 us: shards_banded(): local0 = exchange(s0)]
    ppermute x1, waiting for transfers between devices: 0.01 us -> 9.7 us  [shards_banded(): other0 = lax.ppermute(local0, 'lon', swap)]
  transfers between devices with their start and end apart: 14 -> 17, of which waited for: 6 -> 8; matrix products, arithmetic and copies ran while one was open for 3% -> 4% of each run, Pallas kernels for 42% -> 41%
where the time goes in v4:
time: 393 us; the launch traced here: 392 us
  Pallas kernels  176 us (45%)
  waiting for transfers between devices  104 us (26%)
  starting transfers between devices  63.1 us (16%)
  blocking collectives  23.5 us (6%)
  local copies, waits for them, and re-layouts  16.1 us (4%)
  other arithmetic  8.27 us (2%)
    pallas_call x2, Pallas kernels, mlp_call(): pl.pallas_call(functools.partial(mlp_kernel, steps=steps, width=width, ch...  84.8 us
    pallas_call x2, Pallas kernels, stencil_call(): pl.pallas_call(functools.partial(stencil_kernel, first=band * BAND), grid...  38.9 us
    ppermute x1, waiting for transfers between devices, shards_banded(): top_side = lax.ppermute(ends1[BAND - REACH:], ('lat', 'lon'), across(down))  24.5 us
    all_to_all x1, blocking collectives, shards_banded(): everyone(stacked.reshape(count, -1, channels)).astype(jnp.float32)  23.5 us
    pallas_call x2, Pallas kernels, final_call(): pl.pallas_call(final_kernel, grid=(columns // width,), in_specs=[pl.Block...  20.4 us
    pallas_call x2, Pallas kernels, disco_grad_call(): pl.pallas_call(disco_kernel_grad, grid=(1,), in_specs=[pl.BlockSpec((chan...  17.6 us
    ppermute x1, waiting for transfers between devices, shards_banded(): bottom = lax.ppermute(head, 'lat', up)  17 us
    all_to_all x1, waiting for transfers between devices, shards_banded(): totals = everyone(shares).reshape(-1, channels).astype(jnp.float32)  15.7 us
  transfers between devices with their start and end apart: 17, of which 8 were waited for; matrix products, arithmetic and copies ran while one was open for 4% of the time, Pallas kernels for 41%

profile of v4, /device:TPU:0, one launch (start us, length us, event | category | flops | bytes accessed | tf_op | source)
XLA Modules:
  0.0 391.9 jit_solution(8049786721960332651)
XLA Ops:
  0.7 2.7 gain.1
  3.4 7.4 %all-to-all-start = ((f32[16,8,2,8,128]{4,3,2,1,0:T(8,128)}), f32[16,8,2,8,128]{4,3,2,1,0:T(8,128)S(1)}, u32[]{:S(2)}, u32[]{:S(2)}) async-start(f32[16,8,2,8,128]{4,3,2,1,0:T(8,128)} %bitcast.17), calls=%async_computation | async-start | bytes 2097152 | tf_op jit(solution)/shard_map/all_to_all | solution.py:848
  12.3 42.2 %mlp.3 = (bf16[16,256,512]{2,1,0:T(8,128)(2,1)}, bf16[256,16,128]{2,1,0:T(8,128)(2,1)}, bf16[256,16,128]{2,1,0:T(8,128)(2,1)}, bf16[16,16,256]{2,1,0:T(8,128)(2,...) custom-call(s32[1]{0:T(128)} %bitcast.side, bf16[256,32,512]{2,1,0:T(8,128)(2,1)} %x_ref.3, ...), custom_call_target="tpu_custom_call" | custom-call | flops 11811160064 | bytes 12582912 | tf_op jit(solution)/shard_map/mlp/pallas_call | solution.py:420
  57.3 4.8 %collective-permute-start.5 = (bf16[2,16,256]{2,1,0:T(8,128)(2,1)S(1)}, bf16[2,16,256]{2,1,0:T(8,128)(2,1)S(1)}, u32[]{:S(2)}, u32[]{:S(2)}) collective-permute-start(bf16[2,16,256]{2,1,0:T(8,128)(2,1)S(1)} %slice.30), channel_id=1, source_target_pairs={{2,1},{3,0},{4,3},{5,2},{6,5},{7,4},{8,7},{9,6},{10,9},{11,8},{12,... | collective-permute-start | bytes 49160 | tf_op jit(solution)/shard_map/ppermute | solution.py:855
  62.1 42.6 %mlp.2 = (bf16[16,256,512]{2,1,0:T(8,128)(2,1)}, bf16[256,16,128]{2,1,0:T(8,128)(2,1)}, bf16[256,16,128]{2,1,0:T(8,128)(2,1)}, bf16[16,16,256]{2,1,0:T(8,128)(2,...) custom-call(s32[1]{0:T(128)} %bitcast.side, bf16[256,32,512]{2,1,0:T(8,128)(2,1)} %x_ref.3, ...), custom_call_target="tpu_custom_call" | custom-call | flops 11811160064 | bytes 12582912 | tf_op jit(solution)/shard_map/mlp/pallas_call | solution.py:420
  106.5 3.4 collective-permute-done
  110.0 5.0 %all-to-all-start.1 = ((bf16[16,2,8,16,128]{4,3,2,1,0:T(8,128)(2,1)}), bf16[16,2,8,16,128]{4,3,2,1,0:T(8,128)(2,1)S(1)}, u32[]{:S(2)}, u32[]{:S(2)}) async-start(bf16[16,2,8,16,128]{4,3,2,1,0:T(8,128)(2,1)} %bitcast.5), calls=%async_computation.1 | async-start | bytes 2097152 | tf_op jit(solution)/shard_map/all_to_all | solution.py:867
  116.6 4.0 %collective-permute-start.2 = (bf16[2,256,512]{2,1,0:T(8,128)(2,1)}, bf16[2,256,512]{2,1,0:T(8,128)(2,1)S(1)}, u32[]{:S(2)}, u32[]{:S(2)}) collective-permute-start(bf16[2,256,512]{2,1,0:T(8,128)(2,1)} %get-tuple-element.49), channel_id=1, source_target_pairs={{2,0},{4,2},{6,4},{8,6},{10,8},{12,10},{14,12},{16,14},{18,16},{20... | collective-permute-start | bytes 1572872 | tf_op jit(solution)/shard_map/ppermute | solution.py:853
  121.8 17.0 %collective-permute-done.2.after = bf16[2,256,512]{2,1,0:T(8,128)(2,1)S(1)} collective-permute-done((bf16[2,256,512]{2,1,0:T(8,128)(2,1)}, bf16[2,256,512]{2,1,0:T(8,128)(2,1)S(1)}, u32[]{:S(2)}, u32[]{:S(2)}) %collective-permute-start.2) | collective-permute-done | bytes 524320 | tf_op jit(solution)/shard_map/ppermute | solution.py:853
  138.8 19.5 %stencil.2.q_ref = bf16[16,256,512]{2,1,0:T(8,128)(2,1)S(1)} custom-call(f32[900]{0:T(1024)S(1)} %reshape.63.taps, bf16[16,256,512]{2,1,0:T(8,128)(2,1)} %get-tuple-element.47.before.rows, bf16[16,256,512]{2,1,0:T(8,128)(2,1)} %get-tuple-element.48.rows.after, bf16[2,256,512]{2,1,0:T(8,128)(2,1)S(1)} %collective-permute-done.2.after, ...), custom_call_target="tpu_custom_call" | custom-call | flops 125829120 | bytes 8388608 | tf_op jit(solution)/shard_map/stencil/pallas_call | solution.py:529
  161.6 10.9 %all-to-all-start.2 = ((bf16[16,2,8,16,128]{4,3,2,1,0:T(8,128)(2,1)}), bf16[16,2,8,16,128]{4,3,2,1,0:T(8,128)(2,1)}, u32[]{:S(2)}, u32[]{:S(2)}) async-start(bf16[16,2,8,16,128]{4,3,2,1,0:T(8,128)(2,1)} %bitcast.6), calls=%async_computation.2 | async-start | bytes 2097152 | tf_op jit(solution)/shard_map/all_to_all | solution.py:870
  173.5 2.8 collective-permute-start.7
  177.7 24.5 %collective-permute-done.7 = bf16[2,16,256]{2,1,0:T(8,128)(2,1)S(1)} collective-permute-done((bf16[2,16,256]{2,1,0:T(8,128)(2,1)S(1)}, bf16[2,16,256]{2,1,0:T(8,128)(2,1)S(1)}, u32[]{:S(2)}, u32[]{:S(2)}) %collective-permute-start.7) | collective-permute-done | bytes 16416 | tf_op jit(solution)/shard_map/ppermute | solution.py:862
  202.2 19.4 %stencil.3.q_ref = bf16[16,256,512]{2,1,0:T(8,128)(2,1)S(1)} custom-call(f32[900]{0:T(1024)S(1)} %reshape.63.taps, bf16[2,256,512]{2,1,0:T(8,128)(2,1)S(1)} %collective-permute-done.6.before, bf16[16,256,512]{2,1,0:T(8,128)(2,1)} %get-tuple-element.47.before.rows, bf16[16,256,512]{2,1,0:T(8,128)(2,1)} %get-tuple-element.48.rows.after, ...), custom_call_target="tpu_custom_call" | custom-call | flops 125829120 | bytes 8388608 | tf_op jit(solution)/shard_map/stencil/pallas_call | solution.py:529
  223.6 8.4 %legendre.1 = (f32[16,8,2,8,128]{4,3,2,1,0:T(8,128)S(1)}, bf16[16,16,16,128]{3,2,1,0:T(8,128)(2,1)}, bf16[16,16,16,128]{3,2,1,0:T(8,128)(2,1)}) custom-call(bf16[8,128,512]{2,1,0:T(8,128)(2,1)S(1)} %constant_dynamic-slice_fusion.leg, bf16[16,2,8,16,128]{4,3,2,1,0:T(8,128)(2,1)S(1)} %all-to-all-done.1.r0, bf16[16,2,8,16,128]{4,3,2,1,0:T(8,128)(2,1)} %all-to-all-done.2.r1, ...), custom_call_target="tpu_custom_call" | custom-call | flops 1073741824 | bytes 7340032 | tf_op jit(solution)/shard_map/legendre/pallas_call | solution.py:634
  233.0 6.6 %all-to-all-start.3 = ((bf16[16,16,16,128]{3,2,1,0:T(8,128)(2,1)}), bf16[16,16,16,128]{3,2,1,0:T(8,128)(2,1)S(1)}, u32[]{:S(2)}, u32[]{:S(2)}) async-start(bf16[16,16,16,128]{3,2,1,0:T(8,128)(2,1)} %get-tuple-element.69), calls=%async_computation.3 | async-start | bytes 2097152 | tf_op jit(solution)/shard_map/all_to_all | solution.py:875
  239.6 2.2 copy-done.1
  241.8 8.8 %disco_weight.2 = f32[256,256]{1,0:T(8,128)S(1)} custom-call(bf16[256,32,512]{2,1,0:T(8,128)(2,1)} %bi_ref.3, bf16[16,256,512]{2,1,0:T(8,128)(2,1)S(1)} %copy-done.1), custom_call_target="tpu_custom_call" | custom-call | flops 1073741824 | bytes 8388608 | tf_op jit(solution)/shard_map/disco_weight/pallas_call | solution.py:571
  250.6 11.9 %all-to-all-done.3.own = bf16[16,16,16,128]{3,2,1,0:T(8,128)(2,1)S(1)} async-done(((bf16[16,16,16,128]{3,2,1,0:T(8,128)(2,1)}), bf16[16,16,16,128]{3,2,1,0:T(8,128)(2,1)S(1)}, u32[]{:S(2)}, u32[]{:S(2)}) %all-to-all-start.3) | async-done | bytes 1048608 | tf_op jit(solution)/shard_map/all_to_all | solution.py:875
  262.5 6.9 %all-to-all-start.4 = ((bf16[16,16,16,128]{3,2,1,0:T(8,128)(2,1)}), bf16[16,16,16,128]{3,2,1,0:T(8,128)(2,1)S(1)}, u32[]{:S(2)}, u32[]{:S(2)}) async-start(bf16[16,16,16,128]{3,2,1,0:T(8,128)(2,1)} %get-tuple-element.74), calls=%async_computation.4 | async-start | bytes 2097152 | tf_op jit(solution)/shard_map/all_to_all | solution.py:879
  270.7 2.2 copy-done.3
  272.9 8.8 %disco_weight.3 = f32[256,256]{1,0:T(8,128)S(1)} custom-call(bf16[256,32,512]{2,1,0:T(8,128)(2,1)} %bi_ref.3, bf16[16,256,512]{2,1,0:T(8,128)(2,1)S(1)} %copy-done.3), custom_call_target="tpu_custom_call" | custom-call | flops 1073741824 | bytes 8388608 | tf_op jit(solution)/shard_map/disco_weight/pallas_call | solution.py:571
  281.8 10.5 %all-to-all-done.4.own = bf16[16,16,16,128]{3,2,1,0:T(8,128)(2,1)S(1)} async-done(((bf16[16,16,16,128]{3,2,1,0:T(8,128)(2,1)}), bf16[16,16,16,128]{3,2,1,0:T(8,128)(2,1)S(1)}, u32[]{:S(2)}, u32[]{:S(2)}) %all-to-all-start.4) | async-done | bytes 1048608 | tf_op jit(solution)/shard_map/all_to_all | solution.py:879
  292.3 23.5 %all_to_all.40 = bf16[32,40,256]{2,1,0:T(8,128)(2,1)S(1)} all-to-all(bf16[32,40,256]{2,1,0:T(8,128)(2,1)S(1)} %bitcast.18), channel_id=1, replica_groups=mesh['lat'=16,'lon'=2] {'lat','lon'}, dimensions={0} | all-to-all | bytes 1310720 | tf_op jit(solution)/shard_map/all_to_all | solution.py:891
  316.8 3.7 all-to-all-start.7
  322.6 15.7 %all-to-all-done.7 = bf16[32,40,256]{2,1,0:T(8,128)(2,1)} async-done(((bf16[32,40,256]{2,1,0:T(8,128)(2,1)}), bf16[32,40,256]{2,1,0:T(8,128)(2,1)}, u32[]{:S(2)}, u32[]{:S(2)}) %all-to-all-start.7) | async-done | bytes 655392 | tf_op jit(solution)/shard_map/all_to_all | solution.py:894
  338.3 4.3 %all-to-all-start.6 = ((f32[16,8,2,8,128]{4,3,2,1,0:T(8,128)}), f32[16,8,2,8,128]{4,3,2,1,0:T(8,128)}, u32[]{:S(2)}, u32[]{:S(2)}) async-start(f32[16,8,2,8,128]{4,3,2,1,0:T(8,128)} %copy-done.4), calls=%async_computation.6 | async-start | bytes 2097152 | tf_op jit(solution)/shard_map/all_to_all | solution.py:898
  343.7 9.7 %collective-permute-done.9.other = bf16[16,16,16,128]{3,2,1,0:T(8,128)(2,1)} collective-permute-done((bf16[16,16,16,128]{3,2,1,0:T(8,128)(2,1)S(1)}, bf16[16,16,16,128]{3,2,1,0:T(8,128)(2,1)}, u32[]{:S(2)}, u32[]{:S(2)}) %collective-permute-start.9) | collective-permute-done | bytes 1048608 | tf_op jit(solution)/shard_map/ppermute | solution.py:881
  353.4 10.3 %final.2.rest_0_ = bf16[256,32,512]{2,1,0:T(8,128)(2,1)} custom-call(s32[1]{0:T(128)} %bitcast.side, bf16[16,256,512]{2,1,0:T(8,128)(2,1)} %copy-done.2, bf16[16,16,16,128]{3,2,1,0:T(8,128)(2,1)S(1)} %all-to-all-done.3.own, bf16[16,16,16,128]{3,2,1,0:T(8,128)(2,1)} %collective-permute-done.9.other, bf16[256,512]{1,0:T(8,128)(2,1)S(1)} %dynamic-slice_bitcast_fusion.1.table, ...), custom_call_target="tpu_custom_call" | custom-call | flops 2147483648 | bytes 10485760 | tf_op jit(solution)/shard_map/final/pallas_call | solution.py:692
  363.7 11.5 %collective-permute-done.8.other = bf16[16,16,16,128]{3,2,1,0:T(8,128)(2,1)S(1)} collective-permute-done((bf16[16,16,16,128]{3,2,1,0:T(8,128)(2,1)S(1)}, bf16[16,16,16,128]{3,2,1,0:T(8,128)(2,1)S(1)}, u32[]{:S(2)}, u32[]{:S(2)}) %collective-permute-start.8) | collective-permute-done | bytes 1048608 | tf_op jit(solution)/shard_map/ppermute | solution.py:897
  375.2 10.1 %final.3 = bf16[256,32,512]{2,1,0:T(8,128)(2,1)} custom-call(s32[1]{0:T(128)} %bitcast.side, bf16[16,256,512]{2,1,0:T(8,128)(2,1)} %copy-done, bf16[16,16,16,128]{3,2,1,0:T(8,128)(2,1)S(1)} %all-to-all-done.4.own, bf16[16,16,16,128]{3,2,1,0:T(8,128)(2,1)S(1)} %collective-permute-done.8.other, ...), custom_call_target="tpu_custom_call", output_to_operand_aliasing={{}: (6, {})} | custom-call | flops 2147483648 | bytes 10485760 | tf_op jit(solution)/shard_map/final/pallas_call | solution.py:692
  389.0 2.9 grad_gain.1
  (88 shorter events, 26.7 us)
Async XLA Ops:
  0.6 10.1 %copy-start.13 = (bf16[256,512]{1,0:T(8,128)(2,1)S(1)}, bf16[256,512]{1,0:T(8,128)(2,1)}, u32[]{:S(2)}) copy-start(bf16[256,512]{1,0:T(8,128)(2,1)} %win.3) | copy-start | bytes 786436
  0.6 10.9 %copy-start.16 = (bf16[2,272,512]{2,1,0:T(8,128)(2,1)S(1)}, bf16[2,272,512]{2,1,0:T(8,128)(2,1)}, u32[]{:S(2)}) copy-start(bf16[2,272,512]{2,1,0:T(8,128)(2,1)} %constant.47.clone) | copy-start | bytes 1671172
  3.4 58.7 %all-to-all-start = ((f32[16,8,2,8,128]{4,3,2,1,0:T(8,128)}), f32[16,8,2,8,128]{4,3,2,1,0:T(8,128)S(1)}, u32[]{:S(2)}, u32[]{:S(2)}) async-start(f32[16,8,2,8,128]{4,3,2,1,0:T(8,128)} %bitcast.17), calls=%async_computation | async-start | bytes 2097152 | tf_op jit(solution)/shard_map/all_to_all | solution.py:848
  54.5 7.5 %collective-permute-start.4 = (bf16[16,16,256]{2,1,0:T(8,128)(2,1)}, bf16[16,16,256]{2,1,0:T(8,128)(2,1)S(1)}, u32[]{:S(2)}, u32[]{:S(2)}) collective-permute-start(bf16[16,16,256]{2,1,0:T(8,128)(2,1)} %get-tuple-element.52), channel_id=1, source_target_pairs={{0,1},{1,0},{2,3},{3,2},{4,5},{5,4},{6,7},{7,6},{8,9},{9,8},{10,11... | collective-permute-start | bytes 393224 | tf_op jit(solution)/shard_map/ppermute | solution.py:854
  56.0 49.2 %collective-permute-start.3 = (bf16[256,16,128]{2,1,0:T(8,128)(2,1)}, bf16[256,16,128]{2,1,0:T(8,128)(2,1)S(1)}, u32[]{:S(2)}, u32[]{:S(2)}) collective-permute-start(bf16[256,16,128]{2,1,0:T(8,128)(2,1)} %get-tuple-element.51), channel_id=1, source_target_pairs={{0,1},{1,0},{2,3},{3,2},{4,5},{5,4},{6,7},{7,6},{8,9},{9,8},{10,11... | collective-permute-start | bytes 3145736 | tf_op jit(solution)/shard_map/ppermute | solution.py:852
  57.3 52.7 %collective-permute-start.5 = (bf16[2,16,256]{2,1,0:T(8,128)(2,1)S(1)}, bf16[2,16,256]{2,1,0:T(8,128)(2,1)S(1)}, u32[]{:S(2)}, u32[]{:S(2)}) collective-permute-start(bf16[2,16,256]{2,1,0:T(8,128)(2,1)S(1)} %slice.30), channel_id=1, source_target_pairs={{2,1},{3,0},{4,3},{5,2},{6,5},{7,4},{8,7},{9,6},{10,9},{11,8},{12,... | collective-permute-start | bytes 49160 | tf_op jit(solution)/shard_map/ppermute | solution.py:855
  62.0 42.6 %copy-start.14 = (bf16[16,16,256]{2,1,0:T(8,128)(2,1)}, bf16[16,16,256]{2,1,0:T(8,128)(2,1)S(1)}, u32[]{:S(2)}) copy-start(bf16[16,16,256]{2,1,0:T(8,128)(2,1)S(1)} %collective-permute-done.4) | copy-start | bytes 393220
  62.0 43.2 %copy-start.9 = (bf16[256,16,128]{2,1,0:T(8,128)(2,1)S(1)}, bf16[256,16,128]{2,1,0:T(8,128)(2,1)}, u32[]{:S(2)}) copy-start(bf16[256,16,128]{2,1,0:T(8,128)(2,1)} %get-tuple-element.50) | copy-start | bytes 3145732
  62.1 42.6 %copy-start.7 = (f32[16,8,2,8,128]{4,3,2,1,0:T(8,128)}, f32[16,8,2,8,128]{4,3,2,1,0:T(8,128)S(1)}, u32[]{:S(2)}) copy-start(f32[16,8,2,8,128]{4,3,2,1,0:T(8,128)S(1)} %all-to-all-done.gain) | copy-start | bytes 3145732
  104.7 5.2 %collective-permute-start = (bf16[16,16,256]{2,1,0:T(8,128)(2,1)}, bf16[16,16,256]{2,1,0:T(8,128)(2,1)S(1)}, u32[]{:S(2)}, u32[]{:S(2)}) collective-permute-start(bf16[16,16,256]{2,1,0:T(8,128)(2,1)} %get-tuple-element.45), channel_id=1, source_target_pairs={{0,1},{1,0},{2,3},{3,2},{4,5},{5,4},{6,7},{7,6},{8,9},{9,8},{10,11... | collective-permute-start | bytes 393224 | tf_op jit(solution)/shard_map/ppermute | solution.py:860
  105.3 15.4 %copy-start.19 = (s32[512,12]{0,1:T(8,128)S(1)}, s32[512,12]{0,1:T(8,128)}, u32[]{:S(2)}) copy-start(s32[512,12]{0,1:T(8,128)} %param.26) | copy-start | bytes 73732
  106.5 14.2 %copy-start.18 = (s32[512,12]{0,1:T(8,128)S(1)}, s32[512,12]{0,1:T(8,128)}, u32[]{:S(2)}) copy-start(s32[512,12]{0,1:T(8,128)} %param.27) | copy-start | bytes 73732
  106.5 14.2 %copy-start.20 = (f32[64]{0:T(128)S(1)}, f32[64]{0:T(128)}, u32[]{:S(2)}) copy-start(f32[64]{0:T(128)} %param.24) | copy-start | bytes 772
  106.5 14.6 %copy-start.17 = (s32[512,12]{0,1:T(8,128)S(1)}, s32[512,12]{0,1:T(8,128)}, u32[]{:S(2)}) copy-start(s32[512,12]{0,1:T(8,128)} %param.25) | copy-start | bytes 73732
  106.5 32.3 %copy-start.6 = (bf16[16,128]{1,0:T(8,128)(2,1)S(1)}, bf16[16,128]{1,0:T(8,128)(2,1)}, u32[]{:S(2)}) copy-start(bf16[16,128]{1,0:T(8,128)(2,1)} %constant.50.clone.place) | copy-start | bytes 12292
  110.0 51.6 %all-to-all-start.1 = ((bf16[16,2,8,16,128]{4,3,2,1,0:T(8,128)(2,1)}), bf16[16,2,8,16,128]{4,3,2,1,0:T(8,128)(2,1)S(1)}, u32[]{:S(2)}, u32[]{:S(2)}) async-start(bf16[16,2,8,16,128]{4,3,2,1,0:T(8,128)(2,1)} %bitcast.5), calls=%async_computation.1 | async-start | bytes 2097152 | tf_op jit(solution)/shard_map/all_to_all | solution.py:867
  115.0 45.3 %collective-permute-start.1 = (bf16[256,16,128]{2,1,0:T(8,128)(2,1)}, bf16[256,16,128]{2,1,0:T(8,128)(2,1)S(1)}, u32[]{:S(2)}, u32[]{:S(2)}) collective-permute-start(bf16[256,16,128]{2,1,0:T(8,128)(2,1)} %get-tuple-element.46), channel_id=1, source_target_pairs={{0,1},{1,0},{2,3},{3,2},{4,5},{5,4},{6,7},{7,6},{8,9},{9,8},{10,11... | collective-permute-start | bytes 3145736 | tf_op jit(solution)/shard_map/ppermute | solution.py:864
  116.6 22.2 %collective-permute-start.2 = (bf16[2,256,512]{2,1,0:T(8,128)(2,1)}, bf16[2,256,512]{2,1,0:T(8,128)(2,1)S(1)}, u32[]{:S(2)}, u32[]{:S(2)}) collective-permute-start(bf16[2,256,512]{2,1,0:T(8,128)(2,1)} %get-tuple-element.49), channel_id=1, source_target_pairs={{2,0},{4,2},{6,4},{8,6},{10,8},{12,10},{14,12},{16,14},{18,16},{20... | collective-permute-start | bytes 1572872 | tf_op jit(solution)/shard_map/ppermute | solution.py:853
  138.8 21.5 %copy-start.8 = (bf16[256,16,128]{2,1,0:T(8,128)(2,1)S(1)}, bf16[256,16,128]{2,1,0:T(8,128)(2,1)}, u32[]{:S(2)}) copy-start(bf16[256,16,128]{2,1,0:T(8,128)(2,1)} %get-tuple-element.57) | copy-start | bytes 3145732
  161.6 40.6 %copy-start.15 = (bf16[16,16,256]{2,1,0:T(8,128)(2,1)S(1)}, bf16[16,16,256]{2,1,0:T(8,128)(2,1)}, u32[]{:S(2)}) copy-start(bf16[16,16,256]{2,1,0:T(8,128)(2,1)} %copy-done.14) | copy-start | bytes 393220
  161.6 62.0 %all-to-all-start.2 = ((bf16[16,2,8,16,128]{4,3,2,1,0:T(8,128)(2,1)}), bf16[16,2,8,16,128]{4,3,2,1,0:T(8,128)(2,1)}, u32[]{:S(2)}, u32[]{:S(2)}) async-start(bf16[16,2,8,16,128]{4,3,2,1,0:T(8,128)(2,1)} %bitcast.6), calls=%async_computation.2 | async-start | bytes 2097152 | tf_op jit(solution)/shard_map/all_to_all | solution.py:870
  172.4 29.7 %collective-permute-start.6 = (bf16[2,256,512]{2,1,0:T(8,128)(2,1)}, bf16[2,256,512]{2,1,0:T(8,128)(2,1)S(1)}, u32[]{:S(2)}, u32[]{:S(2)}) collective-permute-start(bf16[2,256,512]{2,1,0:T(8,128)(2,1)} %get-tuple-element.59), channel_id=1, source_target_pairs={{0,2},{2,4},{4,6},{6,8},{8,10},{10,12},{12,14},{14,16},{16,18},{18... | collective-permute-start | bytes 1572872 | tf_op jit(solution)/shard_map/ppermute | solution.py:861
  173.5 28.6 %collective-permute-start.7 = (bf16[2,16,256]{2,1,0:T(8,128)(2,1)S(1)}, bf16[2,16,256]{2,1,0:T(8,128)(2,1)S(1)}, u32[]{:S(2)}, u32[]{:S(2)}) collective-permute-start(bf16[2,16,256]{2,1,0:T(8,128)(2,1)S(1)} %slice.31), channel_id=1, source_target_pairs={{0,3},{1,2},{2,5},{3,4},{4,7},{5,6},{6,9},{7,8},{8,11},{9,10},{10,... | collective-permute-start | bytes 49160 | tf_op jit(solution)/shard_map/ppermute | solution.py:862
  233.0 29.6 %all-to-all-start.3 = ((bf16[16,16,16,128]{3,2,1,0:T(8,128)(2,1)}), bf16[16,16,16,128]{3,2,1,0:T(8,128)(2,1)S(1)}, u32[]{:S(2)}, u32[]{:S(2)}) async-start(bf16[16,16,16,128]{3,2,1,0:T(8,128)(2,1)} %get-tuple-element.69), calls=%async_computation.3 | async-start | bytes 2097152 | tf_op jit(solution)/shard_map/all_to_all | solution.py:875
  250.6 18.8 %copy-start.11 = (f32[256,512]{1,0:T(8,128)S(1)}, f32[256,512]{1,0:T(8,128)}, u32[]{:S(2)}) copy-start(f32[256,512]{1,0:T(8,128)} %get-tuple-element.65) | copy-start | bytes 1572868
  250.6 20.0 %copy-start.10 = (f32[512,256]{1,0:T(8,128)S(1)}, f32[512,256]{1,0:T(8,128)}, u32[]{:S(2)}) copy-start(f32[512,256]{1,0:T(8,128)} %get-tuple-element.67) | copy-start | bytes 1572868
  262.5 29.8 %all-to-all-start.4 = ((bf16[16,16,16,128]{3,2,1,0:T(8,128)(2,1)}), bf16[16,16,16,128]{3,2,1,0:T(8,128)(2,1)S(1)}, u32[]{:S(2)}, u32[]{:S(2)}) async-start(bf16[16,16,16,128]{3,2,1,0:T(8,128)(2,1)} %get-tuple-element.74), calls=%async_computation.4 | async-start | bytes 2097152 | tf_op jit(solution)/shard_map/all_to_all | solution.py:879
  316.8 36.6 %copy-start.5 = (bf16[256,256]{1,0:T(8,128)(2,1)S(1)}, bf16[256,256]{1,0:T(8,128)(2,1)}, u32[]{:S(2)}) copy-start(bf16[256,256]{1,0:T(8,128)(2,1)} %wd.3) | copy-start | bytes 393220
  316.8 21.5 %all-to-all-start.7 = ((bf16[32,40,256]{2,1,0:T(8,128)(2,1)}), bf16[32,40,256]{2,1,0:T(8,128)(2,1)}, u32[]{:S(2)}, u32[]{:S(2)}) async-start(bf16[32,40,256]{2,1,0:T(8,128)(2,1)} %broadcast_in_dim.16), calls=%async_computation.7 | async-start | bytes 1310720 | tf_op jit(solution)/shard_map/all_to_all | solution.py:894
  320.5 32.8 %collective-permute-start.9 = (bf16[16,16,16,128]{3,2,1,0:T(8,128)(2,1)S(1)}, bf16[16,16,16,128]{3,2,1,0:T(8,128)(2,1)}, u32[]{:S(2)}, u32[]{:S(2)}) collective-permute-start(bf16[16,16,16,128]{3,2,1,0:T(8,128)(2,1)S(1)} %all-to-all-done.3.own), channel_id=1, source_target_pairs={{0,1},{1,0},{2,3},{3,2},{4,5},{5,4},{6,7},{7,6},{8,9},{9,8},{10,11... | collective-permute-start | bytes 3145736 | tf_op jit(solution)/shard_map/ppermute | solution.py:881
  322.3 52.9 %collective-permute-start.8 = (bf16[16,16,16,128]{3,2,1,0:T(8,128)(2,1)S(1)}, bf16[16,16,16,128]{3,2,1,0:T(8,128)(2,1)S(1)}, u32[]{:S(2)}, u32[]{:S(2)}) collective-permute-start(bf16[16,16,16,128]{3,2,1,0:T(8,128)(2,1)S(1)} %all-to-all-done.4.own), channel_id=1, source_target_pairs={{0,1},{1,0},{2,3},{3,2},{4,5},{5,4},{6,7},{7,6},{8,9},{9,8},{10,11... | collective-permute-start | bytes 3145736 | tf_op jit(solution)/shard_map/ppermute | solution.py:897
  338.3 50.6 %all-to-all-start.6 = ((f32[16,8,2,8,128]{4,3,2,1,0:T(8,128)}), f32[16,8,2,8,128]{4,3,2,1,0:T(8,128)}, u32[]{:S(2)}, u32[]{:S(2)}) async-start(f32[16,8,2,8,128]{4,3,2,1,0:T(8,128)} %copy-done.4), calls=%async_computation.6 | async-start | bytes 2097152 | tf_op jit(solution)/shard_map/all_to_all | solution.py:898
  (7 other events, 15.8 us)

commit v5 on v4

--- a/solution.py
+++ b/solution.py
@@ -344,10 +344,9 @@
 
 
 def mlp_kernel(
-    side, x_ref, ct_ref, win_t, win, wout, table,
+    side, x_ref, ct_ref, win_t, win, wout, table, earlier,
     gf_ref, own_ref, send_ref, edge_ref, halo_ref, gin_ref, gout_ref,
-    stage, xs, cs, low, high,
-    *, steps, width, chunk, halo,
+    stage, xs, cs, low, high, *slots, steps, width, chunk, halo,
 ):
     step = pl.program_id(0)
 
@@ -361,25 +360,51 @@
     column = pl.multiple_of(step * width, width)
     per = chunk // width
 
-    def body(index, carry):
-        cells = pl.ds(pl.multiple_of(index * chunk, chunk), chunk)
-        x = xs[:, cells]
-        c = cs[:, cells]
-        pre = mm(win_t[...], x)
-        grad = mm(wout[...], c)
+    even, odd = slots[:4], slots[4:]
+
+    def cells(index):
+        return pl.ds(pl.multiple_of(index * chunk, chunk), chunk)
+
+    def project(index, slot):
+        slot[0][...] = mm(win_t[...], xs[:, cells(index)])
+        slot[1][...] = mm(wout[...], cs[:, cells(index)])
+
+    def activate(slot):
+        pre = slot[0][...]
         chance, decay = gelu_both(pre)
-        act = (pre * chance).astype(jnp.bfloat16)
-        gp = (grad * (chance + pre * decay * (1.0 / root_two_pi))).astype(jnp.bfloat16)
+        slot[2][...] = (pre * chance).astype(jnp.bfloat16)
+        slope = chance + pre * decay * (1.0 / root_two_pi)
+        slot[3][...] = (slot[1][...] * slope).astype(jnp.bfloat16)
+
+    def reduce(index, slot):
+        gp = slot[3][...]
         gf = mm(win[...], gp).astype(jnp.bfloat16)
         for part in range(per):
             gf_ref[index * per + part, :, pl.ds(column, width)] = gf[
                 :, part * width : (part + 1) * width
             ]
-        gin_ref[...] += mm_nt(x, gp)
-        gout_ref[...] += mm_nt(act, c)
+        gin_ref[...] += mm_nt(xs[:, cells(index)], gp)
+        gout_ref[...] += mm_nt(slot[2][...], cs[:, cells(index)])
+
+    chunks = BAND * width // chunk
+    project(0, even)
+    activate(even)
+    project(1, odd)
+
+    def body(pair, carry):
+        index = 2 * pair
+        reduce(index, even)
+        activate(odd)
+        project(index + 2, even)
+        reduce(index + 1, odd)
+        activate(even)
+        project(index + 3, odd)
         return carry
 
-    lax.fori_loop(0, BAND * width // chunk, body, 0, unroll=2)
+    lax.fori_loop(0, chunks // 2 - 1, body, 0)
+    reduce(chunks - 2, even)
+    activate(odd)
+    reduce(chunks - 1, odd)
 
     @pl.when(step == steps - 1)
     def _():
@@ -408,12 +433,12 @@
             send_ref[...] = low[...].astype(jnp.bfloat16).reshape(shape)
 
 
-def mlp_call(band, side, filtered, cotangent, win_t, win, wout, table):
+def mlp_call(band, side, filtered, cotangent, win_t, win, wout, table, earlier):
     channels, rows, columns = filtered.shape
     hidden = wout.shape[0]
-    width = LANES
+    width = 2 * LANES
     steps = columns // width
-    chunk = 4 * width
+    chunk = 2 * width
     orders = table.shape[0] - 16
     block = pl.BlockSpec((channels, BAND, width), lambda i: (0, band, i))
     cells = BAND * columns
@@ -430,6 +455,7 @@
             whole_block(win.shape),
             whole_block(wout.shape),
             whole_block(table.shape),
+            pl.BlockSpec(memory_space=pl.ANY),
         ],
         out_specs=[
             whole_block((BAND, channels, columns)),
@@ -455,18 +481,22 @@
             pltpu.VMEM((channels, BAND * width), jnp.bfloat16),
             pltpu.VMEM((orders * BAND, LANES), jnp.float32),
             pltpu.VMEM((orders * BAND, LANES), jnp.float32),
-        ],
-        compiler_params=params(56),
+        ]
+        + [
+            pltpu.VMEM((hidden, chunk), kind)
+            for kind in (jnp.float32, jnp.float32, jnp.bfloat16, jnp.bfloat16) * 2
+        ],
+        compiler_params=params(60),
         cost_estimate=pl.CostEstimate(
             flops=2 * cells * channels * (5 * hidden + orders),
             bytes_accessed=6 * channels * cells,
             transcendentals=2 * hidden * cells,
         ),
         name="mlp",
-    )(side, filtered, cotangent, win_t, win, wout, table)
-
-
-def stencil_kernel(taps, before, rows, after, edges, place, q_ref, field, rim, *, first):
+    )(side, filtered, cotangent, win_t, win, wout, table, earlier)
+
+
+def stencil_kernel(taps, before, rows, after, edges, place, earlier, q_ref, field, rim, *, first):
     channels, columns = field.shape[1:]
     field[0:REACH] = before[...]
     field[REACH : REACH + BAND] = rows[...]
@@ -520,7 +550,7 @@
     lax.fori_loop(0, BAND, row_body, 0)
 
 
-def stencil_call(band, taps, before, rows, after, edges, place):
+def stencil_call(band, taps, before, rows, after, edges, place, earlier):
     _, channels, columns = rows.shape
 
     def pair(index):
@@ -536,6 +566,7 @@
             pair(after[1]),
             whole_block(edges.shape),
             whole_block(place.shape),
+            pl.BlockSpec(memory_space=pl.ANY),
         ],
         out_specs=whole_block(rows.shape),
         out_shape=jax.ShapeDtypeStruct(rows.shape, jnp.bfloat16),
@@ -550,7 +581,7 @@
             transcendentals=0,
         ),
         name="stencil",
-    )(taps, before[0], rows, after[0], edges, place)
+    )(taps, before[0], rows, after[0], edges, place, earlier)
 
 
 def disco_kernel_grad(bi_ref, q_ref, gd_ref, stage, flat):
@@ -591,21 +622,22 @@
     )(block_input, q)
 
 
-def legendre_kernel(leg, r0, r1, gain, owned_ref, s0, s1, stage, *, steps, block):
+def legendre_kernel(leg, p0, t0, p1, t1, gain, s0, s1, stage, *, steps, block):
     order = pl.program_id(0)
     degrees = leg.shape[1]
     half = leg.shape[2] // 2
     total = None
-    for band, ref in enumerate((r0, r1)):
-        pair = jnp.concatenate(
-            [ref[:, r].reshape(half, LANES) for r in range(2)], axis=1
-        )
+    for band, refs in enumerate(((p0, t0), (p1, t1))):
+        pair = jnp.concatenate([ref[...].reshape(half, LANES) for ref in refs], axis=1)
         term = mm(leg[0, :, band * half : (band + 1) * half], pair)
         total = term if total is None else total + term
     real = total[:, :LANES]
     imag = total[:, LANES:]
-    owned_ref[:, 0, 0] = real.reshape(owned_ref.shape[0], -1, LANES)
-    owned_ref[:, 0, 1] = imag.reshape(owned_ref.shape[0], -1, LANES)
+    owners, band = s0.shape[:2]
+    shape = (owners, -1, LANES)
+    s1[:, band + order] = jnp.concatenate(
+        [real.reshape(shape), imag.reshape(shape)], axis=1
+    ).astype(jnp.bfloat16)
     g = gain[:, 0, 0].reshape(degrees, LANES)
     k = gain[:, 0, 1].reshape(degrees, LANES)
     scaled = jnp.concatenate([g * real + k * imag, g * imag - k * real], axis=1).astype(
@@ -620,31 +652,34 @@
     @pl.when(order == steps - 1)
     def _():
         s0[...] = stage[: half * block].astype(jnp.bfloat16).reshape(s0.shape)
-        s1[...] = stage[half * block :].astype(jnp.bfloat16).reshape(s1.shape)
+        s1[:, :band] = stage[half * block :].astype(jnp.bfloat16).reshape(s0.shape)
 
 
 def legendre_call(leg, r0, r1, gain):
-    owners, _, steps, band, lanes = r0.shape
+    owners, block, band, lanes = r0.shape
     degrees = leg.shape[1]
-    block = 2 * steps
-    r_spec = pl.BlockSpec((owners, 2, None, band, lanes), lambda m: (0, 0, m, 0, 0))
+    steps = block // 2
+    real = pl.BlockSpec((owners, None, band, lanes), lambda m: (0, m, 0, 0))
+    imag = pl.BlockSpec((owners, None, band, lanes), lambda m: (0, m + steps, 0, 0))
     g_shape = (owners, 1, 2, degrees // owners, lanes)
     g_spec = pl.BlockSpec(g_shape, lambda m: (0, m, 0, 0, 0))
     out = (owners, band, block, lanes)
+    more = (owners, band + steps + 1, block, lanes)
     return pl.pallas_call(
         functools.partial(legendre_kernel, steps=steps, block=block),
         grid=(steps,),
         in_specs=[
             pl.BlockSpec((1, degrees, leg.shape[2]), lambda m: (m, 0, 0)),
-            r_spec,
-            r_spec,
+            real,
+            imag,
+            real,
+            imag,
             g_spec,
         ],
-        out_specs=[g_spec, whole_block(out), whole_block(out)],
+        out_specs=[whole_block(out), whole_block(more)],
         out_shape=[
-            jax.ShapeDtypeStruct(gain.shape, jnp.float32),
             jax.ShapeDtypeStruct(out, jnp.bfloat16),
-            jax.ShapeDtypeStruct(out, jnp.bfloat16),
+            jax.ShapeDtypeStruct(more, jnp.bfloat16),
         ],
         scratch_shapes=[pltpu.VMEM((2 * owners * band * block, lanes), jnp.float32)],
         compiler_params=params(48),
@@ -654,7 +689,86 @@
             transcendentals=0,
         ),
         name="legendre",
-    )(leg, r0, r1, gain)
+    )(leg, r0, r0, r1, r1, gain)
+
+
+def pair_sum_kernel(kept, arrived, *rest):
+    out = rest[-1]
+    block = kept.shape[0] // out.shape[0]
+    total = kept[...].astype(jnp.float32) + arrived[...].astype(jnp.float32)
+    out[:, :block] = total.astype(jnp.bfloat16).reshape(-1, block, *kept.shape[1:])
+    if out.shape[1] > block:
+        total = rest[0][...].astype(jnp.float32) + rest[1][...].astype(jnp.float32)
+        out[:, block:] = total.astype(jnp.bfloat16)
+
+
+def pair_sum_call(owners, kept, arrived, more, earlier):
+    orders, band, lanes = kept.shape
+    extra = more[0].shape[1] if more else 0
+    shape = (owners, orders // owners + extra, band, lanes)
+    return pl.pallas_call(
+        pair_sum_kernel,
+        grid=(1,),
+        in_specs=[whole_block(array.shape) for array in (kept, arrived, *more)]
+        + [pl.BlockSpec(memory_space=pl.ANY)] * len(earlier),
+        out_specs=whole_block(shape),
+        out_shape=jax.ShapeDtypeStruct(shape, jnp.bfloat16),
+        compiler_params=params(32),
+        name="pair_sum",
+    )(kept, arrived, *more, *earlier)
+
+
+def share_kernel(kept, arrived, before, out):
+    total = kept[...].astype(jnp.float32) + arrived[...].astype(jnp.float32)
+    out[...] = total.astype(jnp.bfloat16).reshape(out.shape)
+
+
+def share_call(kept, arrived, parcel):
+    owners, blocks, band, lanes = parcel.shape
+    return pl.pallas_call(
+        share_kernel,
+        grid=(1,),
+        in_specs=[whole_block(kept.shape)] * 2 + [pl.BlockSpec(memory_space=pl.ANY)],
+        out_specs=pl.BlockSpec((owners, 1, band, lanes), lambda i: (0, blocks - 1, 0, 0)),
+        out_shape=jax.ShapeDtypeStruct(parcel.shape, jnp.bfloat16),
+        input_output_aliases={2: 0},
+        name="share",
+    )(kept, arrived, parcel)
+
+
+def split_kernel(parcel, shares, earlier, synth, owned, totals):
+    band = synth.shape[1]
+    degrees = owned.shape[1]
+    synth[...] = parcel[:, :band]
+    owned[...] = parcel[:, band : band + degrees].astype(jnp.float32)
+    blocks = totals.shape[1] - 1
+    first = shares[...].astype(jnp.float32).sum(axis=0).astype(jnp.bfloat16)
+    last = parcel[:, band + degrees :].astype(jnp.float32).sum(axis=0).astype(jnp.bfloat16)
+    totals[:, :blocks] = jnp.broadcast_to(first[None], (totals.shape[0],) + first.shape)
+    totals[:, blocks:] = jnp.broadcast_to(last[None], (totals.shape[0],) + last.shape)
+
+
+def split_call(count, degrees, parcel, shares, earlier):
+    owners, blocks, band, lanes = parcel.shape
+    more = shares.shape[1] - band
+    shapes = (
+        ((owners, band, band, lanes), jnp.bfloat16),
+        ((owners, degrees, band, lanes), jnp.float32),
+        ((count, more + 1, band, lanes), jnp.bfloat16),
+    )
+    return pl.pallas_call(
+        split_kernel,
+        grid=(1,),
+        in_specs=[
+            whole_block(parcel.shape),
+            pl.BlockSpec((owners, more, band, lanes), lambda i: (0, band // more, 0, 0)),
+            pl.BlockSpec(memory_space=pl.ANY),
+        ],
+        out_specs=[whole_block(shape) for shape, _ in shapes],
+        out_shape=[jax.ShapeDtypeStruct(shape, kind) for shape, kind in shapes],
+        compiler_params=params(32),
+        name="split",
+    )(parcel, shares, earlier)
 
 
 def final_kernel(side, q_ref, own, other, table, wd, *rest):
@@ -695,7 +809,7 @@
         in_specs=[
             pl.BlockSpec(memory_space=pltpu.SMEM),
             pl.BlockSpec((BAND, channels, width), lambda i: (0, 0, i)),
-            whole_block(own.shape),
+            whole_block(other.shape),
             whole_block(other.shape),
             pl.BlockSpec((table.shape[0], width), lambda i: (0, i)),
             whole_block(wd.shape),
@@ -840,65 +954,57 @@
             (a * lon_count + i, b * lon_count + j) for a, b in moves for i, j in swap
         ]
 
-    def summed(kept, arrived):
-        total = (kept.astype(jnp.float32) + arrived.astype(jnp.float32)).astype(jnp.bfloat16)
-        return total.reshape(lat_count, 2, own, BAND, LANES)
+    def dealt(array):
+        blocks = array.astype(jnp.bfloat16).reshape(lat_count, lon_count, -1, BAND, LANES)
+        half = functools.partial(lax.dynamic_index_in_dim, blocks, axis=1, keepdims=False)
+        return half(lon_index), lax.ppermute(half(1 - lon_index), "lon", swap)
 
     gain = gain_call(spectral_gain).reshape(lat_count, own, 2, degrees, LANES)
+    gf0, kept0, sent0, ends0, head, gin0, gout0 = mlp_call(
+        0, side, filtered, cotangent, w_in_t, w_in, w_out, forward, gain
+    )
     gain = exchange(gain)
-    gf0, kept0, sent0, ends0, head, gin0, gout0 = mlp_call(
-        0, side, filtered, cotangent, w_in_t, w_in, w_out, forward
-    )
     arrived0 = lax.ppermute(sent0, "lon", swap)
     bottom = lax.ppermute(head, "lat", up)
     sides0 = lax.ppermute(ends0, "lon", swap)
     bottom_side = lax.ppermute(ends0[:REACH], ("lat", "lon"), across(up))
-    gain, w_in_t = lax.optimization_barrier((gain, w_in_t))
     gf1, kept1, sent1, ends1, tail, gin1, gout1 = mlp_call(
-        1, side, filtered, cotangent, w_in_t, w_in, w_out, forward
+        1, side, filtered, cotangent, w_in_t, w_in, w_out, forward, gain
     )
     sides1 = lax.ppermute(ends1, "lon", swap)
     top = lax.ppermute(tail, "lat", down)
     top_side = lax.ppermute(ends1[BAND - REACH :], ("lat", "lon"), across(down))
-    sent1, sides1 = lax.optimization_barrier((sent1, sides1))
     arrived1 = lax.ppermute(sent1, "lon", swap)
-    edges1 = jnp.concatenate([sides0[BAND - REACH :], sides1, bottom_side], axis=0)
-    sum0, edges1 = lax.optimization_barrier((summed(kept0, arrived0), edges1))
-    received0 = exchange(sum0)
-    q1 = stencil_call(1, taps, (gf0, BAND // REACH - 1), gf1, (bottom, 0), edges1, place)
-    arrived1, q1 = lax.optimization_barrier((arrived1, q1))
-    received1 = exchange(summed(kept1, arrived1))
-    edges0 = jnp.concatenate([top_side, sides0, sides1[:REACH]], axis=0)
-    q0 = stencil_call(0, taps, (top, 0), gf0, (gf1, 0), edges0, place)
-    received0, received1, q0 = lax.optimization_barrier((received0, received1, q0))
-    owned, s0, s1 = legendre_call(legendre, received0, received1, gain)
-    local0 = exchange(s0)
-    q1, owned = lax.optimization_barrier((q1, owned))
-    disco1 = disco_grad_call(1, block_input, q1)
-    local0, disco1, s1, q0 = lax.optimization_barrier((local0, disco1, s1, q0))
-    local1 = exchange(s1)
-    disco0 = disco_grad_call(0, block_input, q0)
-    other0 = lax.ppermute(local0, "lon", swap)
-    everyone = functools.partial(
-        lax.all_to_all, axis_name=("lat", "lon"), split_axis=0, concat_axis=0, tiled=True
-    )
-    count = lat_count * lon_count
     half = w_in.shape[1] // 2
     gin = gin0 + gin1
-    parts = (gin[:, :half], gin[:, half:], gout0 + gout1, disco0 + disco1)
-    stacked = jnp.concatenate(parts, axis=0).astype(jnp.bfloat16)
-    stacked, local1 = lax.optimization_barrier((stacked, local1))
-    shares = everyone(stacked.reshape(count, -1, channels)).astype(jnp.float32).sum(axis=0)
-    shares = jnp.broadcast_to(shares.astype(jnp.bfloat16)[None], (count,) + shares.shape)
-    shares, owned = lax.optimization_barrier((shares, owned))
-    totals = everyone(shares).reshape(-1, channels).astype(jnp.float32)
+    weights = jnp.concatenate([gin[:, :half], gin[:, half:], gout0 + gout1], axis=0)
+    sum0 = pair_sum_call(
+        lat_count, kept0, arrived0, (), (bottom, bottom_side, sides0, top, top_side)
+    )
+    received0 = exchange(sum0)
+    edges1 = jnp.concatenate([sides0[BAND - REACH :], sides1, bottom_side], axis=0)
+    q1 = stencil_call(1, taps, (gf0, BAND // REACH - 1), gf1, (bottom, 0), edges1, place, sum0)
+    received1 = exchange(pair_sum_call(lat_count, kept1, arrived1, dealt(weights), (q1,)))
+    edges0 = jnp.concatenate([top_side, sides0, sides1[:REACH]], axis=0)
+    q0 = stencil_call(0, taps, (top, 0), gf0, (gf1, 0), edges0, place, q1)
+    disco1 = disco_grad_call(1, block_input, q1)
+    disco0 = disco_grad_call(0, block_input, q0)
+    s0, s1 = legendre_call(legendre, received0, received1, gain)
+    local0 = exchange(s0)
+    other0 = lax.ppermute(local0, "lon", swap)
+    parcel = exchange(share_call(*dealt(disco0 + disco1), s1))
+    result = final_call(0, rows, side, q0, local0, other0, inverse, w_disco, None)
+    count = lat_count * lon_count
+    synth1, owned, totals = split_call(count, degrees, parcel, received1, result)
+    other1 = lax.ppermute(synth1, "lon", swap)
+    totals = lax.all_to_all(totals, ("lat", "lon"), split_axis=0, concat_axis=0, tiled=True)
+    grad_gain = grad_gain_call(owned.reshape(M * 2 * degrees, LANES), spectral_saved)
+    result = final_call(1, rows, side, q1, synth1, other1, inverse, w_disco, result)
+    totals = totals.astype(jnp.float32)
+    total_disco = totals[:, -1].reshape(channels, channels)
+    totals = totals[:, :-1].reshape(-1, channels)
     total_in = jnp.concatenate([totals[:channels], totals[channels : 2 * channels]], axis=1)
-    total_out, total_disco = jnp.split(totals[2 * channels :], (2 * half,), axis=0)
-    other1 = lax.ppermute(local1, "lon", swap)
-    owned = exchange(owned).reshape(M * 2 * degrees, LANES)
-    result = final_call(0, rows, side, q0, local0, other0, inverse, w_disco, None)
-    result = final_call(1, rows, side, q1, local1, other1, inverse, w_disco, result)
-    grad_gain = grad_gain_call(owned, spectral_saved)
+    total_out = totals[2 * channels :]
     scale = 1.0 / math.sqrt(NLAT * NLON)
     return (result, grad_gain, total_in * scale, total_out * scale, total_disco * scale)
 

time: 393 us -> 379 us (0.964)
  blocking collectives: 23.5 us -> 0 us
  Pallas kernels: 176 us -> 185 us
  waiting for transfers between devices: 104 us -> 97.2 us
  local copies, waits for them, and re-layouts: 16.1 us -> 22.4 us
  other arithmetic: 8.27 us -> 4.04 us
    ppermute x1 -> x3, waiting for transfers between devices: 11.5 us -> 38.3 us  [the longest x1 27.6 us: shards_banded(): other1 = lax.ppermute(synth1, 'lon', swap)]
    all_to_all x1 -> x0, blocking collectives: 23.5 us -> none  [shards_banded(): everyone(stacked.reshape(count, -1, channels)).astype(jnp.float32)]
    ppermute x1, waiting for transfers between devices: 24.5 us -> 6.72 us  [shards_banded(): top_side = lax.ppermute(ends1[BAND - REACH:], ('lat', 'lon'), across(down))]
    ppermute x1, waiting for transfers between devices: 17 us -> 0.01 us  [shards_banded(): bottom = lax.ppermute(head, 'lat', up)]
    ppermute x1, waiting for transfers between devices: 9.7 us -> 24.3 us  [shards_banded(): other0 = lax.ppermute(local0, 'lon', swap)]
    all_to_all x1, waiting for transfers between devices: 11.9 us -> 0.01 us  [shards_banded(): local0 = exchange(s0)]
    all_to_all x1, starting transfers between devices: 5.03 us -> 15.1 us  [shards_banded(): received0 = exchange(sum0)]
    all_to_all x4 -> x3, starting transfers between devices: 25.8 us -> 17.2 us  [the longest x1 6.22 us: shards_banded(): parcel = exchange(share_call(*dealt(disco0 + disco1), s1))]
  transfers between devices with their start and end apart: 17 -> 18, of which waited for: 8 -> 8; matrix products, arithmetic and copies ran while one was open for 4% -> 3% of each run, Pallas kernels for 41% -> 46%
where the time goes in v5:
time: 379 us; the launch traced here: 375 us
  Pallas kernels  185 us (49%)
  waiting for transfers between devices  97.2 us (26%)
  starting transfers between devices  65.3 us (17%)
  local copies, waits for them, and re-layouts  22.4 us (6%)
  other arithmetic  4.04 us (1%)
    pallas_call x2, Pallas kernels, mlp_call(): pl.pallas_call(functools.partial(mlp_kernel, steps=steps, width=width, ch...  88.4 us
    pallas_call x2, Pallas kernels, stencil_call(): pl.pallas_call(functools.partial(stencil_kernel, first=band * BAND), grid...  39 us
    ppermute x1, waiting for transfers between devices, shards_banded(): other1 = lax.ppermute(synth1, 'lon', swap)  27.6 us
    all_to_all x1, waiting for transfers between devices, shards_banded(): exchange(pair_sum_call(lat_count, kept1, arrived1, dealt(weights), (q1,)))  26.1 us
    ppermute x1, waiting for transfers between devices, shards_banded(): other0 = lax.ppermute(local0, 'lon', swap)  24.3 us
    pallas_call x2, Pallas kernels, final_call(): pl.pallas_call(final_kernel, grid=(columns // width,), in_specs=[pl.Block...  20.6 us
    pallas_call x2, Pallas kernels, disco_grad_call(): pl.pallas_call(disco_kernel_grad, grid=(1,), in_specs=[pl.BlockSpec((chan...  19.1 us
    all_to_all x1, starting transfers between devices, shards_banded(): received0 = exchange(sum0)  15.1 us
  transfers between devices with their start and end apart: 18, of which 8 were waited for; matrix products, arithmetic and copies ran while one was open for 3% of the time, Pallas kernels for 46%

profile of v5, /device:TPU:0, one launch (start us, length us, event | category | flops | bytes accessed | tf_op | source)
XLA Modules:
  0.0 375.3 jit_solution(4107878813614604318)
XLA Ops:
  0.6 2.7 gain.1
  3.3 7.5 %all-to-all-start = ((f32[16,8,2,8,128]{4,3,2,1,0:T(8,128)}), f32[16,8,2,8,128]{4,3,2,1,0:T(8,128)S(1)}, u32[]{:S(2)}, u32[]{:S(2)}) async-start(f32[16,8,2,8,128]{4,3,2,1,0:T(8,128)} %bitcast.36), calls=%async_computation | async-start | bytes 2097152 | tf_op jit(solution)/shard_map/all_to_all | solution.py:966
  12.4 44.2 %mlp.2 = (bf16[16,256,512]{2,1,0:T(8,128)(2,1)}, bf16[256,16,128]{2,1,0:T(8,128)(2,1)}, bf16[256,16,128]{2,1,0:T(8,128)(2,1)}, bf16[16,16,256]{2,1,0:T(8,128)(2,...) custom-call(s32[1]{0:T(128)} %bitcast.side, bf16[256,32,512]{2,1,0:T(8,128)(2,1)} %x_ref.3, ...), custom_call_target="tpu_custom_call" | custom-call | flops 11811160064 | bytes 12582912 | tf_op jit(solution)/shard_map/mlp/pallas_call | solution.py:445
  56.6 4.6 %collective-permute-start = (bf16[2,256,512]{2,1,0:T(8,128)(2,1)}, bf16[2,256,512]{2,1,0:T(8,128)(2,1)S(1)}, u32[]{:S(2)}, u32[]{:S(2)}) collective-permute-start(bf16[2,256,512]{2,1,0:T(8,128)(2,1)} %get-tuple-element.26), channel_id=1, source_target_pairs={{2,0},{4,2},{6,4},{8,6},{10,8},{12,10},{14,12},{16,14},{18,16},{20... | collective-permute-start | bytes 1572872 | tf_op jit(solution)/shard_map/ppermute | solution.py:968
  61.3 1.5 collective-permute-start.4
  63.7 44.2 %mlp.3 = (bf16[16,256,512]{2,1,0:T(8,128)(2,1)}, bf16[256,16,128]{2,1,0:T(8,128)(2,1)}, bf16[256,16,128]{2,1,0:T(8,128)(2,1)}, bf16[16,16,256]{2,1,0:T(8,128)(2,...) custom-call(s32[1]{0:T(128)} %bitcast.side, bf16[256,32,512]{2,1,0:T(8,128)(2,1)} %x_ref.3, ...), custom_call_target="tpu_custom_call" | custom-call | flops 11811160064 | bytes 12582912 | tf_op jit(solution)/shard_map/mlp/pallas_call | solution.py:445
  108.5 5.0 %collective-permute-start.3 = (bf16[2,16,256]{2,1,0:T(8,128)(2,1)S(1)}, bf16[2,16,256]{2,1,0:T(8,128)(2,1)S(1)}, u32[]{:S(2)}, u32[]{:S(2)}) collective-permute-start(bf16[2,16,256]{2,1,0:T(8,128)(2,1)S(1)} %slice.44), channel_id=1, source_target_pairs={{2,1},{3,0},{4,3},{5,2},{6,5},{7,4},{8,7},{9,6},{10,9},{11,8},{12,... | collective-permute-start | bytes 49160 | tf_op jit(solution)/shard_map/ppermute | solution.py:970
  115.0 6.7 %collective-permute-done.6.rest_4_ = bf16[2,16,256]{2,1,0:T(8,128)(2,1)S(1)} collective-permute-done((bf16[2,16,256]{2,1,0:T(8,128)(2,1)S(1)}, bf16[2,16,256]{2,1,0:T(8,128)(2,1)S(1)}, u32[]{:S(2)}, u32[]{:S(2)}) %collective-permute-start.6) | collective-permute-done | bytes 16416 | tf_op jit(solution)/shard_map/ppermute | solution.py:976
  121.8 2.6 pair_sum.2.earlier
  124.4 15.1 %all-to-all-start.1 = ((bf16[16,16,16,128]{3,2,1,0:T(8,128)(2,1)}), bf16[16,16,16,128]{3,2,1,0:T(8,128)(2,1)S(1)}, u32[]{:S(2)}, u32[]{:S(2)}) async-start(bf16[16,16,16,128]{3,2,1,0:T(8,128)(2,1)} %pair_sum.2.earlier), calls=%async_computation.1 | async-start | bytes 2097152 | tf_op jit(solution)/shard_map/all_to_all | solution.py:984
  147.8 19.5 %stencil.2.earlier.q_ref.rest_2_ = bf16[16,256,512]{2,1,0:T(8,128)(2,1)S(1)} custom-call(f32[900]{0:T(1024)S(1)} %reshape.62.taps, bf16[16,256,512]{2,1,0:T(8,128)(2,1)} %get-tuple-element.24.before.rows, bf16[16,256,512]{2,1,0:T(8,128)(2,1)} %get-tuple-element.25.rows.after, bf16[2,256,512]{2,1,0:T(8,128)(2,1)S(1)} %collective-permute-done.rest_0_.after, ...), custom_call_target="tpu_custom_call" | custom-call | flops 125829120 | bytes 8388608 | tf_op jit(solution)/shard_map/stencil/pallas_call | solution.py:559
  167.3 6.9 %collective-permute-done.9.rest_1_ = bf16[16,4,16,128]{3,2,1,0:T(8,128)(2,1)S(1)} collective-permute-done((bf16[16,4,16,128]{3,2,1,0:T(8,128)(2,1)}, bf16[16,4,16,128]{3,2,1,0:T(8,128)(2,1)S(1)}, u32[]{:S(2)}, u32[]{:S(2)}) %collective-permute-start.9) | collective-permute-done | bytes 262176 | tf_op jit(solution)/shard_map/ppermute | solution.py:960
  174.2 1.5 pair_sum.3
  175.7 2.0 copy-done
  178.8 5.8 %all-to-all-start.2 = ((bf16[16,20,16,128]{3,2,1,0:T(8,128)(2,1)}), bf16[16,20,16,128]{3,2,1,0:T(8,128)(2,1)S(1)}, u32[]{:S(2)}, u32[]{:S(2)}) async-start(bf16[16,20,16,128]{3,2,1,0:T(8,128)(2,1)} %copy-done.4), calls=%async_computation.2 | async-start | bytes 2621440 | tf_op jit(solution)/shard_map/all_to_all | solution.py:987
  185.9 26.1 %all-to-all-done.2.p1.t1.shares = bf16[16,20,16,128]{3,2,1,0:T(8,128)(2,1)S(1)} async-done(((bf16[16,20,16,128]{3,2,1,0:T(8,128)(2,1)}), bf16[16,20,16,128]{3,2,1,0:T(8,128)(2,1)S(1)}, u32[]{:S(2)}, u32[]{:S(2)}) %all-to-all-start.2) | async-done | bytes 1310752 | tf_op jit(solution)/shard_map/all_to_all | solution.py:987
  213.2 6.2 %legendre.1 = (bf16[16,16,16,128]{3,2,1,0:T(8,128)(2,1)S(1)}, bf16[16,25,16,128]{3,2,1,0:T(8,128)(2,1)}) custom-call(bf16[8,128,512]{2,1,0:T(8,128)(2,1)S(1)} %constant_dynamic-slice_fusion.leg, bf16[16,16,16,128]{3,2,1,0:T(8,128)(2,1)S(1)} %all-to-all-done.1.p0.t0, bf16[16,16,16,128]{3,2,1,0:T(8,128)(2,1)S(1)} %all-to-all-done.1.p0.t0, ...), custom_call_target="tpu_custom_call" | custom-call | flops 1073741824 | bytes 7340032 | tf_op jit(solution)/shard_map/legendre/pallas_call | solution.py:668
  220.4 8.2 %all-to-all-start.4 = ((bf16[16,16,16,128]{3,2,1,0:T(8,128)(2,1)}), bf16[16,16,16,128]{3,2,1,0:T(8,128)(2,1)}, u32[]{:S(2)}, u32[]{:S(2)}) async-start(bf16[16,16,16,128]{3,2,1,0:T(8,128)(2,1)} %copy-done.12), calls=%async_computation.4 | async-start | bytes 2097152 | tf_op jit(solution)/shard_map/all_to_all | solution.py:993
  229.4 19.5 %stencil.3.q_ref = bf16[16,256,512]{2,1,0:T(8,128)(2,1)S(1)} custom-call(f32[900]{0:T(1024)S(1)} %reshape.62.taps, bf16[2,256,512]{2,1,0:T(8,128)(2,1)S(1)} %copy-done.8, bf16[16,256,512]{2,1,0:T(8,128)(2,1)} %get-tuple-element.24.before.rows, bf16[16,256,512]{2,1,0:T(8,128)(2,1)} %get-tuple-element.25.rows.after, ...), custom_call_target="tpu_custom_call" | custom-call | flops 125829120 | bytes 8388608 | tf_op jit(solution)/shard_map/stencil/pallas_call | solution.py:559
  249.0 10.3 %disco_weight.3 = f32[256,256]{1,0:T(8,128)S(1)} custom-call(bf16[256,32,512]{2,1,0:T(8,128)(2,1)} %bi_ref.3, bf16[16,256,512]{2,1,0:T(8,128)(2,1)S(1)} %copy-done.1), custom_call_target="tpu_custom_call" | custom-call | flops 1073741824 | bytes 8388608 | tf_op jit(solution)/shard_map/disco_weight/pallas_call | solution.py:602
  259.3 8.8 %disco_weight.2 = f32[256,256]{1,0:T(8,128)S(1)} custom-call(bf16[256,32,512]{2,1,0:T(8,128)(2,1)} %bi_ref.3, bf16[16,256,512]{2,1,0:T(8,128)(2,1)S(1)} %stencil.3.q_ref), custom_call_target="tpu_custom_call" | custom-call | flops 1073741824 | bytes 8388608 | tf_op jit(solution)/shard_map/disco_weight/pallas_call | solution.py:602
  269.4 3.8 %collective-permute-done.7.arrived = bf16[16,1,16,128]{3,2,1,0:T(8,128)(2,1)S(1)} collective-permute-done((bf16[16,1,16,128]{3,2,1,0:T(8,128)(2,1)S(1)}, bf16[16,1,16,128]{3,2,1,0:T(8,128)(2,1)S(1)}, u32[]{:S(2)}, u32[]{:S(2)}) %collective-permute-start.7) | collective-permute-done | bytes 65568 | tf_op jit(solution)/shard_map/ppermute | solution.py:960
  273.9 1.5 share.1
  275.4 6.2 %all-to-all-start.3 = ((bf16[16,25,16,128]{3,2,1,0:T(8,128)(2,1)}), bf16[16,25,16,128]{3,2,1,0:T(8,128)(2,1)S(1)}, u32[]{:S(2)}, u32[]{:S(2)}) async-start(bf16[16,25,16,128]{3,2,1,0:T(8,128)(2,1)} %share.1), calls=%async_computation.3 | async-start | bytes 3276800 | tf_op jit(solution)/shard_map/all_to_all | solution.py:995
  283.2 24.3 %collective-permute-done.10.other = bf16[16,16,16,128]{3,2,1,0:T(8,128)(2,1)S(1)} collective-permute-done((bf16[16,16,16,128]{3,2,1,0:T(8,128)(2,1)}, bf16[16,16,16,128]{3,2,1,0:T(8,128)(2,1)S(1)}, u32[]{:S(2)}, u32[]{:S(2)}) %collective-permute-start.10) | collective-permute-done | bytes 1048608 | tf_op jit(solution)/shard_map/ppermute | solution.py:994
  307.5 10.4 %final.2.earlier.rest_0_ = bf16[256,32,512]{2,1,0:T(8,128)(2,1)} custom-call(s32[1]{0:T(128)} %bitcast.side, bf16[16,256,512]{2,1,0:T(8,128)(2,1)} %copy-done.3, bf16[16,16,16,128]{3,2,1,0:T(8,128)(2,1)} %all-to-all-done.4.own, bf16[16,16,16,128]{3,2,1,0:T(8,128)(2,1)S(1)} %collective-permute-done.10.other, ...), custom_call_target="tpu_custom_call" | custom-call | flops 2147483648 | bytes 10485760 | tf_op jit(solution)/shard_map/final/pallas_call | solution.py:806
  317.9 3.4 copy-done.2
  324.4 5.2 %all-to-all-start.5 = ((bf16[32,5,16,128]{3,2,1,0:T(8,128)(2,1)}), bf16[32,5,16,128]{3,2,1,0:T(8,128)(2,1)S(1)}, u32[]{:S(2)}, u32[]{:S(2)}) async-start(bf16[32,5,16,128]{3,2,1,0:T(8,128)(2,1)} %copy-done.15), calls=%async_computation.5 | async-start | bytes 1310720 | tf_op jit(solution)/shard_map/all_to_all | solution.py:1000
  329.6 1.8 collective-permute-start.11
  331.4 2.9 grad_gain.1
  334.3 27.6 %collective-permute-done.11.other = bf16[16,16,16,128]{3,2,1,0:T(8,128)(2,1)S(1)} collective-permute-done((bf16[16,16,16,128]{3,2,1,0:T(8,128)(2,1)}, bf16[16,16,16,128]{3,2,1,0:T(8,128)(2,1)S(1)}, u32[]{:S(2)}, u32[]{:S(2)}) %collective-permute-start.11) | collective-permute-done | bytes 1048608 | tf_op jit(solution)/shard_map/ppermute | solution.py:999
  361.9 10.1 %final.3 = bf16[256,32,512]{2,1,0:T(8,128)(2,1)} custom-call(s32[1]{0:T(128)} %bitcast.side, bf16[16,256,512]{2,1,0:T(8,128)(2,1)} %copy-done, bf16[16,16,16,128]{3,2,1,0:T(8,128)(2,1)S(1)} %copy-done.10, bf16[16,16,16,128]{3,2,1,0:T(8,128)(2,1)S(1)} %collective-permute-done.11.other, ...), custom_call_target="tpu_custom_call", output_to_operand_aliasing={{}: (6, {})} | custom-call | flops 2147483648 | bytes 10485760 | tf_op jit(solution)/shard_map/final/pallas_call | solution.py:806
  (115 shorter events, 27.4 us)
Async XLA Ops:
  0.6 10.2 %copy-start.22 = (bf16[256,512]{1,0:T(8,128)(2,1)S(1)}, bf16[256,512]{1,0:T(8,128)(2,1)}, u32[]{:S(2)}) copy-start(bf16[256,512]{1,0:T(8,128)(2,1)} %win.3) | copy-start | bytes 786436
  3.3 59.5 %all-to-all-start = ((f32[16,8,2,8,128]{4,3,2,1,0:T(8,128)}), f32[16,8,2,8,128]{4,3,2,1,0:T(8,128)S(1)}, u32[]{:S(2)}, u32[]{:S(2)}) async-start(f32[16,8,2,8,128]{4,3,2,1,0:T(8,128)} %bitcast.36), calls=%async_computation | async-start | bytes 2097152 | tf_op jit(solution)/shard_map/all_to_all | solution.py:966
  56.6 58.4 %collective-permute-start = (bf16[2,256,512]{2,1,0:T(8,128)(2,1)}, bf16[2,256,512]{2,1,0:T(8,128)(2,1)S(1)}, u32[]{:S(2)}, u32[]{:S(2)}) collective-permute-start(bf16[2,256,512]{2,1,0:T(8,128)(2,1)} %get-tuple-element.26), channel_id=1, source_target_pairs={{2,0},{4,2},{6,4},{8,6},{10,8},{12,10},{14,12},{16,14},{18,16},{20... | collective-permute-start | bytes 1572872 | tf_op jit(solution)/shard_map/ppermute | solution.py:968
  61.2 46.7 %copy-start.28 = (bf16[16,16,256]{2,1,0:T(8,128)(2,1)S(1)}, bf16[16,16,256]{2,1,0:T(8,128)(2,1)}, u32[]{:S(2)}) copy-start(bf16[16,16,256]{2,1,0:T(8,128)(2,1)} %get-tuple-element.27) | copy-start | bytes 393220
  61.3 60.5 %copy-start.13 = (bf16[256,16,128]{2,1,0:T(8,128)(2,1)S(1)}, bf16[256,16,128]{2,1,0:T(8,128)(2,1)}, u32[]{:S(2)}) copy-start(bf16[256,16,128]{2,1,0:T(8,128)(2,1)} %get-tuple-element.29.kept) | copy-start | bytes 3145732
  61.3 53.8 %collective-permute-start.4 = (bf16[256,16,128]{2,1,0:T(8,128)(2,1)}, bf16[256,16,128]{2,1,0:T(8,128)(2,1)}, u32[]{:S(2)}, u32[]{:S(2)}) collective-permute-start(bf16[256,16,128]{2,1,0:T(8,128)(2,1)} %get-tuple-element.30), channel_id=1, source_target_pairs={{0,1},{1,0},{2,3},{3,2},{4,5},{5,4},{6,7},{7,6},{8,9},{9,8},{10,11... | collective-permute-start | bytes 3145736 | tf_op jit(solution)/shard_map/ppermute | solution.py:967
  107.9 13.8 %collective-permute-start.5 = (bf16[2,256,512]{2,1,0:T(8,128)(2,1)}, bf16[2,256,512]{2,1,0:T(8,128)(2,1)S(1)}, u32[]{:S(2)}, u32[]{:S(2)}) collective-permute-start(bf16[2,256,512]{2,1,0:T(8,128)(2,1)} %get-tuple-element.31), channel_id=1, source_target_pairs={{0,2},{2,4},{4,6},{6,8},{8,10},{10,12},{12,14},{14,16},{16,18},{18... | collective-permute-start | bytes 1572872 | tf_op jit(solution)/shard_map/ppermute | solution.py:975
  107.9 7.1 %collective-permute-start.1 = (bf16[16,16,256]{2,1,0:T(8,128)(2,1)S(1)}, bf16[16,16,256]{2,1,0:T(8,128)(2,1)S(1)}, u32[]{:S(2)}, u32[]{:S(2)}) collective-permute-start(bf16[16,16,256]{2,1,0:T(8,128)(2,1)S(1)} %copy-done.28), channel_id=1, source_target_pairs={{0,1},{1,0},{2,3},{3,2},{4,5},{5,4},{6,7},{7,6},{8,9},{9,8},{10,11... | collective-permute-start | bytes 393224 | tf_op jit(solution)/shard_map/ppermute | solution.py:969
  108.5 6.5 %collective-permute-start.3 = (bf16[2,16,256]{2,1,0:T(8,128)(2,1)S(1)}, bf16[2,16,256]{2,1,0:T(8,128)(2,1)S(1)}, u32[]{:S(2)}, u32[]{:S(2)}) collective-permute-start(bf16[2,16,256]{2,1,0:T(8,128)(2,1)S(1)} %slice.44), channel_id=1, source_target_pairs={{2,1},{3,0},{4,3},{5,2},{6,5},{7,4},{8,7},{9,6},{10,9},{11,8},{12,... | collective-permute-start | bytes 49160 | tf_op jit(solution)/shard_map/ppermute | solution.py:970
  115.0 6.8 %collective-permute-start.6 = (bf16[2,16,256]{2,1,0:T(8,128)(2,1)S(1)}, bf16[2,16,256]{2,1,0:T(8,128)(2,1)S(1)}, u32[]{:S(2)}, u32[]{:S(2)}) collective-permute-start(bf16[2,16,256]{2,1,0:T(8,128)(2,1)S(1)} %slice.45), channel_id=1, source_target_pairs={{0,3},{1,2},{2,5},{3,4},{4,7},{5,6},{6,9},{7,8},{8,11},{9,10},{10,... | collective-permute-start | bytes 49160 | tf_op jit(solution)/shard_map/ppermute | solution.py:976
  115.0 30.7 %copy-start.16 = (bf16[16,16,256]{2,1,0:T(8,128)(2,1)}, bf16[16,16,256]{2,1,0:T(8,128)(2,1)S(1)}, u32[]{:S(2)}) copy-start(bf16[16,16,256]{2,1,0:T(8,128)(2,1)S(1)} %collective-permute-done.1.rest_2_) | copy-start | bytes 393220
  124.4 15.2 %copy-start.26 = (s32[512,12]{0,1:T(8,128)S(1)}, s32[512,12]{0,1:T(8,128)}, u32[]{:S(2)}) copy-start(s32[512,12]{0,1:T(8,128)} %param.27) | copy-start | bytes 73732
  124.4 15.2 %copy-start.29 = (f32[64]{0:T(128)S(1)}, f32[64]{0:T(128)}, u32[]{:S(2)}) copy-start(f32[64]{0:T(128)} %param.24) | copy-start | bytes 772
  124.4 15.5 %copy-start.27 = (s32[512,12]{0,1:T(8,128)S(1)}, s32[512,12]{0,1:T(8,128)}, u32[]{:S(2)}) copy-start(s32[512,12]{0,1:T(8,128)} %param.26) | copy-start | bytes 73732
  124.4 15.6 %copy-start.25 = (s32[512,12]{0,1:T(8,128)S(1)}, s32[512,12]{0,1:T(8,128)}, u32[]{:S(2)}) copy-start(s32[512,12]{0,1:T(8,128)} %param.25) | copy-start | bytes 73732
  124.4 54.4 %all-to-all-start.1 = ((bf16[16,16,16,128]{3,2,1,0:T(8,128)(2,1)}), bf16[16,16,16,128]{3,2,1,0:T(8,128)(2,1)S(1)}, u32[]{:S(2)}, u32[]{:S(2)}) async-start(bf16[16,16,16,128]{3,2,1,0:T(8,128)(2,1)} %pair_sum.2.earlier), calls=%async_computation.1 | async-start | bytes 2097152 | tf_op jit(solution)/shard_map/all_to_all | solution.py:984
  140.1 6.7 %collective-permute-start.2 = (bf16[16,16,256]{2,1,0:T(8,128)(2,1)}, bf16[16,16,256]{2,1,0:T(8,128)(2,1)}, u32[]{:S(2)}, u32[]{:S(2)}) collective-permute-start(bf16[16,16,256]{2,1,0:T(8,128)(2,1)} %get-tuple-element.28), channel_id=1, source_target_pairs={{0,1},{1,0},{2,3},{3,2},{4,5},{5,4},{6,7},{7,6},{8,9},{9,8},{10,11... | collective-permute-start | bytes 393224 | tf_op jit(solution)/shard_map/ppermute | solution.py:974
  140.7 33.5 %collective-permute-start.8 = (bf16[256,16,128]{2,1,0:T(8,128)(2,1)}, bf16[256,16,128]{2,1,0:T(8,128)(2,1)}, u32[]{:S(2)}, u32[]{:S(2)}) collective-permute-start(bf16[256,16,128]{2,1,0:T(8,128)(2,1)} %get-tuple-element.33), channel_id=1, source_target_pairs={{0,1},{1,0},{2,3},{3,2},{4,5},{5,4},{6,7},{7,6},{8,9},{9,8},{10,11... | collective-permute-start | bytes 3145736 | tf_op jit(solution)/shard_map/ppermute | solution.py:977
  144.6 29.6 %collective-permute-start.9 = (bf16[16,4,16,128]{3,2,1,0:T(8,128)(2,1)}, bf16[16,4,16,128]{3,2,1,0:T(8,128)(2,1)S(1)}, u32[]{:S(2)}, u32[]{:S(2)}) collective-permute-start(bf16[16,4,16,128]{3,2,1,0:T(8,128)(2,1)} %get-tuple-element.45), channel_id=1, source_target_pairs={{0,1},{1,0},{2,3},{3,2},{4,5},{5,4},{6,7},{7,6},{8,9},{9,8},{10,11... | collective-permute-start | bytes 786440 | tf_op jit(solution)/shard_map/ppermute | solution.py:960
  147.7 26.4 %copy-start.14 = (bf16[256,16,128]{2,1,0:T(8,128)(2,1)S(1)}, bf16[256,16,128]{2,1,0:T(8,128)(2,1)}, u32[]{:S(2)}) copy-start(bf16[256,16,128]{2,1,0:T(8,128)(2,1)} %get-tuple-element.32.kept) | copy-start | bytes 3145732
  178.8 33.3 %all-to-all-start.2 = ((bf16[16,20,16,128]{3,2,1,0:T(8,128)(2,1)}), bf16[16,20,16,128]{3,2,1,0:T(8,128)(2,1)S(1)}, u32[]{:S(2)}, u32[]{:S(2)}) async-start(bf16[16,20,16,128]{3,2,1,0:T(8,128)(2,1)} %copy-done.4), calls=%async_computation.2 | async-start | bytes 2621440 | tf_op jit(solution)/shard_map/all_to_all | solution.py:987
  220.4 9.0 %copy-start.8 = (bf16[2,256,512]{2,1,0:T(8,128)(2,1)S(1)}, bf16[2,256,512]{2,1,0:T(8,128)(2,1)}, u32[]{:S(2)}) copy-start(bf16[2,256,512]{2,1,0:T(8,128)(2,1)} %copy-done.7) | copy-start | bytes 1572868
  220.4 55.0 %all-to-all-start.4 = ((bf16[16,16,16,128]{3,2,1,0:T(8,128)(2,1)}), bf16[16,16,16,128]{3,2,1,0:T(8,128)(2,1)}, u32[]{:S(2)}, u32[]{:S(2)}) async-start(bf16[16,16,16,128]{3,2,1,0:T(8,128)(2,1)} %copy-done.12), calls=%async_computation.4 | async-start | bytes 2097152 | tf_op jit(solution)/shard_map/all_to_all | solution.py:993
  229.4 19.5 %copy-start.1 = (bf16[16,256,512]{2,1,0:T(8,128)(2,1)S(1)}, bf16[16,256,512]{2,1,0:T(8,128)(2,1)}, u32[]{:S(2)}) copy-start(bf16[16,256,512]{2,1,0:T(8,128)(2,1)} %copy-done) | copy-start | bytes 12582916
  249.0 10.3 %copy-start.3 = (bf16[16,256,512]{2,1,0:T(8,128)(2,1)}, bf16[16,256,512]{2,1,0:T(8,128)(2,1)S(1)}, u32[]{:S(2)}) copy-start(bf16[16,256,512]{2,1,0:T(8,128)(2,1)S(1)} %stencil.3.q_ref) | copy-start | bytes 12582916
  268.9 4.3 %collective-permute-start.7 = (bf16[16,1,16,128]{3,2,1,0:T(8,128)(2,1)S(1)}, bf16[16,1,16,128]{3,2,1,0:T(8,128)(2,1)S(1)}, u32[]{:S(2)}, u32[]{:S(2)}) collective-permute-start(bf16[16,1,16,128]{3,2,1,0:T(8,128)(2,1)S(1)} %get-tuple-element.49), channel_id=1, source_target_pairs={{0,1},{1,0},{2,3},{3,2},{4,5},{5,4},{6,7},{7,6},{8,9},{9,8},{10,11... | collective-permute-start | bytes 196616 | tf_op jit(solution)/shard_map/ppermute | solution.py:960
  275.4 32.1 %copy-start.18 = (bf16[256,256]{1,0:T(8,128)(2,1)S(1)}, bf16[256,256]{1,0:T(8,128)(2,1)}, u32[]{:S(2)}) copy-start(bf16[256,256]{1,0:T(8,128)(2,1)} %wd.3) | copy-start | bytes 393220
  275.4 42.5 %all-to-all-start.3 = ((bf16[16,25,16,128]{3,2,1,0:T(8,128)(2,1)}), bf16[16,25,16,128]{3,2,1,0:T(8,128)(2,1)S(1)}, u32[]{:S(2)}, u32[]{:S(2)}) async-start(bf16[16,25,16,128]{3,2,1,0:T(8,128)(2,1)} %share.1), calls=%async_computation.3 | async-start | bytes 3276800 | tf_op jit(solution)/shard_map/all_to_all | solution.py:995
  281.7 25.8 %collective-permute-start.10 = (bf16[16,16,16,128]{3,2,1,0:T(8,128)(2,1)}, bf16[16,16,16,128]{3,2,1,0:T(8,128)(2,1)S(1)}, u32[]{:S(2)}, u32[]{:S(2)}) collective-permute-start(bf16[16,16,16,128]{3,2,1,0:T(8,128)(2,1)} %all-to-all-done.4.own), channel_id=1, source_target_pairs={{0,1},{1,0},{2,3},{3,2},{4,5},{5,4},{6,7},{7,6},{8,9},{9,8},{10,11... | collective-permute-start | bytes 3145736 | tf_op jit(solution)/shard_map/ppermute | solution.py:994
  324.4 47.7 %all-to-all-start.5 = ((bf16[32,5,16,128]{3,2,1,0:T(8,128)(2,1)}), bf16[32,5,16,128]{3,2,1,0:T(8,128)(2,1)S(1)}, u32[]{:S(2)}, u32[]{:S(2)}) async-start(bf16[32,5,16,128]{3,2,1,0:T(8,128)(2,1)} %copy-done.15), calls=%async_computation.5 | async-start | bytes 1310720 | tf_op jit(solution)/shard_map/all_to_all | solution.py:1000
  329.5 32.4 %copy-start.10 = (bf16[16,16,16,128]{3,2,1,0:T(8,128)(2,1)S(1)}, bf16[16,16,16,128]{3,2,1,0:T(8,128)(2,1)}, u32[]{:S(2)}) copy-start(bf16[16,16,16,128]{3,2,1,0:T(8,128)(2,1)} %copy-done.9) | copy-start | bytes 3145732
  329.6 32.3 %collective-permute-start.11 = (bf16[16,16,16,128]{3,2,1,0:T(8,128)(2,1)}, bf16[16,16,16,128]{3,2,1,0:T(8,128)(2,1)S(1)}, u32[]{:S(2)}, u32[]{:S(2)}) collective-permute-start(bf16[16,16,16,128]{3,2,1,0:T(8,128)(2,1)} %copy-done.9), channel_id=1, source_target_pairs={{0,1},{1,0},{2,3},{3,2},{4,5},{5,4},{6,7},{7,6},{8,9},{9,8},{10,11... | collective-permute-start | bytes 3145736 | tf_op jit(solution)/shard_map/ppermute | solution.py:999
  (16 other events, 45.0 us)
